TPU v7x, 128 devices: a whole 4x4x4 slice. The times are simulated.
128 devices in a mesh: seq: 64 (over x, y, z), head: 2 (over core).
Axes of the slice: x: 4, y: 4, z: 4, core: 2. Of those that a mesh axis runs over, the one named last changes fastest.
Arguments:
- ref_queries: bfloat16 [64, 64, 128], P('seq', 'head'), as said below
- query_pos: int32 [64], P('seq'), may hold values from 32768 to 131071
- cache_keys: bfloat16 [131072, 8, 128], P('seq', 'head'), may hold values from -6 to 6
- cache_values: bfloat16 [131072, 8, 128], P('seq', 'head'), may hold values from -6 to 6
- kept_index: int32 [8, 512], P('head'), may hold values from 0 to 131071
Outputs:
- reference_out: bfloat16 [64, 64, 128], P('seq', 'head')
- fitted_values: float32 [8, 512, 128], P('head', 'seq')
Inputs may be any that keep to these rules, and one draw needn't show every extreme that they name: `kept_index`: cache positions of the kept rows, repeats possible. `ref_queries`: query vectors of order one or larger.
All inputs are finite; a program needn't handle non-finite values.
Results may differ from a plain program's by a relative error of at most 0.01325.
Values may be sent and summed in bfloat16 or wider, within the bound.
No kernel may reach another device: no remote copies, remote signals or barrier semaphores. Data moves between devices by JAX's collectives and lax.ppermute only.
A program may use at most 192 MiB of HBM per device.

v0:
```python
import jax
import jax.numpy as jnp
from jax import lax
from jax.sharding import PartitionSpec as P

ridge_weight = 0.01
neg_floor = -1e30


def combined_all(part, axis, combine):
    gathered = jax.tree.map(lambda a: lax.all_gather(a, axis), part)

    def take(source):
        return jax.tree.map(lambda a: lax.dynamic_index_in_dim(a, source, 0, False), gathered)

    return lax.fori_loop(
        1, lax.axis_size(axis), lambda source, state: combine(state, take(source)), take(0)
    )


def combine_parts(earlier, later_part):
    peak_one, total_one, output_one = earlier
    peak_two, total_two, output_two = later_part
    highest = jnp.maximum(peak_one, peak_two)
    scale_one = jnp.exp(peak_one - highest)
    scale_two = jnp.exp(peak_two - highest)
    totals = total_one * scale_one + total_two * scale_two
    outputs = output_one * scale_one[..., None] + output_two * scale_two[..., None]
    return (highest, totals, outputs)


def solve_head(lower_part, right_part):
    inner_part = jax.scipy.linalg.solve_triangular(lower_part, right_part, lower=True)
    return jax.scipy.linalg.solve_triangular(lower_part, inner_part, lower=True, trans=1)


def on_device(ref_queries, query_pos, cache_keys, cache_values, kept_index):
    seq_count = lax.axis_size("seq")
    seq_index = lax.axis_index("seq")
    local_len = cache_keys.shape[0]
    heads_here = cache_keys.shape[1]
    head_width = cache_keys.shape[2]
    group_size = ref_queries.shape[1] // heads_here
    own_rows = ref_queries.shape[0]
    scaling_factor = head_width ** (-0.5)
    key_pos = seq_index * local_len + jnp.arange(local_len, dtype=jnp.int32)

    def attend_block(inputs):
        queries, positions = inputs
        grouped_heads_view = queries.reshape(queries.shape[0], heads_here, group_size, head_width)
        attention_scores = (
            jnp.einsum(
                "bhgd,shd->bhgs", grouped_heads_view, cache_keys, preferred_element_type=jnp.float32
            )
            * scaling_factor
        )
        allowed = (key_pos[None, :] <= positions[:, None])[:, None, None, :]
        attention_scores = jnp.where(allowed, attention_scores, neg_floor)
        peak_rows = jnp.max(attention_scores, axis=-1)
        weights = jnp.where(allowed, jnp.exp(attention_scores - peak_rows[..., None]), 0.0)
        totals = jnp.sum(weights, axis=-1)
        partial_out = jnp.einsum(
            "bhgs,shd->bhgd",
            weights.astype(jnp.bfloat16),
            cache_values,
            preferred_element_type=jnp.float32,
        )
        return (peak_rows, totals, partial_out)

    queries, positions = lax.all_gather((ref_queries, query_pos), "seq", axis=0, tiled=True)
    count_rows = queries.shape[0]
    stride = 16
    peak_rows, totals, partial_out = lax.map(
        attend_block,
        (
            queries.reshape(count_rows // stride, stride, queries.shape[1], head_width),
            positions.reshape(count_rows // stride, stride),
        ),
    )
    all_heads = heads_here * group_size
    peak_rows, totals, partial_out, all_queries = (
        peak_rows.reshape(count_rows, all_heads),
        totals.reshape(count_rows, all_heads),
        partial_out.reshape(count_rows, all_heads, head_width),
        queries,
    )
    peak_rows, totals, partial_out = combined_all(
        (peak_rows, totals, partial_out), "seq", combine_parts
    )
    full_attended = partial_out / totals[..., None]
    attended = lax.dynamic_slice_in_dim(full_attended, seq_index * own_rows, own_rows, 0)
    reference_out = attended.astype(jnp.bfloat16)
    local_index = kept_index - seq_index * local_len
    inside = (local_index >= 0) & (local_index < local_len)
    clipped = jnp.clip(local_index, 0, local_len - 1)
    head_iota = jnp.arange(heads_here, dtype=jnp.int32)[:, None]
    picked_keys = jnp.where(
        inside[..., None], cache_keys[clipped, head_iota].astype(jnp.float32), 0.0
    )
    picked_values = jnp.where(
        inside[..., None], cache_values[clipped, head_iota].astype(jnp.float32), 0.0
    )
    picked_keys, picked_values = lax.psum((picked_keys, picked_values), "seq")
    retained_key_rows = picked_keys.astype(jnp.bfloat16)
    fit_rows = ref_queries.shape[0]
    grouped_heads_view = ref_queries.reshape(fit_rows, heads_here, group_size, head_width)
    attention_scores = (
        jnp.einsum(
            "jfal,fwl->fjaw",
            grouped_heads_view,
            retained_key_rows,
            preferred_element_type=jnp.float32,
        )
        * scaling_factor
    )
    count_kept = retained_key_rows.shape[1]
    mixing_weights = jax.nn.softmax(attention_scores, axis=-1).reshape(
        heads_here, fit_rows * group_size, count_kept
    )
    target_outputs = attended.reshape(fit_rows, heads_here, group_size, head_width).transpose(
        1, 0, 2, 3
    )
    target_outputs = target_outputs.reshape(heads_here, fit_rows * group_size, head_width)
    gram_matrix = jnp.einsum(
        "hkm,hkn->hmn", mixing_weights, mixing_weights, precision=lax.Precision.HIGHEST
    )
    cross_products_matrix = jnp.einsum(
        "jze,jzv->jev", mixing_weights, target_outputs, precision=lax.Precision.HIGHEST
    )
    gram_matrix, cross_products_matrix = lax.psum((gram_matrix, cross_products_matrix), "seq")
    left_side = gram_matrix + ridge_weight * jnp.eye(count_kept, dtype=jnp.float32)
    right_side = cross_products_matrix + ridge_weight * picked_values
    lower_factor = jnp.linalg.cholesky(left_side)
    fitted = jax.vmap(solve_head)(lower_factor, right_side)
    per_device = count_kept // seq_count
    fitted_values = lax.dynamic_slice_in_dim(fitted, seq_index * per_device, per_device, 1)
    return (reference_out, fitted_values)


def solution(mesh):
    in_specs = (
        P("seq", "head", None),
        P("seq"),
        P("seq", "head", None),
        P("seq", "head", None),
        P("head", None),
    )
    out_specs = (P("seq", "head", None), P("head", "seq", None))
    return jax.shard_map(
        on_device, mesh=mesh, in_specs=in_specs, out_specs=out_specs, check_vma=False
    )
```

profile of v0, /device:TPU:8, one launch (start us, length us, event | category | flops | bytes accessed | tf_op | source)
XLA Modules:
  0.0 1921.2 jit_solution(12936912775996230282)
XLA Ops:
  10.0 23.4 %all-reduce.1 = s32[64]{0:T(128)S(1)} all-reduce(s32[64]{0:T(128)S(1)} %dynamic-update-slice.23), channel_id=1, replica_groups=mesh['seq'=64,'head'=2] {'seq'}, use_global_device_ids=true, to_apply=%add.1 | all-reduce | flops 64 | bytes 512
  37.4 164.1 %all_gather.16 = bf16[64,32,128]{2,1,0:T(8,128)(2,1)S(1)} all-gather(bf16[1,32,128]{2,1,0:T(8,128)(2,1)S(1)} %copy-done.9), channel_id=1, replica_groups=mesh['seq'=64,'head'=2] {'seq'}, dimensions={0}, use_global_device_ids=true | all-gather | bytes 532480 | tf_op jit(solution)/shard_map/all_gather | solution.py:70
  201.5 21.8 %while.37 = (s32[]{:T(128)}, f32[4,16,4,8]{1,0,3,2:T(4,128)S(1)}, f32[4,16,4,8]{1,0,3,2:T(4,128)S(1)}, f32[4,16,4,8,128]{4,3,2,1,0:T(8,128)}, s32[4,16]{1,0:T(4,...) while((s32[]{:T(128)}, f32[4,16,4,8]{1,0,3,2:T(4,128)S(1)}, ...), condition=%wide.region_3.4_spmd.clone, body=%wide.region_0.3_spmd.clone.sunk | while | flops 550536192 | bytes 26256220 | solution.py:73
  223.4 82.9 %gather_fusion = bf16[2048,128]{1,0:T(8,128)(2,1)S(1)} fusion(bf16[2048,4,128]{2,1,0:T(4,128)(2,1)} %param.11, s32[2048]{0:T(1024)S(1)} %bitcast.183), kind=kCustom, calls=%fused_computation | custom fusion | bytes 1064960 | tf_op jit(solution)/shard_map/gather | solution.py:98
  306.3 11.1 gather_fusion.1
  317.5 190.8 %all_gather.17 = f32[64,64,32]{1,2,0:T(8,128)S(1)} all-gather(f32[1,64,32]{1,2,0:T(8,128)S(1)} %all_gather_reshape.9), channel_id=1, replica_groups=mesh['seq'=64,'head'=2] {'seq'}, dimensions={0}, use_global_device_ids=true | all-gather | bytes 532480 | tf_op jit(solution)/shard_map/all_gather | solution.py:11
  509.6 176.0 %all_gather.18 = f32[64,64,32]{1,2,0:T(8,128)S(1)} all-gather(f32[1,64,32]{1,2,0:T(8,128)S(1)} %all_gather_reshape.10), channel_id=1, replica_groups=mesh['seq'=64,'head'=2] {'seq'}, dimensions={0}, use_global_device_ids=true | all-gather | bytes 532480 | tf_op jit(solution)/shard_map/all_gather | solution.py:11
  688.0 351.9 %all-reduce.7 = bf16[4,512,128]{2,1,0:T(8,128)(2,1)S(1)} all-reduce(f32[4,512,128]{2,1,0:T(8,128)S(1)} %get-tuple-element.382), channel_id=1, replica_groups=mesh['seq'=64,'head'=2] {'seq'}, use_global_device_ids=true, to_apply=%region_6.7 | all-reduce | flops 262144 | bytes 1572864 | tf_op jit(solution)/shard_map/psum | solution.py:103
  1040.4 5.3 fusion.79
  1047.0 180.9 %while.35 = (s32[]{:T(128)}, f32[64,32]{1,0:T(8,128)S(1)}, f32[64,32]{1,0:T(8,128)S(1)}, f32[64,32,128]{2,1,0:T(8,128)S(1)}, f32[64,64,32]{1,2,0:T(8,128)}, /*in...) while((s32[]{:T(128)}, f32[64,32]{1,0:T(8,128)S(1)}, ...), condition=%wide.region_5.6_spmd, body=%wide.region_4.5_spmd.sunk | while | flops 798725 | bytes 3293335 | solution.py:16
  1227.8 2.9 fusion.77
  1231.7 152.3 %all-reduce.6.cloned.1.call-done = (f32[4,512,512]{1,2,0:T(8,128)}, f32[4,512,128]{2,1,0:T(8,128)}, f32[4,512,128]{2,1,0:T(8,128)}) async-done(((f32[4,512,512]{1,2,0:T(8,128)}, f32[4,512,128]{2,1,0:T(8,128)}, f32[4,512,128]{2,1,0:T(8,128)}), (f32[4,512,512]{1,2,0:T(8,128)}, f32[4,512,128]{2,1,0:T(8,128)}, f32[4,512,128]{2,1,0:T(8,128)})) %all-reduce.6.cloned.1.call-update) | async-done | bytes 6291472 | tf_op jit(solution)/shard_map/psum | solution.py:130
  1384.0 4.8 broadcast_add_fusion
  1388.7 5.2 copy.82
  1394.0 4.6 fusion.29
  1400.6 46.9 %custom-call.38 = f32[4,128,128]{2,1,0:T(8,128)S(1)} custom-call(f32[4,128,128]{2,1,0:T(8,128)S(1)} %cholesky.274), custom_call_target="Cholesky" | custom-call | tf_op jit(solution)/shard_map/jit(cholesky)/cholesky | solution.py:133
  1450.0 39.5 %custom-call.39 = f32[4,1,128,128]{2,3,1,0:T(8,128)S(1)} custom-call(f32[4,1,128,128]{3,2,1,0:T(8,128)S(1)} %select_bitcast_fusion.2), custom_call_target="InvertDiagBlocksLowerTriangular" | custom-call | tf_op jit(solution)/shard_map/jit(cholesky)/cholesky | solution.py:133
  1489.5 2.9 constant_dynamic-update-slice_fusion.3
  1494.4 46.9 %custom-call.40 = f32[4,128,128]{2,1,0:T(8,128)S(1)} custom-call(f32[4,128,128]{2,1,0:T(8,128)S(1)} %cholesky.278), custom_call_target="Cholesky" | custom-call | tf_op jit(solution)/shard_map/jit(cholesky)/cholesky | solution.py:133
  1542.1 39.3 %custom-call.41 = f32[4,1,128,128]{2,3,1,0:T(8,128)S(1)} custom-call(f32[4,1,128,128]{3,2,1,0:T(8,128)S(1)} %get-tuple-element.379), custom_call_target="InvertDiagBlocksLowerTriangular" | custom-call | tf_op jit(solution)/shard_map/jit(cholesky)/cholesky | solution.py:133
  1582.9 2.6 convolution_subtract_fusion.1
  1585.5 47.1 %custom-call.42 = f32[4,128,128]{2,1,0:T(8,128)S(1)} custom-call(f32[4,128,128]{2,1,0:T(8,128)S(1)} %cholesky.283), custom_call_target="Cholesky" | custom-call | tf_op jit(solution)/shard_map/jit(cholesky)/cholesky | solution.py:133
  1633.4 39.3 %custom-call.43 = f32[4,1,128,128]{2,3,1,0:T(8,128)S(1)} custom-call(f32[4,1,128,128]{3,2,1,0:T(8,128)S(1)} %get-tuple-element.377), custom_call_target="InvertDiagBlocksLowerTriangular" | custom-call | tf_op jit(solution)/shard_map/jit(cholesky)/cholesky | solution.py:133
  1673.8 2.6 convolution_subtract_fusion.6
  1676.5 47.1 %custom-call.44 = f32[4,128,128]{2,1,0:T(8,128)S(1)} custom-call(f32[4,128,128]{2,1,0:T(8,128)S(1)} %convolution_subtract_fusion.6), custom_call_target="Cholesky" | custom-call | tf_op jit(solution)/shard_map/jit(cholesky)/cholesky | solution.py:133
  1724.8 5.1 select_select_fusion
  1729.9 14.9 while.36
  1730.5 3.1 bitcast_dynamic-update-slice_fusion.2
  1734.2 3.1 bitcast_dynamic-update-slice_fusion.2
  1738.0 3.1 bitcast_dynamic-update-slice_fusion.2
  1741.8 3.0 bitcast_dynamic-update-slice_fusion.2
  1744.8 158.0 %custom-call.45 = f32[4,4,128,128]{2,3,1,0:T(8,128)S(1)} custom-call(f32[4,4,128,128]{3,2,1,0:T(8,128)} %bitcast.191), custom_call_target="InvertDiagBlocksLowerTriangular" | custom-call | tf_op jit(solution)/shard_map/vmap(jit(_solve_triangular))/triangular_solve | solution.py:34
  (461 shorter events, 238.4 us)
Async XLA Ops:
  7.2 1038.5 %all-gather.2.cloned.1.call-start = ((), (), s32[]{:S(2)}) async-start(), calls=%async_computation | async-start | bytes 68157440 | tf_op jit(solution)/shard_map/all_gather | solution.py:11
  33.5 2.2 copy-start
  33.5 3.8 copy-start.9
  201.5 21.9 %copy-start.10 = (s32[4,512]{1,0:T(4,128)S(1)}, s32[4,512]{1,0:T(4,128)}, u32[]{:S(2)}) copy-start(s32[4,512]{1,0:T(4,128)} %param.13) | copy-start | bytes 24580
  201.5 1.6 copy-start.4
  207.0 1.6 copy-start.4
  212.4 1.6 copy-start.4
  217.9 1.6 copy-start.4
  223.3 83.0 %copy-start.1 = (bf16[2048,4,128]{2,1,0:T(4,128)(2,1)S(1)}, bf16[2048,4,128]{2,1,0:T(4,128)(2,1)}, u32[]{:S(2)}) copy-start(bf16[2048,4,128]{2,1,0:T(4,128)(2,1)} %param.12) | copy-start | bytes 6291460
  223.4 1160.6 %all-reduce.6.cloned.1.call-start = ((), (), s32[]{:S(2)}) async-start(), calls=%async_computation.1 | async-start | bytes 12582912 | tf_op jit(solution)/shard_map/psum | solution.py:130
  508.4 1.0 copy-start.5
  685.6 1.0 copy-start.6
  1398.6 1.9 copy-start.3
  1724.8 178.0 %copy-start.7 = (f32[4,512,128]{2,1,0:T(8,128)S(1)}, f32[4,512,128]{2,1,0:T(8,128)}, u32[]{:S(2)}) copy-start(f32[4,512,128]{2,1,0:T(8,128)} %get-tuple-element.364) | copy-start | bytes 3145732
  1724.8 178.0 %copy-start.8 = (f32[4,512,128]{2,1,0:T(8,128)S(1)}, f32[4,512,128]{2,1,0:T(8,128)}, u32[]{:S(2)}) copy-start(f32[4,512,128]{2,1,0:T(8,128)} %get-tuple-element.365) | copy-start | bytes 3145732
  1902.8 3.1 copy-start.2
Sparse Core Ops, SparseCore 0:
  223.5 296.1 all-gather.1
  1230.9 153.0 all-reduce.5
where the time goes:
time: 1940 us; the launch traced here: 1920 us
  blocking collectives  906 us (47%)
  other arithmetic  613 us (32%)
  local copies, waits for them, and re-layouts  191 us (10%)
  waiting for transfers between devices  152 us (8%)
  matrix products  41 us (2%)
    all_gather x2, blocking collectives, combined_all(): gathered = jax.tree.map(lambda a: lax.all_gather(a, axis), part)  367 us
    psum x1, blocking collectives, on_device(): picked_keys, picked_values = lax.psum((picked_keys, picked_values), 'seq')  352 us
    another operation x16, other arithmetic, on_device(): lower_factor = jnp.linalg.cholesky(left_side)  309 us
    all_gather x1, blocking collectives, on_device(): lax.all_gather((ref_queries, query_pos), 'seq', axis=0, tiled=True)  164 us
    another operation x5, other arithmetic, solve_head(): jax.scipy.linalg.solve_triangular(lower_part, inner_part, lower=True, tra...  164 us
    psum x1, waiting for transfers between devices, on_device(): lax.psum((gram_matrix, cross_products_matrix), 'seq')  152 us
    add x63, other arithmetic, combine_parts(): output_one * scale_one[..., None] + output_two * scale_two[..., None]  119 us
    gather x1, local copies, waits for them, and re-layouts, on_device(): cache_keys[clipped, head_iota].astype(jnp.float32)  82.9 us
  transfers between devices with their start and end apart: 2, of which 1 were waited for; matrix products, arithmetic and copies ran while one was open for 5% of the time, Pallas kernels for 0%

commit v1 on v0

v1 whole, which is shorter than its diff:
```python
import functools
import math

import jax
import jax.numpy as jnp
from jax import lax
from jax.experimental import pallas as pl
from jax.experimental.pallas import tpu as pltpu
from jax.sharding import Mesh, PartitionSpec as P

ridge_weight = 0.01
masked_score = -1e30
highest = lax.Precision.HIGHEST
f32 = jnp.float32
bf16 = jnp.bfloat16

seq_axes = ("x", "y", "z")
count_rows = 64
heads_here = 4
group = 8
width = 128
local_len = 2048
kept = 512
chunk = 512
scale = width ** (-0.5)
scale_log2 = scale * math.log2(math.e)


def params(mib=56, **more):
    return pltpu.CompilerParams(vmem_limit_bytes=mib * 2**20, **more)


def call(kernel, name, out_shape, **more):
    if "compiler_params" not in more:
        more["compiler_params"] = params()
    return pl.pallas_call(kernel, name=name, out_shape=out_shape, **more)


def shape(dims, dtype):
    return jax.ShapeDtypeStruct(dims, dtype)


whole_vmem = pl.BlockSpec(memory_space=pltpu.VMEM)
whole_smem = pl.BlockSpec(memory_space=pltpu.SMEM)


def prepare_kernel(index_ref, keys_ref, values_ref, both_ref, packet_ref, wide, spread, total):
    step = pl.program_id(0)

    @pl.when(step == 0)
    def _():
        for h in range(heads_here):
            row = jnp.broadcast_to(index_ref[h : h + 1, :], (width, kept))
            spread[h] = row.T

    lane = lax.broadcasted_iota(jnp.int32, (kept, width), 1)
    wide[0] = keys_ref[...].astype(f32)
    wide[1] = values_ref[...].astype(f32)
    for h in range(heads_here):
        rows_k = wide[0, pl.ds(h, chunk, stride=heads_here), :].astype(bf16)
        rows_v = wide[1, pl.ds(h, chunk, stride=heads_here), :].astype(bf16)
        rows = jnp.concatenate([rows_k, rows_v], 1)
        both_ref[h] = rows
        wanted = spread[h] - step * chunk
        hot = jnp.concatenate(
            [
                jnp.where(wanted == lane + g * width, 1.0, 0.0).astype(bf16)
                for g in range(chunk // width)
            ],
            1,
        )
        found = jnp.dot(hot, rows, preferred_element_type=f32)

        @pl.when(step == 0)
        def _():
            total[h] = found

        @pl.when(step > 0)
        def _():
            total[h] += found

    @pl.when(step == local_len // chunk - 1)
    def _():
        for h in range(heads_here):
            packet_ref[16 * h : 16 * h + 16] = total[h].reshape(16, 32, 2 * width).astype(bf16)


def prepare(local_index, keys, values):
    rows = chunk * heads_here
    return call(
        prepare_kernel,
        "prepare",
        (
            shape((heads_here, local_len, 2 * width), bf16),
            shape((count_rows, 32, 2 * width), bf16),
        ),
        grid=(local_len // chunk,),
        in_specs=[
            pl.BlockSpec((heads_here, kept), lambda i: (0, 0)),
            pl.BlockSpec((rows, width), lambda i: (i, 0)),
            pl.BlockSpec((rows, width), lambda i: (i, 0)),
        ],
        out_specs=[
            pl.BlockSpec((heads_here, chunk, 2 * width), lambda i: (0, i, 0)),
            pl.BlockSpec((count_rows, 32, 2 * width), lambda i: (0, 0, 0)),
        ],
        scratch_shapes=[
            pltpu.VMEM((2, rows, width), f32),
            pltpu.VMEM((heads_here, kept, width), jnp.int32),
            pltpu.VMEM((heads_here, kept, 2 * width), f32),
        ],
        cost_estimate=pl.CostEstimate(
            flops=2 * 2 * 512 * 2048 * 256 * 4, bytes_accessed=12 * 2**20, transcendentals=0
        ),
    )(local_index, keys, values)


def attend_kernel(base_ref, queries_ref, both_ref, packet_ref, keys, values):
    h = pl.program_id(0)
    lane = lax.broadcasted_iota(jnp.int32, (local_len, width), 1)

    @pl.when(h == 0)
    def _():
        pieces = queries_ref[:, heads_here].astype(f32)
        row_id = lax.broadcasted_iota(jnp.int32, (count_rows, width), 0)
        lane_id = lax.broadcasted_iota(jnp.int32, (count_rows, width), 1)
        place = pieces[:, 0] + 256.0 * pieces[:, 1] + 65536.0 * pieces[:, 2]
        place = jnp.sum(jnp.where(row_id == lane_id, place, 0.0), axis=0, keepdims=True)
        spot = lax.broadcasted_iota(jnp.int32, (local_len, width), 0) + base_ref[0]
        late = (spot.astype(f32) > place) & (lane < count_rows)
        keys[:, width:] = jnp.where(late, masked_score, 0.0).astype(bf16)
        values[:, width:] = jnp.where(lane == 0, 1.0, 0.0).astype(bf16)

    keys[:, :width] = both_ref[0, :, :width]
    values[:, :width] = both_ref[0, :, width:]
    q = queries_ref[:, h].astype(f32).reshape(count_rows * group, width)
    tile = 256
    lane_t = lax.broadcasted_iota(jnp.int32, (tile, width), 1)
    row_t = lax.broadcasted_iota(jnp.int32, (tile, width), 0)
    for part in range(count_rows * group // tile):
        own = jnp.where(row_t // group + part * (tile // group) == lane_t, 1.0, 0.0)
        q_part = jnp.concatenate([q[part * tile : (part + 1) * tile], own], 1).astype(bf16)
        s = lax.dot_general(
            q_part, keys[...], (((1,), (1,)), ((), ())), preferred_element_type=f32
        )
        peak = jnp.max(s, axis=1, keepdims=True)
        w = jnp.exp2((s - peak) * scale_log2).astype(bf16)
        o = jnp.dot(w, values[...], preferred_element_type=f32)
        sums = o[:, width : width + 1]
        mass = peak * scale_log2 + jnp.log2(sums)
        high = mass.astype(bf16).astype(f32)
        middle = (mass - high).astype(bf16).astype(f32)
        low = mass - high - middle
        side = jnp.where(
            lane_t == 0,
            high,
            jnp.where(lane_t == 1, middle, jnp.where(lane_t == 2, low, 0.0)),
        )
        done = jnp.concatenate([o[:, :width] / sums, side], 1)
        rows = tile // group
        packet_ref[part * rows : (part + 1) * rows, 0] = done.reshape(
            rows, group, 2 * width
        ).astype(bf16)


def attend(base, queries, both):
    return call(
        attend_kernel,
        "attend",
        shape((count_rows, heads_here, group, 2 * width), bf16),
        grid=(heads_here,),
        in_specs=[
            whole_smem,
            pl.BlockSpec((count_rows, heads_here + 1, group, width), lambda h: (0, 0, 0, 0)),
            pl.BlockSpec((1, local_len, 2 * width), lambda h: (h, 0, 0)),
        ],
        out_specs=pl.BlockSpec((count_rows, 1, group, 2 * width), lambda h: (0, h, 0, 0)),
        scratch_shapes=[
            pltpu.VMEM((local_len, 2 * width), bf16),
            pltpu.VMEM((local_len, 2 * width), bf16),
        ],
        cost_estimate=pl.CostEstimate(
            flops=2 * 2 * 512 * 2048 * 256 * 4,
            bytes_accessed=6 * 2**20,
            transcendentals=4 * 512 * 2048,
        ),
    )(base, queries, both)


def combine_kernel(parts_ref, out_ref, spread_ref):
    for h in range(heads_here):
        part = parts_ref[:, h].astype(f32)
        mass = jnp.sum(part[:, :, width:], axis=2, keepdims=True)
        top = jnp.max(mass, axis=0, keepdims=True)
        share = jnp.exp2(mass - top)
        full = jnp.sum(share * part[:, :, :width], axis=0) / jnp.sum(share, axis=0)
        out_ref[h] = full.astype(bf16)
        spread_ref[16 * h : 16 * h + 16] = jnp.broadcast_to(full[None], (16, group, width))


def combine(parts):
    return call(
        combine_kernel,
        "combine",
        (shape((heads_here, group, width), bf16), shape((count_rows, group, width), f32)),
        cost_estimate=pl.CostEstimate(
            flops=2 * 2**20, bytes_accessed=2 * 2**20, transcendentals=2048
        ),
    )(parts)


def gather_kernel(parts_ref, out_ref):
    found = jnp.sum(parts_ref[...].astype(f32), axis=0).astype(bf16)
    out_ref[...] = jnp.broadcast_to(found[None], out_ref.shape)


def add_kept(parts):
    return call(
        gather_kernel,
        "add_kept",
        shape((16, 32, 2 * width), bf16),
        cost_estimate=pl.CostEstimate(flops=2**20, bytes_accessed=2**20, transcendentals=0),
    )(parts)


def reciprocal(x):
    r = pl.reciprocal(x, approx=True)
    r = r * (2.0 - x * r)
    return r * (2.0 - x * r)


def invert_small(d, n):
    if n == 1:
        return [[reciprocal(d[0][0])]]
    if n == 2:
        r = reciprocal(d[0][0] * d[1][1] - d[0][1] * d[0][1])
        off = -d[0][1] * r
        return [[d[1][1] * r, off], [off, d[0][0] * r]]
    h = n // 2
    side = range(h)
    p = [[d[i][j] for j in side] for i in side]
    q = [[d[i][h + j] for j in side] for i in side]
    pin = invert_small(p, h)
    pq = [[sum(pin[i][k] * q[k][j] for k in side) for j in side] for i in side]
    t = [[None] * h for _ in side]
    for i in side:
        for j in range(i, h):
            t[i][j] = t[j][i] = d[h + i][h + j] - sum(q[k][i] * pq[k][j] for k in side)
    tin = invert_small(t, h)
    pqt = [[sum(pq[i][k] * tin[k][j] for k in side) for j in side] for i in side]
    out = [[None] * n for _ in range(n)]
    for i in side:
        for j in side:
            out[h + i][h + j] = tin[i][j]
            out[i][h + j] = -pqt[i][j]
            out[h + j][i] = -pqt[i][j]
    for i in side:
        for j in range(i, h):
            out[i][j] = out[j][i] = pin[i][j] + sum(pqt[i][k] * pq[j][k] for k in side)
    return out


def invert_block(a, n, b, h):
    lane = lax.broadcasted_iota(jnp.int32, (8, n), 1)
    sub = lax.broadcasted_iota(jnp.int32, (8, n), 0)
    lane_n = lax.broadcasted_iota(jnp.int32, (n, n), 1)
    for first in range(0, n, h):
        tiles = [a[first + 8 * i : first + 8 * i + 8, :] for i in range(h // 8)]
        for k in range(first, first + h, b):
            at, off = (k - first) // 8, k % 8
            rows = [
                jnp.broadcast_to(tiles[at][off + s : off + s + 1, :], (8, n)) for s in range(b)
            ]
            d = [[None] * b for _ in range(b)]
            for s in range(b):
                for t in range(s, b):
                    d[s][t] = d[t][s] = jnp.broadcast_to(rows[s][:, k + t : k + t + 1], (8, n))
            columns = [
                [jnp.broadcast_to(tile[:, k + s : k + s + 1], (8, n)) for tile in tiles]
                for s in range(b)
            ]
            inverse = invert_small(d, b)
            inside = (lane >= k) & (lane < k + b)
            rows = [
                jnp.where(lane == k + s, 1.0, jnp.where(inside, 0.0, rows[s])) for s in range(b)
            ]
            new = [sum(inverse[s][t] * rows[t] for t in range(b)) for s in range(b)]
            after = []
            for i, tile in enumerate(tiles):
                left = jnp.where(inside, 0.0, tile)
                left = left - sum(columns[s][i] * new[s] for s in range(b))
                if i == at:
                    for s in range(b):
                        left = jnp.where(sub == off + s, new[s], left)
                after.append(left)
            tiles = after
        r = jnp.concatenate(tiles, 0)
        inside_n = (lane_n >= first) & (lane_n < first + h)
        rest = jnp.where(inside_n, 0.0, a) - jnp.dot(
            a[:, first : first + h], r, precision=highest, preferred_element_type=f32
        )
        pieces = ([rest[:first]] if first else []) + [r]
        a = jnp.concatenate(pieces + ([rest[first + h :]] if first + h < n else []), 0)
    return a


def fit_kernel(place_ref, queries_ref, kept_ref, weight_ref, plain_ref, mixing, a):
    n = 128
    head, own = place_ref[0], place_ref[1]
    q = queries_ref[:, head].astype(f32).reshape(count_rows * group, width).astype(bf16)
    s = lax.dot_general(
        kept_ref[:, :width], q, (((1,), (1,)), ((), ())), preferred_element_type=f32
    )
    e = jnp.exp((s - jnp.max(s, axis=0, keepdims=True)) * scale)
    mixing[...] = e / jnp.sum(e, axis=0, keepdims=True)
    m = mixing[...]
    row = lax.broadcasted_iota(jnp.int32, (kept, kept), 0)
    column = lax.broadcasted_iota(jnp.int32, (kept, kept), 1)
    a[...] = lax.dot_general(
        m, m, (((1,), (1,)), ((), ())), precision=highest, preferred_element_type=f32
    ) + jnp.where(row == column, ridge_weight, 0.0)
    eye = jnp.where(row[:n, :n] == column[:n, :n], 1.0, 0.0)

    def step(k, _):
        at = pl.ds(pl.multiple_of(k * n, n), n)
        p = invert_block(a[at, at], n, 4, 32)
        a[at, at] = -eye
        left = a[:, at]
        a[:, at] = jnp.zeros((kept, n), f32)
        a[at, at] = eye
        r = jnp.dot(p, a[at, :], precision=highest, preferred_element_type=f32)
        a[at, :] = jnp.zeros((n, kept), f32)
        a[...] -= jnp.dot(left, r, precision=highest, preferred_element_type=f32)
        return 0

    lax.fori_loop(0, kept // n, step, 0)
    picked = jnp.concatenate(
        [a[pl.ds(pl.multiple_of(128 * i + 8 * own, 8), 8), :] for i in range(4)], 0
    )
    weight_ref[...] = jnp.dot(picked, m, precision=highest, preferred_element_type=f32)
    plain_ref[...] = ridge_weight * jnp.dot(
        picked, kept_ref[:, width:].astype(f32), precision=highest, preferred_element_type=f32
    )


def fit(place, queries, kept_rows):
    return call(
        fit_kernel,
        "fit",
        (shape((32, kept), f32), shape((32, width), f32)),
        in_specs=[whole_smem, whole_vmem, whole_vmem],
        scratch_shapes=[pltpu.VMEM((kept, kept), f32), pltpu.VMEM((kept, kept), f32)],
        cost_estimate=pl.CostEstimate(
            flops=40 * 10**9, bytes_accessed=2 * 2**20, transcendentals=2**18
        ),
    )(place, queries, kept_rows)


def finish_kernel(weight_ref, plain_ref, targets_ref, out_ref):
    targets = targets_ref[...].reshape(count_rows * group, width)
    out = plain_ref[...] + jnp.dot(
        weight_ref[...], targets, precision=highest, preferred_element_type=f32
    )
    out_ref[...] = out.reshape(4, 8, width)


def finish(weight, plain, targets):
    return call(
        finish_kernel,
        "finish",
        shape((4, 8, width), f32),
        cost_estimate=pl.CostEstimate(
            flops=6 * 2 * 32 * 512 * 128, bytes_accessed=2**19, transcendentals=0
        ),
    )(weight, plain, targets)


def on_device(ref_queries, query_pos, cache_keys, cache_values, kept_index):
    at_x, at_y, at_z = (lax.axis_index(a) for a in seq_axes)
    own = at_y * 4 + at_z
    base = ((at_x * 16 + own) * local_len).astype(jnp.int32)
    place = jnp.stack([at_x, own]).astype(jnp.int32)

    at = query_pos[0]
    pieces = jnp.stack([at & 255, (at >> 8) & 255, at >> 16]).astype(bf16)
    pieces = jnp.pad(jnp.broadcast_to(pieces[:, None], (3, width)), ((0, group - 3), (0, 0)))
    packet = jnp.concatenate(
        [ref_queries.reshape(heads_here, group, width), pieces[None]], 0
    )
    queries = lax.all_to_all(
        jnp.broadcast_to(packet[None], (count_rows,) + packet.shape), seq_axes, 0, 0
    )

    both, kept_parts = prepare(
        kept_index - base,
        cache_keys.reshape(local_len * heads_here, width),
        cache_values.reshape(local_len * heads_here, width),
    )
    kept_parts = lax.all_to_all(kept_parts, seq_axes, 0, 0)
    kept_rows = lax.all_to_all(add_kept(kept_parts), ("y", "z"), 0, 0).reshape(kept, 2 * width)

    parts = lax.all_to_all(attend(base[None], queries, both), seq_axes, 0, 0)
    out, targets = combine(parts)
    targets = lax.all_to_all(targets, seq_axes, 0, 0)
    weight, plain = fit(place, queries, kept_rows)
    fitted = lax.all_to_all(finish(weight, plain, targets), "x", 0, 0)
    return (out.reshape(1, heads_here * group, width), fitted)


def solution(mesh):
    split = Mesh(mesh.devices.reshape(4, 4, 4, 2), seq_axes + ("head",))
    in_specs = (
        P(seq_axes, "head", None),
        P(seq_axes),
        P(seq_axes, "head", None),
        P(seq_axes, "head", None),
        P("head", None),
    )
    out_specs = (P(seq_axes, "head", None), P("head", seq_axes, None))
    return jax.shard_map(
        on_device, mesh=split, in_specs=in_specs, out_specs=out_specs, check_vma=False
    )
```

time: 1940 us -> 146 us (0.08)
  blocking collectives: 906 us -> 9.72 us
  other arithmetic: 613 us -> 2.72 us
  local copies, waits for them, and re-layouts: 191 us -> 2.31 us
  waiting for transfers between devices: 152 us -> 24.1 us
  Pallas kernels: 0 us -> 66.5 us
  matrix products: 41 us -> 0 us
  starting transfers between devices: 0.08 us -> 38.2 us
    all_gather x3 -> x0, blocking collectives: 531 us -> none  [the longest x2 367 us: combined_all(): gathered = jax.tree.map(lambda a: lax.all_gather(a, axis), part)]
    another operation x23 -> x2, other arithmetic: 473 us -> 0.72 us  [the longest x1 0.64 us: on_device(): place = jnp.stack([at_x, own]).astype(jnp.int32)]
    psum x1 -> x0, blocking collectives: 352 us -> none  [on_device(): picked_keys, picked_values = lax.psum((picked_keys, picked_values), 'seq')]
    psum x1 -> x0, waiting for transfers between devices: 152 us -> none  [on_device(): lax.psum((gram_matrix, cross_products_matrix), 'seq')]
    add x132 -> x0, other arithmetic: 127 us -> none  [the longest x63 119 us: combine_parts(): output_one * scale_one[..., None] + output_two * scale_two[..., None]]
    gather x2 -> x0, local copies, waits for them, and re-layouts: 94 us -> none  [the longest x1 82.9 us: on_device(): cache_keys[clipped, head_iota].astype(jnp.float32)]
    pallas_call x0 -> x6, Pallas kernels: none -> 66.5 us  [the longest x1 37.3 us: fit(): call(fit_kernel, 'fit', (shape((32, kept), f32), shape((32, width), f32))...]
    dynamic_slice x190 -> x0, local copies, waits for them, and re-layouts: 56.9 us -> none  [the longest x189 56.9 us: take(): lax.dynamic_index_in_dim(a, source, 0, False)]
  transfers between devices with their start and end apart: 2 -> 5, of which waited for: 1 -> 4; matrix products, arithmetic and copies ran while one was open for 5% -> 1% of each run, Pallas kernels for 0% -> 45%
where the time goes in v1:
time: 146 us; the launch traced here: 145 us
  Pallas kernels  66.5 us (46%)
  starting transfers between devices  38.2 us (26%)
  waiting for transfers between devices  24.1 us (17%)
  blocking collectives  9.72 us (7%)
  other arithmetic  2.72 us (2%)
  local copies, waits for them, and re-layouts  2.31 us (2%)
    pallas_call x1, Pallas kernels, fit(): call(fit_kernel, 'fit', (shape((32, kept), f32), shape((32, width), f32))...  37.3 us
    all_to_all x1, waiting for transfers between devices, on_device(): parts = lax.all_to_all(attend(base[None], queries, both), seq_axes, 0, 0)  14.2 us
    pallas_call x1, Pallas kernels, attend(): call(attend_kernel, 'attend', shape((count_rows, heads_here, group, 2 * w...  11.6 us
    all_to_all x1, starting transfers between devices, on_device(): lax.all_to_all(jnp.broadcast_to(packet[None], (count_rows,) + packet.shap...  11.4 us
    pallas_call x1, Pallas kernels, prepare(): call(prepare_kernel, 'prepare', (shape((heads_here, local_len, 2 * width)...  11.1 us
    all_to_all x1, blocking collectives, on_device(): fitted = lax.all_to_all(finish(weight, plain, targets), 'x', 0, 0)  9.72 us
    all_to_all x1, starting transfers between devices, on_device(): kept_parts = lax.all_to_all(kept_parts, seq_axes, 0, 0)  9.36 us
    all_to_all x1, starting transfers between devices, on_device(): targets = lax.all_to_all(targets, seq_axes, 0, 0)  6.46 us
  transfers between devices with their start and end apart: 5, of which 4 were waited for; matrix products, arithmetic and copies ran while one was open for 1% of the time, Pallas kernels for 45%

profile of v1, /device:TPU:8, one launch (start us, length us, event | category | flops | bytes accessed | tf_op | source)
XLA Modules:
  0.0 145.0 jit_solution(3516613539885737456)
XLA Ops:
  1.3 0.1 select_maximum_fusion
  1.4 0.1 broadcast_in_dim.7
  1.4 0.7 pad_maximum_fusion
  2.1 0.9 broadcast_in_dim.8
  3.1 11.4 %all-to-all-start = ((bf16[64,5,8,128]{3,2,1,0:T(8,128)(2,1)}), bf16[64,5,8,128]{3,2,1,0:T(8,128)(2,1)S(1)}, u32[]{:S(2)}, u32[]{:S(2)}) async-start(bf16[64,5,8,128]{3,2,1,0:T(8,128)(2,1)} %broadcast_in_dim.8), calls=%async_computation | async-start | bytes 1310720 | tf_op jit(solution)/shard_map/all_to_all | solution.py:390
  14.5 1.3 broadcast_subtract_fusion.index_ref
  15.8 11.1 %prepare.1 = (bf16[4,2048,256]{2,1,0:T(8,128)(2,1)}, bf16[64,32,256]{2,1,0:T(8,128)(2,1)}) custom-call(s32[4,512]{1,0:T(4,128)} %broadcast_subtract_fusion.index_ref, bf16[8192,128]{1,0:T(8,128)(2,1)} %bitcast.10, bf16[8192,128]{1,0:T(8,128)(2,1)} %bitcast.11), custom_call_target="tpu_custom_call" | custom-call | flops 4294967296 | bytes 12582912 | tf_op jit(solution)/shard_map/prepare/pallas_call | solution.py:90
  26.9 1.0 all-to-all-done.queries_ref
  27.9 0.0 copy-start.3
  27.9 9.4 %all-to-all-start.2 = ((bf16[64,32,256]{2,1,0:T(8,128)(2,1)}), bf16[64,32,256]{2,1,0:T(8,128)(2,1)S(1)}, u32[]{:S(2)}, u32[]{:S(2)}) async-start(bf16[64,32,256]{2,1,0:T(8,128)(2,1)} %get-tuple-element.10), calls=%async_computation.2 | async-start | bytes 2097152 | tf_op jit(solution)/shard_map/all_to_all | solution.py:399
  37.3 0.0 copy-done.3
  37.3 11.6 %attend.1 = bf16[64,4,8,256]{3,2,1,0:T(8,128)(2,1)} custom-call(s32[1]{0:T(128)} %bitcast.base_ref, bf16[64,5,8,128]{3,2,1,0:T(8,128)(2,1)} %copy-done.3, bf16[4,2048,256]{2,1,0:T(8,128)(2,1)} %get-tuple-element.8.both_ref), custom_call_target="tpu_custom_call" | custom-call | flops 4294967296 | bytes 6291456 | tf_op jit(solution)/shard_map/attend/pallas_call | solution.py:167
  49.0 5.2 %all-to-all-done.2.parts_ref = bf16[64,32,256]{2,1,0:T(8,128)(2,1)S(1)} async-done(((bf16[64,32,256]{2,1,0:T(8,128)(2,1)}), bf16[64,32,256]{2,1,0:T(8,128)(2,1)S(1)}, u32[]{:S(2)}, u32[]{:S(2)}) %all-to-all-start.2) | async-done | bytes 1048608 | tf_op jit(solution)/shard_map/all_to_all | solution.py:399
  54.1 0.0 copy-start
  54.1 6.0 %all-to-all-start.1 = ((bf16[64,4,8,256]{3,2,1,0:T(8,128)(2,1)}), bf16[64,4,8,256]{3,2,1,0:T(8,128)(2,1)S(1)}, u32[]{:S(2)}, u32[]{:S(2)}) async-start(bf16[64,4,8,256]{3,2,1,0:T(8,128)(2,1)} %attend.1), calls=%async_computation.1 | async-start | bytes 2097152 | tf_op jit(solution)/shard_map/all_to_all | solution.py:402
  60.2 0.0 copy-done
  60.2 2.1 %add_kept.1 = bf16[16,32,256]{2,1,0:T(8,128)(2,1)} custom-call(bf16[64,32,256]{2,1,0:T(8,128)(2,1)} %copy-done), custom_call_target="tpu_custom_call" | custom-call | flops 1048576 | bytes 1048576 | tf_op jit(solution)/shard_map/add_kept/pallas_call | solution.py:218
  62.3 14.2 %all-to-all-done.1.parts_ref = bf16[64,4,8,256]{3,2,1,0:T(8,128)(2,1)S(1)} async-done(((bf16[64,4,8,256]{3,2,1,0:T(8,128)(2,1)}), bf16[64,4,8,256]{3,2,1,0:T(8,128)(2,1)S(1)}, u32[]{:S(2)}, u32[]{:S(2)}) %all-to-all-start.1) | async-done | bytes 1048608 | tf_op jit(solution)/shard_map/all_to_all | solution.py:402
  76.5 0.0 copy-start.1
  76.5 4.9 %all-to-all-start.3 = ((bf16[16,32,256]{2,1,0:T(8,128)(2,1)}), bf16[16,32,256]{2,1,0:T(8,128)(2,1)S(1)}, u32[]{:S(2)}, u32[]{:S(2)}) async-start(bf16[16,32,256]{2,1,0:T(8,128)(2,1)} %add_kept.1), calls=%async_computation.3 | async-start | bytes 524288 | tf_op jit(solution)/shard_map/all_to_all | solution.py:400
  81.5 0.6 pad_add_fusion.place_ref
  82.1 0.0 copy-done.1
  82.1 2.5 %combine.1 = (bf16[4,8,128]{2,1,0:T(8,128)(2,1)}, f32[64,8,128]{2,1,0:T(8,128)}) custom-call(bf16[64,4,8,256]{3,2,1,0:T(8,128)(2,1)} %copy-done.1), custom_call_target="tpu_custom_call" | custom-call | flops 2097152 | bytes 2097152 | tf_op jit(solution)/shard_map/combine/pallas_call | solution.py:202
  84.6 3.7 %all-to-all-done.3 = bf16[16,32,256]{2,1,0:T(8,128)(2,1)S(1)} async-done(((bf16[16,32,256]{2,1,0:T(8,128)(2,1)}), bf16[16,32,256]{2,1,0:T(8,128)(2,1)S(1)}, u32[]{:S(2)}, u32[]{:S(2)}) %all-to-all-start.3) | async-done | bytes 262176 | tf_op jit(solution)/shard_map/all_to_all | solution.py:400
  88.3 6.5 %all-to-all-start.4 = ((f32[64,8,128]{2,1,0:T(8,128)}), f32[64,8,128]{2,1,0:T(8,128)S(1)}, u32[]{:S(2)}, u32[]{:S(2)}) async-start(f32[64,8,128]{2,1,0:T(8,128)} %get-tuple-element.13), calls=%async_computation.4 | async-start | bytes 524288 | tf_op jit(solution)/shard_map/all_to_all | solution.py:404
  94.8 0.0 copy-done.4
  94.8 37.3 %fit.1 = (f32[32,512]{1,0:T(8,128)}, f32[32,128]{1,0:T(8,128)}) custom-call(s32[2]{0:T(128)} %pad_add_fusion.place_ref, bf16[64,5,8,128]{3,2,1,0:T(8,128)(2,1)} %copy-done.3, bf16[512,256]{1,0:T(8,128)(2,1)} %bitcast.8), custom_call_target="tpu_custom_call" | custom-call | flops 40000000000 | bytes 2097152 | tf_op jit(solution)/shard_map/fit/pallas_call | solution.py:347
  132.1 0.0 all-to-all-done.4.targets_ref
  132.1 0.7 copy-done.2
  132.8 1.8 %finish.1 = f32[4,8,128]{2,1,0:T(8,128)} custom-call(f32[32,512]{1,0:T(8,128)} %get-tuple-element.11.weight_ref, f32[32,128]{1,0:T(8,128)} %get-tuple-element.12.plain_ref, f32[64,8,128]{2,1,0:T(8,128)} %copy-done.2), custom_call_target="tpu_custom_call" | custom-call | flops 25165824 | bytes 524288 | tf_op jit(solution)/shard_map/finish/pallas_call | solution.py:368
  134.7 9.7 %all_to_all.30 = f32[4,8,128]{2,1,0:T(8,128)S(1)} all-to-all(f32[4,8,128]{2,1,0:T(8,128)} %finish.1), channel_id=1, replica_groups=mesh['x'=4,'y'=4,'z'=4,'head'=2] {'x'}, dimensions={0} | all-to-all | bytes 32768 | tf_op jit(solution)/shard_map/all_to_all | solution.py:406
  144.4 0.6 copy.9
  (2 shorter events, 0.0 us)
Async XLA Ops:
  3.1 24.9 %all-to-all-start = ((bf16[64,5,8,128]{3,2,1,0:T(8,128)(2,1)}), bf16[64,5,8,128]{3,2,1,0:T(8,128)(2,1)S(1)}, u32[]{:S(2)}, u32[]{:S(2)}) async-start(bf16[64,5,8,128]{3,2,1,0:T(8,128)(2,1)} %broadcast_in_dim.8), calls=%async_computation | async-start | bytes 1310720 | tf_op jit(solution)/shard_map/all_to_all | solution.py:390
  27.9 9.4 %copy-start.3 = (bf16[64,5,8,128]{3,2,1,0:T(8,128)(2,1)}, bf16[64,5,8,128]{3,2,1,0:T(8,128)(2,1)S(1)}, u32[]{:S(2)}) copy-start(bf16[64,5,8,128]{3,2,1,0:T(8,128)(2,1)S(1)} %all-to-all-done.queries_ref) | copy-start | bytes 1966084
  27.9 26.2 %all-to-all-start.2 = ((bf16[64,32,256]{2,1,0:T(8,128)(2,1)}), bf16[64,32,256]{2,1,0:T(8,128)(2,1)S(1)}, u32[]{:S(2)}, u32[]{:S(2)}) async-start(bf16[64,32,256]{2,1,0:T(8,128)(2,1)} %get-tuple-element.10), calls=%async_computation.2 | async-start | bytes 2097152 | tf_op jit(solution)/shard_map/all_to_all | solution.py:399
  54.1 6.0 %copy-start = (bf16[64,32,256]{2,1,0:T(8,128)(2,1)}, bf16[64,32,256]{2,1,0:T(8,128)(2,1)S(1)}, u32[]{:S(2)}) copy-start(bf16[64,32,256]{2,1,0:T(8,128)(2,1)S(1)} %all-to-all-done.2.parts_ref) | copy-start | bytes 3145732
  54.1 22.4 %all-to-all-start.1 = ((bf16[64,4,8,256]{3,2,1,0:T(8,128)(2,1)}), bf16[64,4,8,256]{3,2,1,0:T(8,128)(2,1)S(1)}, u32[]{:S(2)}, u32[]{:S(2)}) async-start(bf16[64,4,8,256]{3,2,1,0:T(8,128)(2,1)} %attend.1), calls=%async_computation.1 | async-start | bytes 2097152 | tf_op jit(solution)/shard_map/all_to_all | solution.py:402
  76.5 5.6 %copy-start.1 = (bf16[64,4,8,256]{3,2,1,0:T(8,128)(2,1)}, bf16[64,4,8,256]{3,2,1,0:T(8,128)(2,1)S(1)}, u32[]{:S(2)}) copy-start(bf16[64,4,8,256]{3,2,1,0:T(8,128)(2,1)S(1)} %all-to-all-done.1.parts_ref) | copy-start | bytes 3145732
  76.5 11.8 %all-to-all-start.3 = ((bf16[16,32,256]{2,1,0:T(8,128)(2,1)}), bf16[16,32,256]{2,1,0:T(8,128)(2,1)S(1)}, u32[]{:S(2)}, u32[]{:S(2)}) async-start(bf16[16,32,256]{2,1,0:T(8,128)(2,1)} %add_kept.1), calls=%async_computation.3 | async-start | bytes 524288 | tf_op jit(solution)/shard_map/all_to_all | solution.py:400
  88.3 6.5 %copy-start.4 = (bf16[16,32,256]{2,1,0:T(8,128)(2,1)}, bf16[16,32,256]{2,1,0:T(8,128)(2,1)S(1)}, u32[]{:S(2)}) copy-start(bf16[16,32,256]{2,1,0:T(8,128)(2,1)S(1)} %all-to-all-done.3) | copy-start | bytes 786436
  88.3 43.8 %all-to-all-start.4 = ((f32[64,8,128]{2,1,0:T(8,128)}), f32[64,8,128]{2,1,0:T(8,128)S(1)}, u32[]{:S(2)}, u32[]{:S(2)}) async-start(f32[64,8,128]{2,1,0:T(8,128)} %get-tuple-element.13), calls=%async_computation.4 | async-start | bytes 524288 | tf_op jit(solution)/shard_map/all_to_all | solution.py:404
  132.1 0.7 copy-start.2

commit v2 on v1

v2 whole, which is shorter than its diff:
```python
import functools
import math

import jax
import jax.numpy as jnp
from jax import lax
from jax.experimental import pallas as pl
from jax.experimental.pallas import tpu as pltpu
from jax.sharding import Mesh, PartitionSpec as P

ridge_weight = 0.01
masked_score = -1e30
highest = lax.Precision.HIGHEST
f32 = jnp.float32
bf16 = jnp.bfloat16

seq_axes = ("x", "y", "z")
count_rows = 64
heads_here = 4
group = 8
width = 128
local_len = 2048
kept = 512
chunk = 512
slots = 32
panel = 64
early = 1
scale = width ** (-0.5)
scale_log2 = scale * math.log2(math.e)


def params(mib=56, **more):
    return pltpu.CompilerParams(vmem_limit_bytes=mib * 2**20, **more)


def call(kernel, name, out_shape, **more):
    if "compiler_params" not in more:
        more["compiler_params"] = params()
    return pl.pallas_call(kernel, name=name, out_shape=out_shape, **more)


def shape(dims, dtype):
    return jax.ShapeDtypeStruct(dims, dtype)


whole_vmem = pl.BlockSpec(memory_space=pltpu.VMEM)
whole_smem = pl.BlockSpec(memory_space=pltpu.SMEM)


def spread_index():
    at = [lax.axis_index(name) for name in seq_axes]
    return at[0], at[1] * 4 + at[2]


def own_base():
    plane, own = spread_index()
    return (plane * 16 + own) * local_len


def pack_kernel(pos_ref, index_ref, queries_ref, keys_ref, packet_ref, slot, found, crowd):
    step = pl.program_id(0)
    rows = chunk * heads_here

    @pl.when(step == 0)
    def _():
        local = index_ref[...] - own_base()
        inside = (local >= 0) & (local < local_len)
        row_id = lax.broadcasted_iota(jnp.int32, (kept, kept), 0)
        lane_id = lax.broadcasted_iota(jnp.int32, (kept, kept), 1)
        before = jnp.where(row_id < lane_id, 1.0, 0.0).astype(bf16)
        rank = jnp.dot(
            jnp.where(inside, 1.0, 0.0).astype(bf16), before, preferred_element_type=f32
        )
        rank = jnp.where(inside, rank, -1.0)
        most = jnp.max(jnp.max(rank, axis=1, keepdims=True), axis=0, keepdims=True)
        crowd[...] = jnp.broadcast_to(jnp.where(most >= slots - 1.0, 1.0, 0.0), crowd.shape)
        spot = (local * heads_here + 1).astype(f32)
        slot_id = lax.broadcasted_iota(jnp.int32, (slots, kept), 0).astype(f32)
        for h in range(heads_here):
            mine = jnp.where(rank[h : h + 1] == slot_id, spot[h : h + 1] + float(h), 0.0)
            taken = jnp.sum(mine, axis=1, keepdims=True) - 1.0
            slot[h * slots : (h + 1) * slots] = jnp.broadcast_to(taken, (slots, width))
        found[...] = jnp.zeros(found.shape, f32)

    found[...] += jnp.dot(
        one_hot(slot[...] - (step * rows).astype(f32), rows),
        keys_ref[...],
        preferred_element_type=f32,
    )

    @pl.when(step == local_len // chunk - 1)
    def _():
        at = pos_ref[0]
        sub = lax.broadcasted_iota(jnp.int32, (group, width), 0)
        lane = lax.broadcasted_iota(jnp.int32, (group, width), 1)
        pieces = jnp.where(
            lane == 0, at & 255, jnp.where(lane == 1, (at >> 8) & 255, at >> 16)
        ).astype(f32)
        pieces = jnp.where(lane == 3, crowd[...], pieces)
        for h in range(heads_here):
            sent = found[h * slots : (h + 1) * slots].reshape(4, 8, width)
            last = jnp.where(sub == 7, pieces, sent[3])
            full = jnp.concatenate(
                [queries_ref[...].astype(f32), sent[:3], last[None]], 0
            ).astype(bf16)
            packet_ref[16 * h : 16 * h + 16] = jnp.broadcast_to(full[None], (16,) + full.shape)


def one_hot(wanted, size):
    lane = lax.broadcasted_iota(jnp.int32, wanted.shape, 1).astype(wanted.dtype)
    return jnp.concatenate(
        [
            jnp.where(wanted == lane + g * width, 1.0, 0.0).astype(bf16)
            for g in range(size // width)
        ],
        1,
    )


def pack(query_pos, kept_index, queries, keys):
    rows = chunk * heads_here
    return call(
        pack_kernel,
        "pack",
        (
            shape((count_rows, 8, 8, width), bf16),
            shape((heads_here * slots, width), f32),
        ),
        grid=(local_len // chunk,),
        in_specs=[
            whole_smem,
            pl.BlockSpec((heads_here, kept), lambda i: (0, 0)),
            pl.BlockSpec((heads_here, group, width), lambda i: (0, 0, 0)),
            pl.BlockSpec((rows, width), lambda i: (i, 0)),
        ],
        out_specs=[
            pl.BlockSpec((count_rows, 8, 8, width), lambda i: (0, 0, 0, 0)),
            pl.BlockSpec((heads_here * slots, width), lambda i: (0, 0)),
        ],
        scratch_shapes=[
            pltpu.VMEM((heads_here * slots, width), f32),
            pltpu.VMEM((group, width), f32),
        ],
        cost_estimate=pl.CostEstimate(
            flops=2 * 128 * 8192 * 128, bytes_accessed=3 * 2**20, transcendentals=0
        ),
    )(query_pos, kept_index, queries, keys)


def regroup_kernel(slot_ref, keys_ref, values_ref, both_ref, found_ref, wide, found):
    step = pl.program_id(0)
    rows = chunk * heads_here
    wide[0] = keys_ref[...].astype(f32)
    wide[1] = values_ref[...].astype(f32)
    for h in range(heads_here):
        at = pl.ds(h, chunk, stride=heads_here)
        both_ref[h] = jnp.concatenate([wide[0, at, :], wide[1, at, :]], 1).astype(bf16)

    @pl.when(step == 0)
    def _():
        found[...] = jnp.zeros(found.shape, f32)

    found[...] += jnp.dot(
        one_hot(slot_ref[...] - (step * rows).astype(f32), rows),
        values_ref[...],
        preferred_element_type=f32,
    )

    @pl.when(step == local_len // chunk - 1)
    def _():
        found_ref[...] = found[...].reshape(found_ref.shape).astype(bf16)


def regroup(slot, keys, values):
    rows = chunk * heads_here
    return call(
        regroup_kernel,
        "regroup",
        (
            shape((heads_here, local_len, 2 * width), bf16),
            shape((heads_here, 4, 8, width), bf16),
        ),
        grid=(local_len // chunk,),
        in_specs=[
            pl.BlockSpec((heads_here * slots, width), lambda i: (0, 0)),
            pl.BlockSpec((rows, width), lambda i: (i, 0)),
            pl.BlockSpec((rows, width), lambda i: (i, 0)),
        ],
        out_specs=[
            pl.BlockSpec((heads_here, chunk, 2 * width), lambda i: (0, i, 0)),
            pl.BlockSpec((heads_here, 4, 8, width), lambda i: (0, 0, 0, 0)),
        ],
        scratch_shapes=[
            pltpu.VMEM((2, rows, width), f32),
            pltpu.VMEM((heads_here * slots, width), f32),
        ],
        cost_estimate=pl.CostEstimate(
            flops=2 * 128 * 8192 * 128, bytes_accessed=8 * 2**20, transcendentals=0
        ),
    )(slot, keys, values)


def attend_kernel(queries_ref, both_ref, packet_ref, keys, values, side):
    h = pl.program_id(0)
    lane = lax.broadcasted_iota(jnp.int32, (local_len, width), 1)

    @pl.when(h == 0)
    def _():
        pieces = queries_ref[:, 7].astype(f32)[:, 7]
        row_id = lax.broadcasted_iota(jnp.int32, (count_rows, width), 0)
        lane_id = lax.broadcasted_iota(jnp.int32, (count_rows, width), 1)
        place = pieces[:, 0:1] + 256.0 * pieces[:, 1:2] + 65536.0 * pieces[:, 2:3]
        place = jnp.sum(jnp.where(row_id == lane_id, place, 0.0), axis=0, keepdims=True)
        spot = lax.broadcasted_iota(jnp.int32, (local_len, width), 0) + own_base()
        late = (spot.astype(f32) > place) & (lane < count_rows)
        keys[:, width:] = jnp.where(late, masked_score, 0.0).astype(bf16)
        values[:, width:] = jnp.where(lane == 0, 1.0, 0.0).astype(bf16)
        side[...] = jnp.zeros(side.shape, f32)

    keys[:, :width] = both_ref[0, :, :width]
    values[:, :width] = both_ref[0, :, width:]
    q = queries_ref[:, h].astype(f32).reshape(count_rows * group, width)
    tile = 256
    lane_t = lax.broadcasted_iota(jnp.int32, (tile, width), 1)
    row_t = lax.broadcasted_iota(jnp.int32, (tile, width), 0)

    def scores(part):
        own = jnp.where(row_t // group + part * (tile // group) == lane_t, 1.0, 0.0)
        q_part = jnp.concatenate([q[part * tile : (part + 1) * tile], own], 1).astype(bf16)
        return lax.dot_general(
            q_part, keys[...], (((1,), (1,)), ((), ())), preferred_element_type=f32
        )

    parts = count_rows * group // tile
    s = scores(0)
    for part in range(parts):
        after = scores(part + 1) if part + 1 < parts else None
        peak = jnp.max(s, axis=1, keepdims=True)
        w = jnp.exp2((s - peak) * scale_log2).astype(bf16)
        o = jnp.dot(w, values[...], preferred_element_type=f32)
        sums = o[:, width : width + 1]
        mass = peak * scale_log2 + jnp.log2(sums)
        high = mass.astype(bf16).astype(f32)
        middle = (mass - high).astype(bf16).astype(f32)
        low = mass - high - middle
        first = 3 * h
        mark = jnp.where(
            lane_t == first,
            high,
            jnp.where(lane_t == first + 1, middle, jnp.where(lane_t == first + 2, low, 0.0)),
        )
        rows = tile // group
        own = slice(part * rows, (part + 1) * rows)
        side[own] += mark.reshape(rows, group, width)
        packet_ref[own, h] = (o[:, :width] / sums).reshape(rows, group, width).astype(bf16)
        s = after

    @pl.when(h == heads_here - 1)
    def _():
        packet_ref[:, heads_here] = side[...].astype(bf16)


def attend(packets, both):
    return call(
        attend_kernel,
        "attend",
        shape((count_rows, heads_here + 1, group, width), bf16),
        grid=(heads_here,),
        in_specs=[
            pl.BlockSpec((count_rows, 8, group, width), lambda h: (0, 0, 0, 0)),
            pl.BlockSpec((1, local_len, 2 * width), lambda h: (h, 0, 0)),
        ],
        out_specs=pl.BlockSpec(
            (count_rows, heads_here + 1, group, width), lambda h: (0, 0, 0, 0)
        ),
        scratch_shapes=[
            pltpu.VMEM((local_len, 2 * width), bf16),
            pltpu.VMEM((local_len, 2 * width), bf16),
            pltpu.VMEM((count_rows, group, width), f32),
        ],
        cost_estimate=pl.CostEstimate(
            flops=2 * 2 * 512 * 2048 * 256 * 4,
            bytes_accessed=6 * 2**20,
            transcendentals=4 * 512 * 2048,
        ),
    )(packets, both)


def combine_kernel(parts_ref, values_ref, out_ref, spread_ref):
    side = parts_ref[:, heads_here].astype(f32)
    lane = lax.broadcasted_iota(jnp.int32, side.shape, 2)
    for h in range(heads_here):
        part = parts_ref[:, h].astype(f32)
        own = (lane >= 3 * h) & (lane < 3 * h + 3)
        mass = jnp.sum(jnp.where(own, side, 0.0), axis=2, keepdims=True)
        top = jnp.max(mass, axis=0, keepdims=True)
        share = jnp.exp2(mass - top)
        full = jnp.sum(share * part, axis=0) / jnp.sum(share, axis=0)
        high = full.astype(bf16)
        out_ref[h] = high
        low = (full - high.astype(f32)).astype(bf16)
        sent = jnp.concatenate([high[None], low[None], values_ref[h]], 0)
        spread_ref[16 * h : 16 * h + 16] = jnp.broadcast_to(sent[None], (16,) + sent.shape)


def combine(parts, kept_values):
    return call(
        combine_kernel,
        "combine",
        (
            shape((heads_here, group, width), bf16),
            shape((count_rows, 6, group, width), bf16),
        ),
        cost_estimate=pl.CostEstimate(
            flops=2 * 2**20, bytes_accessed=2 * 2**20, transcendentals=2048
        ),
    )(parts, kept_values)


def reciprocal(x):
    r = pltpu.reciprocal(x, approx=True)
    return r * (2.0 - x * r)


def eliminate(w, o, size):
    p, q, s = w[o, o], w[o, o + 1], w[o + 1, o + 1]
    r = reciprocal(p * s - q * q)
    side = range(o + 2, size)
    turned = {u: (s * w[o, u] - q * w[o + 1, u], p * w[o + 1, u] - q * w[o, u]) for u in side}
    left = {}
    for u in side:
        for v in range(u, size):
            left[u, v] = w[u, v] - (w[o, u] * turned[v][0] + w[o + 1, u] * turned[v][1]) * r
    return left, turned, (s * r, -q * r, p * r), r


def invert_block(a, n, h):
    b = 4
    lane = lax.broadcasted_iota(jnp.int32, (8, n), 1)
    sub = lax.broadcasted_iota(jnp.int32, (8, n), 0)
    lane_n = lax.broadcasted_iota(jnp.int32, (n, n), 1)

    def over(v, r):
        return jnp.broadcast_to(v[r % 8 : r % 8 + 1, :], (8, n))

    for first in range(0, n, h):
        tiles = [a[first + 8 * i : first + 8 * i + 8, :] for i in range(h // 8)]
        d = None
        for k in range(first, first + h, b):
            at, off = (k - first) // 8, k % 8
            last = k + b >= first + h
            columns = [
                [jnp.broadcast_to(tile[:, k + s : k + s + 1], (8, n)) for tile in tiles]
                for s in range(b)
            ]
            if d is None:
                d = {(s, t): over(columns[s][at], k + t) for s in range(b) for t in range(s, b)}
            w = dict(d)
            if not last:
                then = (k + b - first) // 8
                for s in range(b):
                    for t in range(b):
                        w[s, b + t] = over(columns[s][then], k + b + t)
                    ahead = jnp.broadcast_to(
                        tiles[then][:, k + b + s : k + b + s + 1], (8, n)
                    )
                    for t in range(s, b):
                        w[b + s, b + t] = over(ahead, k + b + t)
            inside = (lane >= k) & (lane < k + b)
            rows = [
                jnp.where(lane == k + s, 1.0, jnp.where(inside, 0.0, over(tiles[at], off + s)))
                for s in range(b)
            ]
            size = b if last else 2 * b
            w1, turned, (i00, i01, i11), r1 = eliminate(w, 0, size)
            w2, _, (j00, j01, j11), _ = eliminate(w1, 2, size)
            n0 = i00 * rows[0] + i01 * rows[1]
            n1 = i01 * rows[0] + i11 * rows[1]
            m2 = rows[2] - (w[0, 2] * n0 + w[1, 2] * n1)
            m3 = rows[3] - (w[0, 3] * n0 + w[1, 3] * n1)
            n2 = j00 * m2 + j01 * m3
            n3 = j01 * m2 + j11 * m3
            n0 = n0 - (turned[2][0] * r1 * n2 + turned[3][0] * r1 * n3)
            n1 = n1 - (turned[2][1] * r1 * n2 + turned[3][1] * r1 * n3)
            new = [n0, n1, n2, n3]
            if not last:
                d = {(s, t): w2[b + s, b + t] for s in range(b) for t in range(s, b)}
            after = []
            for i, tile in enumerate(tiles):
                c = [columns[s][i] for s in range(b)]
                left = jnp.where(inside, 0.0, tile) - (
                    (c[0] * n0 + c[1] * n1) + (c[2] * n2 + c[3] * n3)
                )
                if i == at:
                    for s in range(b):
                        left = jnp.where(sub == off + s, new[s], left)
                after.append(left)
            tiles = after
        r = jnp.concatenate(tiles, 0)
        inside_n = (lane_n >= first) & (lane_n < first + h)
        rest = jnp.where(inside_n, 0.0, a) - jnp.dot(
            a[:, first : first + h], r, precision=highest, preferred_element_type=f32
        )
        pieces = ([rest[:first]] if first else []) + [r]
        a = jnp.concatenate(pieces + ([rest[first + h :]] if first + h < n else []), 0)
    return a


def block_steps(a, d, left, r, first, stop):
    n = 128
    row = lax.broadcasted_iota(jnp.int32, (n, n), 0)
    column = lax.broadcasted_iota(jnp.int32, (n, n), 1)
    eye = jnp.where(row == column, 1.0, 0.0)

    def step(k, _):
        at = pl.ds(pl.multiple_of(k * n, n), n)
        then = pl.ds(pl.multiple_of(jnp.minimum(k + 1, kept // n - 1) * n, n), n)
        a[...] -= jnp.dot(left[...], r[...], precision=highest, preferred_element_type=f32)
        p = invert_block(d[...], n, panel)
        a[at, at] = -eye
        left[...] = a[:, at]
        a[:, at] = jnp.zeros((kept, n), f32)
        a[at, at] = eye
        r[...] = jnp.dot(p, a[at, :], precision=highest, preferred_element_type=f32)
        a[at, :] = jnp.zeros((n, kept), f32)
        d[...] = a[then, then] - jnp.dot(
            left[then, :], r[:, then], precision=highest, preferred_element_type=f32
        )
        return 0

    lax.fori_loop(first, stop, step, 0)


def gram_kernel(flag_ref, index_ref, packets_ref, dense_ref, slot_ref, mixing, a, d, left, r, keys):
    head = spread_index()[0]
    index = index_ref[pl.ds(head, 1), :]
    holder = jnp.broadcast_to(index >> 11, (width, kept))
    down = holder.T
    row = lax.broadcasted_iota(jnp.int32, (kept, width), 0)
    lane = lax.broadcasted_iota(jnp.int32, (kept, width), 1)
    same = jnp.zeros((kept, width), f32)
    for g in range(kept // width):
        across = holder[:1, g * width : (g + 1) * width]
        same += jnp.where((down == across) & (lane + g * width < row), 1.0, 0.0)
    rank = jnp.sum(same, axis=1, keepdims=True)
    slot_ref[...] = (down * slots).astype(f32) + rank
    sent = packets_ref[:, heads_here:].astype(f32).reshape(count_rows * slots, width).astype(bf16)
    keys[...] = jnp.dot(
        one_hot(slot_ref[...], count_rows * slots), sent, preferred_element_type=f32
    ).astype(bf16)

    @pl.when(flag_ref[0] > 0)
    def _():
        keys[...] = dense_ref[:, :width]

    q = packets_ref[:, head].astype(f32).reshape(count_rows * group, width).astype(bf16)
    s = lax.dot_general(
        keys[...], q, (((1,), (1,)), ((), ())), preferred_element_type=f32
    )
    e = jnp.exp((s - jnp.max(s, axis=0, keepdims=True)) * scale)
    mixing[...] = e / jnp.sum(e, axis=0, keepdims=True)
    row = lax.broadcasted_iota(jnp.int32, (kept, kept), 0)
    column = lax.broadcasted_iota(jnp.int32, (kept, kept), 1)
    a[...] = lax.dot_general(
        mixing[...],
        mixing[...],
        (((1,), (1,)), ((), ())),
        precision=highest,
        preferred_element_type=f32,
    ) + jnp.where(row == column, ridge_weight, 0.0)
    n = 128
    d[...] = a[:n, :n]
    left[...] = jnp.zeros(left.shape, f32)
    r[...] = jnp.zeros(r.shape, f32)
    if early:
        block_steps(a, d, left, r, 0, early)


def gram(flag, kept_index, packets, dense):
    n = 128
    return call(
        gram_kernel,
        "gram",
        (
            shape((kept, width), f32),
            shape((kept, kept), f32),
            shape((kept, kept), f32),
            shape((n, n), f32),
            shape((kept, n), f32),
            shape((n, kept), f32),
        ),
        in_specs=[whole_smem] + [whole_vmem] * 3,
        out_specs=tuple([whole_vmem] * 6),
        scratch_shapes=[pltpu.VMEM((kept, width), bf16)],
        cost_estimate=pl.CostEstimate(
            flops=10**10, bytes_accessed=6 * 2**20, transcendentals=2**18
        ),
    )(flag, kept_index, packets, dense)


def in_pieces(x):
    high = x.astype(bf16)
    rest = x - high.astype(f32)
    middle = rest.astype(bf16)
    low = (rest - middle.astype(f32)).astype(bf16)
    return jnp.concatenate([high, middle, low], 0)


def weigh_kernel(
    flag_ref, slot_ref, mixing, a_ref, d_ref, left_ref, r_ref, dense_ref,
    weight_ref, share_ref, plain_ref, a, d, left, r,
):
    a[...] = a_ref[...]
    d[...] = d_ref[...]
    left[...] = left_ref[...]
    r[...] = r_ref[...]
    own = spread_index()[1]
    block_steps(a, d, left, r, early, 4)
    rows = [pl.ds(pl.multiple_of(128 * i + 8 * own, 8), 8) for i in range(4)]
    picked = jnp.concatenate([a[at, :] for at in rows], 0)
    picked -= jnp.dot(
        jnp.concatenate([left[at, :] for at in rows], 0),
        r[...],
        precision=highest,
        preferred_element_type=f32,
    )
    weight_ref[...] = in_pieces(
        jnp.dot(picked, mixing[...], precision=highest, preferred_element_type=f32)
    )

    @pl.when(flag_ref[0] == 0)
    def _():
        hot = one_hot(slot_ref[...], count_rows * slots)
        share_ref[...] = jnp.dot(
            in_pieces(ridge_weight * picked), hot, preferred_element_type=f32
        ).astype(bf16)
        plain_ref[...] = jnp.zeros(plain_ref.shape, f32)

    @pl.when(flag_ref[0] > 0)
    def _():
        share_ref[...] = jnp.zeros(share_ref.shape, bf16)
        plain_ref[...] = jnp.dot(
            ridge_weight * picked,
            dense_ref[:, width:].astype(f32),
            precision=highest,
            preferred_element_type=f32,
        )


def weigh(flag, slot, mixing, a, d, left, r, dense):
    n = 128
    return call(
        weigh_kernel,
        "weigh",
        (
            shape((96, kept), bf16),
            shape((96, count_rows * slots), bf16),
            shape((32, width), f32),
        ),
        in_specs=[whole_smem] + [whole_vmem] * 7,
        scratch_shapes=[
            pltpu.VMEM((kept, kept), f32),
            pltpu.VMEM((n, n), f32),
            pltpu.VMEM((kept, n), f32),
            pltpu.VMEM((n, kept), f32),
        ],
        cost_estimate=pl.CostEstimate(
            flops=2 * 10**10, bytes_accessed=6 * 2**20, transcendentals=0
        ),
    )(flag, slot, mixing, a, d, left, r, dense)


def finish_kernel(weight_ref, share_ref, plain_ref, sent_ref, out_ref):
    sent = sent_ref[...].astype(f32)
    targets = jnp.concatenate(
        [sent[:, i].reshape(count_rows * group, width) for i in range(2)], 1
    ).astype(bf16)
    values = sent[:, 2:].reshape(count_rows * slots, width).astype(bf16)
    fitted = jnp.dot(weight_ref[...], targets, preferred_element_type=f32)
    shared = jnp.dot(share_ref[...], values, preferred_element_type=f32)
    total = fitted[:, :width] + fitted[:, width:] + shared
    total = total[:32] + total[32:64] + total[64:] + plain_ref[...]
    out_ref[...] = total.reshape(4, 8, width)


def finish(weight, share, plain, sent):
    return call(
        finish_kernel,
        "finish",
        shape((4, 8, width), f32),
        cost_estimate=pl.CostEstimate(
            flops=2 * 96 * 2560 * 256, bytes_accessed=2**20, transcendentals=0
        ),
    )(weight, share, plain, sent)


def dense_rows(kept_index, cache_keys, cache_values):
    local_index = kept_index - own_base()
    inside = (local_index >= 0) & (local_index < local_len)
    at = jnp.clip(local_index, 0, local_len - 1)
    head = jnp.arange(heads_here, dtype=jnp.int32)[:, None]
    rows = jnp.concatenate([cache_keys[at, head], cache_values[at, head]], -1)
    rows = jnp.where(inside[..., None], rows, 0).reshape(count_rows, 32, 2 * width)
    parts = lax.all_to_all(rows, seq_axes, 0, 0)
    found = jnp.sum(parts.astype(f32), axis=0).astype(bf16)
    found = jnp.broadcast_to(found[None], (16,) + found.shape)
    return lax.all_to_all(found, ("y", "z"), 0, 0).reshape(kept, 2 * width)


def on_device(ref_queries, query_pos, cache_keys, cache_values, kept_index):
    keys = cache_keys.reshape(local_len * heads_here, width)
    values = cache_values.reshape(local_len * heads_here, width)
    packets, slot = pack(
        query_pos, kept_index, ref_queries.reshape(heads_here, group, width), keys
    )
    packets = lax.all_to_all(packets, seq_axes, 0, 0)
    both, kept_values = regroup(slot, keys, values)
    crowded = jnp.max(packets[:, 7, 7, 3].astype(f32)) > 0.0
    dense = lax.cond(
        crowded,
        dense_rows,
        lambda *_: jnp.zeros((kept, 2 * width), bf16),
        kept_index,
        cache_keys,
        cache_values,
    )
    flag = crowded.astype(jnp.int32)[None]

    parts = lax.all_to_all(attend(packets, both), seq_axes, 0, 0)
    state = gram(flag, kept_index, packets, dense)
    out, sent = combine(parts, kept_values)
    sent = lax.all_to_all(sent, seq_axes, 0, 0)
    fitted = finish(*weigh(flag, *state, dense), sent)
    fitted = lax.all_to_all(fitted, "x", 0, 0)
    return (out.reshape(1, heads_here * group, width), fitted)


def solution(mesh):
    split = Mesh(mesh.devices.reshape(4, 4, 4, 2), seq_axes + ("head",))
    in_specs = (
        P(seq_axes, "head", None),
        P(seq_axes),
        P(seq_axes, "head", None),
        P(seq_axes, "head", None),
        P("head", None),
    )
    out_specs = (P(seq_axes, "head", None), P("head", seq_axes, None))
    return jax.shard_map(
        on_device, mesh=split, in_specs=in_specs, out_specs=out_specs, check_vma=False
    )
```

time: 146 us -> 110 us (0.75)
  starting transfers between devices: 38.2 us -> 26 us
  Pallas kernels: 66.5 us -> 54.6 us
  waiting for transfers between devices: 24.1 us -> 13.6 us
  other arithmetic: 2.72 us -> 0.85 us
    pallas_call x4 -> x5, Pallas kernels: 62.2 us -> 49.8 us  [the longest x1 18.7 us: weigh(): call(weigh_kernel, 'weigh', (shape((96, kept), bf16), shape((96, count_ro...]
    all_to_all x5 -> x3, starting transfers between devices: 38.2 us -> 26 us  [the longest x1 11.4 us: on_device(): packets = lax.all_to_all(packets, seq_axes, 0, 0)]
    all_to_all x5 -> x3, waiting for transfers between devices: 24.1 us -> 13.6 us  [the longest x1 11.9 us: on_device(): packets = lax.all_to_all(packets, seq_axes, 0, 0)]
  transfers between devices with their start and end apart: 5 -> 3, of which waited for: 4 -> 2; matrix products, arithmetic and copies ran while one was open for 1% -> 0% of each run, Pallas kernels for 45% -> 32%
where the time goes in v2:
time: 110 us; the launch traced here: 109 us
  Pallas kernels  54.6 us (50%)
  starting transfers between devices  26 us (24%)
  waiting for transfers between devices  13.6 us (12%)
  blocking collectives  9.73 us (9%)
  local copies, waits for them, and re-layouts  2.37 us (2%)
  between operations  2.02 us (2%)
    pallas_call x1, Pallas kernels, weigh(): call(weigh_kernel, 'weigh', (shape((96, kept), bf16), shape((96, count_ro...  18.7 us
    all_to_all x1, waiting for transfers between devices, on_device(): packets = lax.all_to_all(packets, seq_axes, 0, 0)  11.9 us
    all_to_all x1, starting transfers between devices, on_device(): packets = lax.all_to_all(packets, seq_axes, 0, 0)  11.4 us
    pallas_call x1, Pallas kernels, gram(): call(gram_kernel, 'gram', (shape((kept, width), f32), shape((kept, kept),...  11 us
    pallas_call x1, Pallas kernels, attend(): call(attend_kernel, 'attend', shape((count_rows, heads_here + 1, group, w...  10 us
    all_to_all x1, blocking collectives, on_device(): fitted = lax.all_to_all(fitted, 'x', 0, 0)  9.73 us
    all_to_all x1, starting transfers between devices, on_device(): sent = lax.all_to_all(sent, seq_axes, 0, 0)  8.74 us
    all_to_all x1, starting transfers between devices, on_device(): parts = lax.all_to_all(attend(packets, both), seq_axes, 0, 0)  5.84 us
  transfers between devices with their start and end apart: 3, of which 2 were waited for; matrix products, arithmetic and copies ran while one was open for 0% of the time, Pallas kernels for 32%

profile of v2, /device:TPU:8, one launch (start us, length us, event | category | flops | bytes accessed | tf_op | source)
XLA Modules:
  0.0 109.1 jit_solution(3673284921470592305)
XLA Ops:
  1.3 0.0 copy-start
  1.3 4.6 %pack.1 = (bf16[64,8,8,128]{3,2,1,0:T(8,128)(2,1)}, f32[128,128]{1,0:T(8,128)}) custom-call(s32[1]{0:T(128)S(6)} %copy.11.pos_ref, s32[4,512]{1,0:T(4,128)} %index_ref.3, bf16[4,8,128]{2,1,0:T(8,128)(2,1)} %bitcast.26, bf16[8192,128]{1,0:T(8,128)(2,1)} %bitcast.20), custom_call_target="tpu_custom_call" | custom-call | flops 268435456 | bytes 3145728 | tf_op jit(solution)/shard_map/pack/pallas_call | solution.py:122
  5.9 11.4 %all-to-all-start.2 = ((bf16[64,8,8,128]{3,2,1,0:T(8,128)(2,1)}), bf16[64,8,8,128]{3,2,1,0:T(8,128)(2,1)S(1)}, u32[]{:S(2)}, u32[]{:S(2)}) async-start(bf16[64,8,8,128]{3,2,1,0:T(8,128)(2,1)} %get-tuple-element.29), calls=%async_computation.2 | async-start | bytes 2097152 | tf_op jit(solution)/shard_map/all_to_all | solution.py:616
  17.3 0.0 copy-done
  17.4 0.0 copy-start.4
  17.4 5.4 %regroup.1 = (bf16[4,2048,256]{2,1,0:T(8,128)(2,1)}, bf16[4,4,8,128]{3,2,1,0:T(8,128)(2,1)}) custom-call(f32[128,128]{1,0:T(8,128)} %get-tuple-element.30.slot_ref, bf16[8192,128]{1,0:T(8,128)(2,1)S(1)} %bitcast.21, bf16[8192,128]{1,0:T(8,128)(2,1)} %bitcast.22), custom_call_target="tpu_custom_call" | custom-call | flops 268435456 | bytes 8388608 | tf_op jit(solution)/shard_map/regroup/pallas_call | solution.py:176
  22.8 11.9 %all-to-all-done.2.queries_ref.packets_ref = bf16[64,8,8,128]{3,2,1,0:T(8,128)(2,1)S(1)} async-done(((bf16[64,8,8,128]{3,2,1,0:T(8,128)(2,1)}), bf16[64,8,8,128]{3,2,1,0:T(8,128)(2,1)S(1)}, u32[]{:S(2)}, u32[]{:S(2)}) %all-to-all-start.2) | async-done | bytes 1048608 | tf_op jit(solution)/shard_map/all_to_all | solution.py:616
  34.7 0.0 copy-start.3
  34.7 0.9 slice_reduce_fusion
  36.2 0.0 copy-done.4
  36.3 0.0 copy-done.3
  36.3 10.0 %attend.1 = bf16[64,5,8,128]{3,2,1,0:T(8,128)(2,1)} custom-call(bf16[64,8,8,128]{3,2,1,0:T(8,128)(2,1)} %copy-done.3, bf16[4,2048,256]{2,1,0:T(8,128)(2,1)} %get-tuple-element.31.both_ref), custom_call_target="tpu_custom_call" | custom-call | flops 4294967296 | bytes 6291456 | tf_op jit(solution)/shard_map/attend/pallas_call | solution.py:264
  46.3 5.8 %all-to-all-start.3 = ((bf16[64,5,8,128]{3,2,1,0:T(8,128)(2,1)}), bf16[64,5,8,128]{3,2,1,0:T(8,128)(2,1)S(1)}, u32[]{:S(2)}, u32[]{:S(2)}) async-start(bf16[64,5,8,128]{3,2,1,0:T(8,128)(2,1)} %attend.1), calls=%async_computation.3 | async-start | bytes 1310720 | tf_op jit(solution)/shard_map/all_to_all | solution.py:629
  52.2 11.0 %gram.1 = (f32[512,128]{1,0:T(8,128)}, f32[512,512]{1,0:T(8,128)}, f32[512,512]{1,0:T(8,128)}, f32[128,128]{1,0:T(8,128)}, f32[512,128]{1,0:T(8,128)}, /*index=5*/f32[128,512]{1,0:T(8,128)}) custom-call(s32[1]{0:T(128)} %bitcast.8.flag_ref, s32[4,512]{1,0:T(4,128)S(1)} %copy-done.4, bf16[64,8,8,128]{3,2,1,0:T(8,128)(2,1)} %copy-done.3, ...), custom_call_target="tpu_custom_call" | custom-call | flops 10000000000 | bytes 6291456 | tf_op jit(solution)/shard_map/gram/pallas_call | solution.py:481
  63.1 1.6 %all-to-all-done.3.parts_ref = bf16[64,5,8,128]{3,2,1,0:T(8,128)(2,1)S(1)} async-done(((bf16[64,5,8,128]{3,2,1,0:T(8,128)(2,1)}), bf16[64,5,8,128]{3,2,1,0:T(8,128)(2,1)S(1)}, u32[]{:S(2)}, u32[]{:S(2)}) %all-to-all-start.3) | async-done | bytes 655392 | tf_op jit(solution)/shard_map/all_to_all | solution.py:629
  64.7 0.0 copy-start.2
  64.8 0.8 copy-done.2
  65.6 2.6 %combine.1 = (bf16[4,8,128]{2,1,0:T(8,128)(2,1)}, bf16[64,6,8,128]{3,2,1,0:T(8,128)(2,1)}) custom-call(bf16[64,5,8,128]{3,2,1,0:T(8,128)(2,1)} %copy-done.2, bf16[4,4,8,128]{3,2,1,0:T(8,128)(2,1)} %get-tuple-element.32.values_ref), custom_call_target="tpu_custom_call" | custom-call | flops 2097152 | bytes 2097152 | tf_op jit(solution)/shard_map/combine/pallas_call | solution.py:307
  68.2 8.7 %all-to-all-start.4 = ((bf16[64,6,8,128]{3,2,1,0:T(8,128)(2,1)}), bf16[64,6,8,128]{3,2,1,0:T(8,128)(2,1)S(1)}, u32[]{:S(2)}, u32[]{:S(2)}) async-start(bf16[64,6,8,128]{3,2,1,0:T(8,128)(2,1)} %get-tuple-element.43), calls=%async_computation.4 | async-start | bytes 1572864 | tf_op jit(solution)/shard_map/all_to_all | solution.py:632
  76.9 18.7 %weigh.1 = (bf16[96,512]{1,0:T(8,128)(2,1)}, bf16[96,2048]{1,0:T(8,128)(2,1)}, f32[32,128]{1,0:T(8,128)}) custom-call(s32[1]{0:T(128)} %bitcast.8.flag_ref, f32[512,128]{1,0:T(8,128)} %get-tuple-element.34.slot_ref, f32[512,512]{1,0:T(8,128)} %get-tuple-element.35.mixing, f32[512,512]{1,0:T(8,128)} %get-tuple-element.36.a_ref, ...), custom_call_target="tpu_custom_call" | custom-call | flops 20000000000 | bytes 6291456 | tf_op jit(solution)/shard_map/weigh/pallas_call | solution.py:552
  95.6 0.0 all-to-all-done.4.sent_ref
  95.6 0.0 copy-start.1
  95.7 0.9 copy-done.1
  96.5 2.2 %finish.1 = f32[4,8,128]{2,1,0:T(8,128)} custom-call(bf16[96,512]{1,0:T(8,128)(2,1)} %get-tuple-element.40.weight_ref, bf16[96,2048]{1,0:T(8,128)(2,1)} %get-tuple-element.41.share_ref, f32[32,128]{1,0:T(8,128)} %get-tuple-element.42.plain_ref, bf16[64,6,8,128]{3,2,1,0:T(8,128)(2,1)} %copy-done.1), custom_call_target="tpu_custom_call" | custom-call | flops 125829120 | bytes 1048576 | tf_op jit(solution)/shard_map/finish/pallas_call | solution.py:587
  98.8 9.7 %all_to_all.30 = f32[4,8,128]{2,1,0:T(8,128)S(1)} all-to-all(f32[4,8,128]{2,1,0:T(8,128)} %finish.1), channel_id=1, replica_groups=mesh['x'=4,'y'=4,'z'=4,'head'=2] {'x'}, dimensions={0} | all-to-all | bytes 32768 | tf_op jit(solution)/shard_map/all_to_all | solution.py:634
  108.5 0.6 copy.12
  (2 shorter events, 0.1 us)
Async XLA Ops:
  1.3 16.1 %copy-start = (bf16[2048,4,128]{2,1,0:T(4,128)(2,1)S(1)}, bf16[2048,4,128]{2,1,0:T(4,128)(2,1)}, u32[]{:S(2)}) copy-start(bf16[2048,4,128]{2,1,0:T(4,128)(2,1)} %param.9) | copy-start | bytes 6291460
  5.9 28.8 %all-to-all-start.2 = ((bf16[64,8,8,128]{3,2,1,0:T(8,128)(2,1)}), bf16[64,8,8,128]{3,2,1,0:T(8,128)(2,1)S(1)}, u32[]{:S(2)}, u32[]{:S(2)}) async-start(bf16[64,8,8,128]{3,2,1,0:T(8,128)(2,1)} %get-tuple-element.29), calls=%async_computation.2 | async-start | bytes 2097152 | tf_op jit(solution)/shard_map/all_to_all | solution.py:616
  17.4 18.9 %copy-start.4 = (s32[4,512]{1,0:T(4,128)S(1)}, s32[4,512]{1,0:T(4,128)}, u32[]{:S(2)}) copy-start(s32[4,512]{1,0:T(4,128)} %index_ref.3) | copy-start | bytes 24580
  34.7 1.5 %copy-start.3 = (bf16[64,8,8,128]{3,2,1,0:T(8,128)(2,1)}, bf16[64,8,8,128]{3,2,1,0:T(8,128)(2,1)S(1)}, u32[]{:S(2)}) copy-start(bf16[64,8,8,128]{3,2,1,0:T(8,128)(2,1)S(1)} %all-to-all-done.2.queries_ref.packets_ref) | copy-start | bytes 3145732
  46.3 18.4 %all-to-all-start.3 = ((bf16[64,5,8,128]{3,2,1,0:T(8,128)(2,1)}), bf16[64,5,8,128]{3,2,1,0:T(8,128)(2,1)S(1)}, u32[]{:S(2)}, u32[]{:S(2)}) async-start(bf16[64,5,8,128]{3,2,1,0:T(8,128)(2,1)} %attend.1), calls=%async_computation.3 | async-start | bytes 1310720 | tf_op jit(solution)/shard_map/all_to_all | solution.py:629
  64.7 0.8 copy-start.2
  68.2 27.5 %all-to-all-start.4 = ((bf16[64,6,8,128]{3,2,1,0:T(8,128)(2,1)}), bf16[64,6,8,128]{3,2,1,0:T(8,128)(2,1)S(1)}, u32[]{:S(2)}, u32[]{:S(2)}) async-start(bf16[64,6,8,128]{3,2,1,0:T(8,128)(2,1)} %get-tuple-element.43), calls=%async_computation.4 | async-start | bytes 1572864 | tf_op jit(solution)/shard_map/all_to_all | solution.py:632
  95.6 0.9 copy-start.1

commit v3 on v2

--- a/solution.py
+++ b/solution.py
@@ -22,20 +22,19 @@
 local_len = 2048
 kept = 512
 chunk = 512
-slots = 32
+slots = 24
+slot_tiles = slots // 8
 panel = 64
 early = 1
 scale = width ** (-0.5)
 scale_log2 = scale * math.log2(math.e)
 
 
-def params(mib=56, **more):
-    return pltpu.CompilerParams(vmem_limit_bytes=mib * 2**20, **more)
+def params(mib):
+    return pltpu.CompilerParams(vmem_limit_bytes=mib * 2**20)
 
 
 def call(kernel, name, out_shape, **more):
-    if "compiler_params" not in more:
-        more["compiler_params"] = params()
     return pl.pallas_call(kernel, name=name, out_shape=out_shape, **more)
 
 
@@ -45,6 +44,8 @@
 
 whole_vmem = pl.BlockSpec(memory_space=pltpu.VMEM)
 whole_smem = pl.BlockSpec(memory_space=pltpu.SMEM)
+whole_any = pl.BlockSpec(memory_space=pl.ANY)
+whole_hbm = pl.BlockSpec(memory_space=pltpu.HBM)
 
 
 def spread_index():
@@ -57,7 +58,10 @@
     return (plane * 16 + own) * local_len
 
 
-def pack_kernel(pos_ref, index_ref, queries_ref, keys_ref, packet_ref, slot, found, crowd):
+def pack_kernel(
+    pos_ref, index_ref, queries_ref, keys_ref, values_ref, packet_ref, *refs
+):
+    later_refs, (slot, found, crowd) = refs[:4], refs[4:]
     step = pl.program_id(0)
     rows = chunk * heads_here
 
@@ -84,7 +88,7 @@
 
     found[...] += jnp.dot(
         one_hot(slot[...] - (step * rows).astype(f32), rows),
-        keys_ref[...],
+        jnp.concatenate([keys_ref[...], values_ref[...]], 1),
         preferred_element_type=f32,
     )
 
@@ -98,12 +102,16 @@
         ).astype(f32)
         pieces = jnp.where(lane == 3, crowd[...], pieces)
         for h in range(heads_here):
-            sent = found[h * slots : (h + 1) * slots].reshape(4, 8, width)
-            last = jnp.where(sub == 7, pieces, sent[3])
+            sent = found[h * slots : (h + 1) * slots, :width].reshape(slot_tiles, 8, width)
+            last = jnp.where(sub == 7, pieces, sent[slot_tiles - 1])
             full = jnp.concatenate(
-                [queries_ref[...].astype(f32), sent[:3], last[None]], 0
+                [queries_ref[...].astype(f32), sent[: slot_tiles - 1], last[None]], 0
             ).astype(bf16)
             packet_ref[16 * h : 16 * h + 16] = jnp.broadcast_to(full[None], (16,) + full.shape)
+        plane = spread_index()[0]
+        for k, later_ref in enumerate(later_refs):
+            own = pl.ds(pl.multiple_of((plane ^ k) * slots, 8), slots)
+            later_ref[...] = found[own, width:].reshape(slot_tiles, 8, width).astype(bf16)
 
 
 def one_hot(wanted, size):
@@ -117,190 +125,158 @@
     )
 
 
-def pack(query_pos, kept_index, queries, keys):
+def pack(query_pos, kept_index, queries, keys, values):
     rows = chunk * heads_here
     return call(
         pack_kernel,
         "pack",
         (
-            shape((count_rows, 8, 8, width), bf16),
-            shape((heads_here * slots, width), f32),
-        ),
+            shape((count_rows, heads_here + slot_tiles, 8, width), bf16),
+        )
+        + (shape((slot_tiles, 8, width), bf16),) * 4,
         grid=(local_len // chunk,),
         in_specs=[
             whole_smem,
             pl.BlockSpec((heads_here, kept), lambda i: (0, 0)),
             pl.BlockSpec((heads_here, group, width), lambda i: (0, 0, 0)),
             pl.BlockSpec((rows, width), lambda i: (i, 0)),
+            pl.BlockSpec((rows, width), lambda i: (i, 0)),
         ],
         out_specs=[
-            pl.BlockSpec((count_rows, 8, 8, width), lambda i: (0, 0, 0, 0)),
-            pl.BlockSpec((heads_here * slots, width), lambda i: (0, 0)),
-        ],
+            pl.BlockSpec(
+                (count_rows, heads_here + slot_tiles, 8, width), lambda i: (0, 0, 0, 0)
+            ),
+        ]
+        + [pl.BlockSpec((slot_tiles, 8, width), lambda i: (0, 0, 0))] * 4,
         scratch_shapes=[
             pltpu.VMEM((heads_here * slots, width), f32),
+            pltpu.VMEM((heads_here * slots, 2 * width), f32),
             pltpu.VMEM((group, width), f32),
         ],
         cost_estimate=pl.CostEstimate(
-            flops=2 * 128 * 8192 * 128, bytes_accessed=3 * 2**20, transcendentals=0
-        ),
-    )(query_pos, kept_index, queries, keys)
-
-
-def regroup_kernel(slot_ref, keys_ref, values_ref, both_ref, found_ref, wide, found):
-    step = pl.program_id(0)
-    rows = chunk * heads_here
+            flops=2 * 128 * 8192 * 256, bytes_accessed=5 * 2**20, transcendentals=0
+        ),
+        compiler_params=params(60),
+    )(query_pos, kept_index, queries, keys, values)
+
+
+def attend_kernel(
+    queries_ref, keys_ref, values_ref, packet_ref, flag_ref, raw, wide, keys, values, side, sem
+):
+    move = pltpu.make_async_copy(values_ref, raw, sem)
+    move.start()
+    tile = 256
+    parts = count_rows * group // tile
     wide[0] = keys_ref[...].astype(f32)
-    wide[1] = values_ref[...].astype(f32)
-    for h in range(heads_here):
-        at = pl.ds(h, chunk, stride=heads_here)
-        both_ref[h] = jnp.concatenate([wide[0, at, :], wide[1, at, :]], 1).astype(bf16)
-
-    @pl.when(step == 0)
-    def _():
-        found[...] = jnp.zeros(found.shape, f32)
-
-    found[...] += jnp.dot(
-        one_hot(slot_ref[...] - (step * rows).astype(f32), rows),
-        values_ref[...],
-        preferred_element_type=f32,
-    )
-
-    @pl.when(step == local_len // chunk - 1)
-    def _():
-        found_ref[...] = found[...].reshape(found_ref.shape).astype(bf16)
-
-
-def regroup(slot, keys, values):
-    rows = chunk * heads_here
-    return call(
-        regroup_kernel,
-        "regroup",
-        (
-            shape((heads_here, local_len, 2 * width), bf16),
-            shape((heads_here, 4, 8, width), bf16),
-        ),
-        grid=(local_len // chunk,),
-        in_specs=[
-            pl.BlockSpec((heads_here * slots, width), lambda i: (0, 0)),
-            pl.BlockSpec((rows, width), lambda i: (i, 0)),
-            pl.BlockSpec((rows, width), lambda i: (i, 0)),
-        ],
-        out_specs=[
-            pl.BlockSpec((heads_here, chunk, 2 * width), lambda i: (0, i, 0)),
-            pl.BlockSpec((heads_here, 4, 8, width), lambda i: (0, 0, 0, 0)),
-        ],
-        scratch_shapes=[
-            pltpu.VMEM((2, rows, width), f32),
-            pltpu.VMEM((heads_here * slots, width), f32),
-        ],
-        cost_estimate=pl.CostEstimate(
-            flops=2 * 128 * 8192 * 128, bytes_accessed=8 * 2**20, transcendentals=0
-        ),
-    )(slot, keys, values)
-
-
-def attend_kernel(queries_ref, both_ref, packet_ref, keys, values, side):
-    h = pl.program_id(0)
     lane = lax.broadcasted_iota(jnp.int32, (local_len, width), 1)
-
-    @pl.when(h == 0)
-    def _():
-        pieces = queries_ref[:, 7].astype(f32)[:, 7]
-        row_id = lax.broadcasted_iota(jnp.int32, (count_rows, width), 0)
-        lane_id = lax.broadcasted_iota(jnp.int32, (count_rows, width), 1)
-        place = pieces[:, 0:1] + 256.0 * pieces[:, 1:2] + 65536.0 * pieces[:, 2:3]
-        place = jnp.sum(jnp.where(row_id == lane_id, place, 0.0), axis=0, keepdims=True)
-        spot = lax.broadcasted_iota(jnp.int32, (local_len, width), 0) + own_base()
-        late = (spot.astype(f32) > place) & (lane < count_rows)
-        keys[:, width:] = jnp.where(late, masked_score, 0.0).astype(bf16)
-        values[:, width:] = jnp.where(lane == 0, 1.0, 0.0).astype(bf16)
-        side[...] = jnp.zeros(side.shape, f32)
-
-    keys[:, :width] = both_ref[0, :, :width]
-    values[:, :width] = both_ref[0, :, width:]
-    q = queries_ref[:, h].astype(f32).reshape(count_rows * group, width)
-    tile = 256
     lane_t = lax.broadcasted_iota(jnp.int32, (tile, width), 1)
     row_t = lax.broadcasted_iota(jnp.int32, (tile, width), 0)
-
-    def scores(part):
-        own = jnp.where(row_t // group + part * (tile // group) == lane_t, 1.0, 0.0)
-        q_part = jnp.concatenate([q[part * tile : (part + 1) * tile], own], 1).astype(bf16)
+    pieces = queries_ref[:, heads_here + slot_tiles - 1].astype(f32)[:, 7]
+    flag_ref[0] = (jnp.max(pieces[:, 3:4]) > 0.0).astype(jnp.int32)
+    row_id = lax.broadcasted_iota(jnp.int32, (count_rows, width), 0)
+    lane_id = lax.broadcasted_iota(jnp.int32, (count_rows, width), 1)
+    place = pieces[:, 0:1] + 256.0 * pieces[:, 1:2] + 65536.0 * pieces[:, 2:3]
+    place = jnp.sum(jnp.where(row_id == lane_id, place, 0.0), axis=0, keepdims=True)
+    spot = lax.broadcasted_iota(jnp.int32, (local_len, width), 0) + own_base()
+    late = (spot.astype(f32) > place) & (lane < count_rows)
+    late = jnp.where(late, masked_score, 0.0).astype(bf16)
+    ones = jnp.where(lane == 0, 1.0, 0.0).astype(bf16)
+    for i in range(2):
+        keys[i, :, width:] = late
+        values[i, :, width:] = ones
+    side[...] = jnp.zeros(side.shape, f32)
+
+    def scores(h, part):
+        at = pl.ds(h, local_len, stride=heads_here)
+        if part == 0:
+            keys[h % 2, :, :width] = wide[0, at, :].astype(bf16)
+            if h == 0:
+                move.wait()
+                wide[1] = raw[...].astype(f32)
+            values[h % 2, :, :width] = wide[1, at, :].astype(bf16)
+        rows = tile // group
+        q = queries_ref[part * rows : (part + 1) * rows, h].astype(f32).reshape(tile, width)
+        own = jnp.where(row_t // group + part * rows == lane_t, 1.0, 0.0)
+        q = jnp.concatenate([q, own], 1).astype(bf16)
         return lax.dot_general(
-            q_part, keys[...], (((1,), (1,)), ((), ())), preferred_element_type=f32
-        )
-
-    parts = count_rows * group // tile
-    s = scores(0)
-    for part in range(parts):
-        after = scores(part + 1) if part + 1 < parts else None
+            q, keys[h % 2], (((1,), (1,)), ((), ())), preferred_element_type=f32
+        )
+
+    steps = [(h, part) for h in range(heads_here) for part in range(parts)]
+    s = scores(*steps[0])
+    for i, (h, part) in enumerate(steps):
+        after = scores(*steps[i + 1]) if i + 1 < len(steps) else None
         peak = jnp.max(s, axis=1, keepdims=True)
         w = jnp.exp2((s - peak) * scale_log2).astype(bf16)
-        o = jnp.dot(w, values[...], preferred_element_type=f32)
+        o = jnp.dot(w, values[h % 2], preferred_element_type=f32)
         sums = o[:, width : width + 1]
         mass = peak * scale_log2 + jnp.log2(sums)
         high = mass.astype(bf16).astype(f32)
         middle = (mass - high).astype(bf16).astype(f32)
         low = mass - high - middle
-        first = 3 * h
+        first = 3 * (row_t // 128 + part * 2)
         mark = jnp.where(
             lane_t == first,
             high,
             jnp.where(lane_t == first + 1, middle, jnp.where(lane_t == first + 2, low, 0.0)),
         )
-        rows = tile // group
-        own = slice(part * rows, (part + 1) * rows)
-        side[own] += mark.reshape(rows, group, width)
-        packet_ref[own, h] = (o[:, :width] / sums).reshape(rows, group, width).astype(bf16)
+        to = slice(16 * h, 16 * h + 16)
+        mark = mark.reshape(2, 16, group, width)
+        done = (o[:, :width] / sums).reshape(2, 16, group, width).astype(bf16)
+        for x in range(2):
+            packet_ref[to, 2 * part + x] = done[x]
+        side[to] += mark[0] + mark[1]
         s = after
-
-    @pl.when(h == heads_here - 1)
-    def _():
-        packet_ref[:, heads_here] = side[...].astype(bf16)
-
-
-def attend(packets, both):
+    packet_ref[:, 4] = side[...].astype(bf16)
+
+
+def attend(packets, keys, values):
     return call(
         attend_kernel,
         "attend",
-        shape((count_rows, heads_here + 1, group, width), bf16),
-        grid=(heads_here,),
-        in_specs=[
-            pl.BlockSpec((count_rows, 8, group, width), lambda h: (0, 0, 0, 0)),
-            pl.BlockSpec((1, local_len, 2 * width), lambda h: (h, 0, 0)),
-        ],
-        out_specs=pl.BlockSpec(
-            (count_rows, heads_here + 1, group, width), lambda h: (0, 0, 0, 0)
-        ),
+        (
+            shape((count_rows, heads_here + 1, group, width), bf16),
+            shape((1,), jnp.int32),
+        ),
+        in_specs=[whole_vmem] * 2 + [whole_hbm],
+        out_specs=[whole_vmem, whole_smem],
         scratch_shapes=[
-            pltpu.VMEM((local_len, 2 * width), bf16),
-            pltpu.VMEM((local_len, 2 * width), bf16),
+            pltpu.VMEM((local_len * heads_here, width), bf16),
+            pltpu.VMEM((2, local_len * heads_here, width), f32),
+            pltpu.VMEM((2, local_len, 2 * width), bf16),
+            pltpu.VMEM((2, local_len, 2 * width), bf16),
             pltpu.VMEM((count_rows, group, width), f32),
+            pltpu.SemaphoreType.DMA,
         ],
         cost_estimate=pl.CostEstimate(
             flops=2 * 2 * 512 * 2048 * 256 * 4,
             bytes_accessed=6 * 2**20,
             transcendentals=4 * 512 * 2048,
         ),
-    )(packets, both)
-
-
-def combine_kernel(parts_ref, values_ref, out_ref, spread_ref):
-    side = parts_ref[:, heads_here].astype(f32)
+        compiler_params=params(36),
+    )(packets, keys, values)
+
+
+def combine_kernel(parts_ref, v0_ref, v1_ref, v2_ref, v3_ref, full_ref, spread_ref):
+    side = parts_ref[:, 4].astype(f32)
     lane = lax.broadcasted_iota(jnp.int32, side.shape, 2)
-    for h in range(heads_here):
-        part = parts_ref[:, h].astype(f32)
-        own = (lane >= 3 * h) & (lane < 3 * h + 3)
+    for i in range(4):
+        part = parts_ref[:, i].astype(f32)
+        own = (lane >= 3 * i) & (lane < 3 * i + 3)
         mass = jnp.sum(jnp.where(own, side, 0.0), axis=2, keepdims=True)
         top = jnp.max(mass, axis=0, keepdims=True)
         share = jnp.exp2(mass - top)
         full = jnp.sum(share * part, axis=0) / jnp.sum(share, axis=0)
+        full_ref[i] = full
         high = full.astype(bf16)
-        out_ref[h] = high
         low = (full - high.astype(f32)).astype(bf16)
-        sent = jnp.concatenate([high[None], low[None], values_ref[h]], 0)
-        spread_ref[16 * h : 16 * h + 16] = jnp.broadcast_to(sent[None], (16,) + sent.shape)
+        spread_ref[:, i] = jnp.broadcast_to(high[None], (16, group, width))
+        spread_ref[:, 4 + i] = jnp.broadcast_to(low[None], (16, group, width))
+    for k, ref in enumerate((v0_ref, v1_ref, v2_ref, v3_ref)):
+        at = 8 + k * slot_tiles
+        spread_ref[:, at : at + slot_tiles] = jnp.broadcast_to(
+            ref[...][None], (16, slot_tiles, 8, width)
+        )
 
 
 def combine(parts, kept_values):
@@ -308,13 +284,16 @@
         combine_kernel,
         "combine",
         (
-            shape((heads_here, group, width), bf16),
-            shape((count_rows, 6, group, width), bf16),
-        ),
+            shape((4, group, width), f32),
+            shape((16, 8 + 4 * slot_tiles, group, width), bf16),
+        ),
+        in_specs=[whole_vmem] * 5,
+        out_specs=[whole_vmem] * 2,
         cost_estimate=pl.CostEstimate(
             flops=2 * 2**20, bytes_accessed=2 * 2**20, transcendentals=2048
         ),
-    )(parts, kept_values)
+        compiler_params=params(12),
+    )(parts, *kept_values)
 
 
 def reciprocal(x):
@@ -431,7 +410,10 @@
     lax.fori_loop(first, stop, step, 0)
 
 
-def gram_kernel(flag_ref, index_ref, packets_ref, dense_ref, slot_ref, mixing, a, d, left, r, keys):
+def gram_kernel(
+    flag_ref, index_ref, packets_ref, dense_ref,
+    slot_ref, mixing_ref, a, d, left, r, keys, dense, slot, mixing, sems,
+):
     head = spread_index()[0]
     index = index_ref[pl.ds(head, 1), :]
     holder = jnp.broadcast_to(index >> 11, (width, kept))
@@ -443,15 +425,24 @@
         across = holder[:1, g * width : (g + 1) * width]
         same += jnp.where((down == across) & (lane + g * width < row), 1.0, 0.0)
     rank = jnp.sum(same, axis=1, keepdims=True)
-    slot_ref[...] = (down * slots).astype(f32) + rank
+    own = (down & 15) * 4 + ((down >> 4) ^ head)
+    slot[...] = (own * slots).astype(f32) + rank
+    slot_out = pltpu.make_async_copy(slot, slot_ref, sems.at[0])
+    slot_out.start()
     sent = packets_ref[:, heads_here:].astype(f32).reshape(count_rows * slots, width).astype(bf16)
     keys[...] = jnp.dot(
-        one_hot(slot_ref[...], count_rows * slots), sent, preferred_element_type=f32
+        one_hot((down * slots).astype(f32) + rank, count_rows * slots),
+        sent,
+        preferred_element_type=f32,
     ).astype(bf16)
 
     @pl.when(flag_ref[0] > 0)
     def _():
-        keys[...] = dense_ref[:, :width]
+        slot_out.wait()
+        pltpu.sync_copy(dense_ref, dense)
+        keys[...] = dense[:, :width]
+        slot[...] = dense[:, width:].astype(f32)
+        slot_out.start()
 
     q = packets_ref[:, head].astype(f32).reshape(count_rows * group, width).astype(bf16)
     s = lax.dot_general(
@@ -459,6 +450,8 @@
     )
     e = jnp.exp((s - jnp.max(s, axis=0, keepdims=True)) * scale)
     mixing[...] = e / jnp.sum(e, axis=0, keepdims=True)
+    mixing_out = pltpu.make_async_copy(mixing, mixing_ref, sems.at[1])
+    mixing_out.start()
     row = lax.broadcasted_iota(jnp.int32, (kept, kept), 0)
     column = lax.broadcasted_iota(jnp.int32, (kept, kept), 1)
     a[...] = lax.dot_general(
@@ -472,8 +465,9 @@
     d[...] = a[:n, :n]
     left[...] = jnp.zeros(left.shape, f32)
     r[...] = jnp.zeros(r.shape, f32)
-    if early:
-        block_steps(a, d, left, r, 0, early)
+    block_steps(a, d, left, r, 0, early)
+    slot_out.wait()
+    mixing_out.wait()
 
 
 def gram(flag, kept_index, packets, dense):
@@ -489,12 +483,19 @@
             shape((kept, n), f32),
             shape((n, kept), f32),
         ),
-        in_specs=[whole_smem] + [whole_vmem] * 3,
-        out_specs=tuple([whole_vmem] * 6),
-        scratch_shapes=[pltpu.VMEM((kept, width), bf16)],
+        in_specs=[whole_smem] + [whole_vmem] * 2 + [whole_any],
+        out_specs=[whole_any] * 2 + [whole_vmem] * 4,
+        scratch_shapes=[
+            pltpu.VMEM((kept, width), bf16),
+            pltpu.VMEM((kept, 2 * width), bf16),
+            pltpu.VMEM((kept, width), f32),
+            pltpu.VMEM((kept, kept), f32),
+            pltpu.SemaphoreType.DMA((2,)),
+        ],
         cost_estimate=pl.CostEstimate(
             flops=10**10, bytes_accessed=6 * 2**20, transcendentals=2**18
         ),
+        compiler_params=params(24),
     )(flag, kept_index, packets, dense)
 
 
@@ -507,16 +508,20 @@
 
 
 def weigh_kernel(
-    flag_ref, slot_ref, mixing, a_ref, d_ref, left_ref, r_ref, dense_ref,
-    weight_ref, share_ref, plain_ref, a, d, left, r,
+    flag_ref, slot_ref, mixing_ref, a_ref, d_ref, left_ref, r_ref,
+    weight_ref, share_ref, plain_ref, a, d, left, r, slot, mixing, sems,
 ):
+    slot_in = pltpu.make_async_copy(slot_ref, slot, sems.at[0])
+    mixing_in = pltpu.make_async_copy(mixing_ref, mixing, sems.at[1])
+    slot_in.start()
+    mixing_in.start()
     a[...] = a_ref[...]
     d[...] = d_ref[...]
     left[...] = left_ref[...]
     r[...] = r_ref[...]
-    own = spread_index()[1]
+    plane, own = spread_index()
     block_steps(a, d, left, r, early, 4)
-    rows = [pl.ds(pl.multiple_of(128 * i + 8 * own, 8), 8) for i in range(4)]
+    rows = [pl.ds(pl.multiple_of(128 * (plane ^ k) + 8 * own, 8), 8) for k in range(4)]
     picked = jnp.concatenate([a[at, :] for at in rows], 0)
     picked -= jnp.dot(
         jnp.concatenate([left[at, :] for at in rows], 0),
@@ -524,13 +529,15 @@
         precision=highest,
         preferred_element_type=f32,
     )
+    slot_in.wait()
+    mixing_in.wait()
     weight_ref[...] = in_pieces(
         jnp.dot(picked, mixing[...], precision=highest, preferred_element_type=f32)
     )
 
     @pl.when(flag_ref[0] == 0)
     def _():
-        hot = one_hot(slot_ref[...], count_rows * slots)
+        hot = one_hot(slot[...], count_rows * slots)
         share_ref[...] = jnp.dot(
             in_pieces(ridge_weight * picked), hot, preferred_element_type=f32
         ).astype(bf16)
@@ -540,14 +547,11 @@
     def _():
         share_ref[...] = jnp.zeros(share_ref.shape, bf16)
         plain_ref[...] = jnp.dot(
-            ridge_weight * picked,
-            dense_ref[:, width:].astype(f32),
-            precision=highest,
-            preferred_element_type=f32,
-        )
-
-
-def weigh(flag, slot, mixing, a, d, left, r, dense):
+            ridge_weight * picked, slot[...], precision=highest, preferred_element_type=f32
+        )
+
+
+def weigh(flag, slot, mixing, a, d, left, r):
     n = 128
     return call(
         weigh_kernel,
@@ -557,41 +561,76 @@
             shape((96, count_rows * slots), bf16),
             shape((32, width), f32),
         ),
-        in_specs=[whole_smem] + [whole_vmem] * 7,
+        in_specs=[whole_smem] + [whole_any] * 2 + [whole_vmem] * 4,
+        out_specs=[whole_vmem] * 3,
         scratch_shapes=[
             pltpu.VMEM((kept, kept), f32),
             pltpu.VMEM((n, n), f32),
             pltpu.VMEM((kept, n), f32),
             pltpu.VMEM((n, kept), f32),
+            pltpu.VMEM((kept, width), f32),
+            pltpu.VMEM((kept, kept), f32),
+            pltpu.SemaphoreType.DMA((2,)),
         ],
         cost_estimate=pl.CostEstimate(
             flops=2 * 10**10, bytes_accessed=6 * 2**20, transcendentals=0
         ),
-    )(flag, slot, mixing, a, d, left, r, dense)
-
-
-def finish_kernel(weight_ref, share_ref, plain_ref, sent_ref, out_ref):
+        compiler_params=params(20),
+    )(flag, slot, mixing, a, d, left, r)
+
+
+def finish_kernel(weight_ref, share_ref, plain_ref, full_ref, sent_ref, *out_refs):
     sent = sent_ref[...].astype(f32)
-    targets = jnp.concatenate(
-        [sent[:, i].reshape(count_rows * group, width) for i in range(2)], 1
-    ).astype(bf16)
-    values = sent[:, 2:].reshape(count_rows * slots, width).astype(bf16)
-    fitted = jnp.dot(weight_ref[...], targets, preferred_element_type=f32)
+    targets = [
+        jnp.concatenate(
+            [sent[:, 4 * i + x].reshape(16 * group, width) for x in range(4)], 0
+        )
+        for i in range(2)
+    ]
+    values = sent[:, 8:].reshape(count_rows * slots, width).astype(bf16)
+    fitted = jnp.dot(
+        weight_ref[...], jnp.concatenate(targets, 1).astype(bf16), preferred_element_type=f32
+    )
     shared = jnp.dot(share_ref[...], values, preferred_element_type=f32)
     total = fitted[:, :width] + fitted[:, width:] + shared
     total = total[:32] + total[32:64] + total[64:] + plain_ref[...]
-    out_ref[...] = total.reshape(4, 8, width)
-
-
-def finish(weight, share, plain, sent):
+    plane = spread_index()[0]
+    for k, out_ref in enumerate(out_refs):
+        out_ref[:8] = total[8 * k : 8 * k + 8]
+        out_ref[8:] = full_ref[plane ^ k]
+
+
+def finish(weight, share, plain, full, sent):
     return call(
         finish_kernel,
         "finish",
-        shape((4, 8, width), f32),
+        [shape((16, width), f32)] * 4,
+        in_specs=[whole_vmem] * 5,
+        out_specs=[whole_vmem] * 4,
         cost_estimate=pl.CostEstimate(
             flops=2 * 96 * 2560 * 256, bytes_accessed=2**20, transcendentals=0
         ),
-    )(weight, share, plain, sent)
+        compiler_params=params(10),
+    )(weight, share, plain, full, sent)
+
+
+def arrange_kernel(b0_ref, b1_ref, b2_ref, b3_ref, out_ref, fitted_ref):
+    plane = spread_index()[0]
+    for k, ref in enumerate((b0_ref, b1_ref, b2_ref, b3_ref)):
+        fitted_ref[plane ^ k] = ref[:8]
+        out_ref[plane ^ k] = ref[8:].astype(bf16)
+
+
+def arrange(blocks):
+    return call(
+        arrange_kernel,
+        "arrange",
+        (shape((heads_here, group, width), bf16), shape((heads_here, 8, width), f32)),
+        in_specs=[whole_vmem] * 4,
+        out_specs=[whole_vmem] * 2,
+        cost_estimate=pl.CostEstimate(flops=2**13, bytes_accessed=2**16, transcendentals=0),
+        compiler_params=params(4),
+    )(*blocks)
 
 
 def dense_rows(kept_index, cache_keys, cache_values):
@@ -607,31 +646,34 @@
     return lax.all_to_all(found, ("y", "z"), 0, 0).reshape(kept, 2 * width)
 
 
+def along_x(blocks):
+    return [blocks[0]] + [
+        lax.ppermute(blocks[k], "x", [(i, i ^ k) for i in range(4)]) for k in range(1, 4)
+    ]
+
+
 def on_device(ref_queries, query_pos, cache_keys, cache_values, kept_index):
     keys = cache_keys.reshape(local_len * heads_here, width)
     values = cache_values.reshape(local_len * heads_here, width)
-    packets, slot = pack(
-        query_pos, kept_index, ref_queries.reshape(heads_here, group, width), keys
+    packets, *kept_values = pack(
+        query_pos, kept_index, ref_queries.reshape(heads_here, group, width), keys, values
     )
     packets = lax.all_to_all(packets, seq_axes, 0, 0)
-    both, kept_values = regroup(slot, keys, values)
-    crowded = jnp.max(packets[:, 7, 7, 3].astype(f32)) > 0.0
+    kept_values = along_x(kept_values)
+    parts, flag = attend(packets, keys, values)
+    parts = lax.all_to_all(parts, seq_axes, 0, 0)
     dense = lax.cond(
-        crowded,
+        flag[0] > 0,
         dense_rows,
         lambda *_: jnp.zeros((kept, 2 * width), bf16),
         kept_index,
         cache_keys,
         cache_values,
     )
-    flag = crowded.astype(jnp.int32)[None]
-
-    parts = lax.all_to_all(attend(packets, both), seq_axes, 0, 0)
     state = gram(flag, kept_index, packets, dense)
-    out, sent = combine(parts, kept_values)
-    sent = lax.all_to_all(sent, seq_axes, 0, 0)
-    fitted = finish(*weigh(flag, *state, dense), sent)
-    fitted = lax.all_to_all(fitted, "x", 0, 0)
+    full, sent = combine(parts, kept_values)
+    sent = lax.all_to_all(sent, ("y", "z"), 0, 0)
+    out, fitted = arrange(along_x(finish(*weigh(flag, *state), full, sent)))
     return (out.reshape(1, heads_here * group, width), fitted)
 
 

time: 110 us -> 98.5 us (0.90)
  Pallas kernels: 54.6 us -> 42.7 us
  blocking collectives: 9.73 us -> 0 us
  starting transfers between devices: 26 us -> 31.9 us
  waiting for transfers between devices: 13.6 us -> 18.2 us
    all_to_all x1 -> x0, blocking collectives: 9.73 us -> none  [on_device(): fitted = lax.all_to_all(fitted, 'x', 0, 0)]
    ppermute x0 -> x6, starting transfers between devices: none -> 9.56 us  [along_x(): lax.ppermute(blocks[k], 'x', [(i, i ^ k) for i in range(4)])]
    pallas_call x5, Pallas kernels: 24.9 us -> 16.8 us  [the longest x1 9.51 us: attend(): call(attend_kernel, 'attend', (shape((count_rows, heads_here + 1, group,...]
    ppermute x0 -> x6, waiting for transfers between devices: none -> 4.58 us  [along_x(): lax.ppermute(blocks[k], 'x', [(i, i ^ k) for i in range(4)])]
    all_to_all x2, starting transfers between devices: 14.6 us -> 10.9 us  [the longest x1 5.89 us: on_device(): parts = lax.all_to_all(parts, seq_axes, 0, 0)]
    pallas_call x1, Pallas kernels: 18.7 us -> 16.8 us  [weigh(): call(weigh_kernel, 'weigh', (shape((96, kept), bf16), shape((96, count_ro...]
    pallas_call x1, Pallas kernels: 11 us -> 9.06 us  [gram(): call(gram_kernel, 'gram', (shape((kept, width), f32), shape((kept, kept),...]
    unnamed x11 -> x12, local copies, waits for them, and re-layouts: 2.35 us -> 2.92 us
  transfers between devices with their start and end apart: 3 -> 9, of which waited for: 2 -> 4; matrix products, arithmetic and copies ran while one was open for 0% -> 0% of each run, Pallas kernels for 32% -> 36%
where the time goes in v3:
time: 98.5 us; the launch traced here: 97.9 us
  Pallas kernels  42.7 us (43%)
  starting transfers between devices  31.9 us (32%)
  waiting for transfers between devices  18.2 us (18%)
  local copies, waits for them, and re-layouts  2.95 us (3%)
  between operations  1.95 us (2%)
    pallas_call x1, Pallas kernels, weigh(): call(weigh_kernel, 'weigh', (shape((96, kept), bf16), shape((96, count_ro...  16.8 us
    all_to_all x1, starting transfers between devices, on_device(): packets = lax.all_to_all(packets, seq_axes, 0, 0)  11.4 us
    all_to_all x1, waiting for transfers between devices, on_device(): packets = lax.all_to_all(packets, seq_axes, 0, 0)  11.4 us
    ppermute x6, starting transfers between devices, along_x(): lax.ppermute(blocks[k], 'x', [(i, i ^ k) for i in range(4)])  9.56 us
    pallas_call x1, Pallas kernels, attend(): call(attend_kernel, 'attend', (shape((count_rows, heads_here + 1, group,...  9.51 us
    pallas_call x1, Pallas kernels, gram(): call(gram_kernel, 'gram', (shape((kept, width), f32), shape((kept, kept),...  9.06 us
    all_to_all x1, starting transfers between devices, on_device(): parts = lax.all_to_all(parts, seq_axes, 0, 0)  5.89 us
    all_to_all x1, starting transfers between devices, on_device(): sent = lax.all_to_all(sent, ('y', 'z'), 0, 0)  5.02 us
  transfers between devices with their start and end apart: 9, of which 4 were waited for; matrix products, arithmetic and copies ran while one was open for 0% of the time, Pallas kernels for 36%

profile of v3, /device:TPU:8, one launch (start us, length us, event | category | flops | bytes accessed | tf_op | source)
XLA Modules:
  0.0 97.9 jit_solution(10200328087815343463)
XLA Ops:
  1.3 0.0 copy-start.3
  1.3 5.0 %pack.1 = (bf16[64,7,8,128]{3,2,1,0:T(8,128)(2,1)}, bf16[3,8,128]{2,1,0:T(8,128)(2,1)}, bf16[3,8,128]{2,1,0:T(8,128)(2,1)}, bf16[3,8,128]{2,1,0:T(8,128)(2,1)}, bf16[3,8,128]{2,1,0:T(8,128)(2,1)}) custom-call(s32[1]{0:T(128)S(6)} %copy.10.pos_ref, s32[4,512]{1,0:T(4,128)} %index_ref.3, bf16[4,8,128]{2,1,0:T(8,128)(2,1)} %bitcast.27, ...), custom_call_target="tpu_custom_call" | custom-call | flops 536870912 | bytes 5242880 | tf_op jit(solution)/shard_map/pack/pallas_call | solution.py:130
  6.2 11.4 %all-to-all-start.2 = ((bf16[64,7,8,128]{3,2,1,0:T(8,128)(2,1)}), bf16[64,7,8,128]{3,2,1,0:T(8,128)(2,1)S(1)}, u32[]{:S(2)}, u32[]{:S(2)}) async-start(bf16[64,7,8,128]{3,2,1,0:T(8,128)(2,1)} %get-tuple-element.38), calls=%async_computation.2 | async-start | bytes 1835008 | tf_op jit(solution)/shard_map/all_to_all | solution.py:661
  17.7 1.6 %collective-permute-start = (bf16[3,8,128]{2,1,0:T(8,128)(2,1)}, bf16[3,8,128]{2,1,0:T(8,128)(2,1)S(1)}, u32[]{:S(2)}, u32[]{:S(2)}) collective-permute-start(bf16[3,8,128]{2,1,0:T(8,128)(2,1)} %get-tuple-element.51), channel_id=1, source_target_pairs={{0,32},{32,0},{64,96},{96,64},{1,33},{33,1},{65,97},{97,65},{2,34}... | collective-permute-start | bytes 18440 | tf_op jit(solution)/shard_map/ppermute | solution.py:651
  19.2 2.9 %collective-permute-start.1 = (bf16[3,8,128]{2,1,0:T(8,128)(2,1)}, bf16[3,8,128]{2,1,0:T(8,128)(2,1)S(1)}, u32[]{:S(2)}, u32[]{:S(2)}) collective-permute-start(bf16[3,8,128]{2,1,0:T(8,128)(2,1)} %get-tuple-element.52), channel_id=1, source_target_pairs={{0,64},{32,96},{64,0},{96,32},{1,65},{33,97},{65,1},{97,33},{2,66}... | collective-permute-start | bytes 18440 | tf_op jit(solution)/shard_map/ppermute | solution.py:651
  22.1 0.3 collective-permute-start.2
  22.5 11.4 %all-to-all-done.2.queries_ref.packets_ref = bf16[64,7,8,128]{3,2,1,0:T(8,128)(2,1)S(1)} async-done(((bf16[64,7,8,128]{3,2,1,0:T(8,128)(2,1)}), bf16[64,7,8,128]{3,2,1,0:T(8,128)(2,1)S(1)}, u32[]{:S(2)}, u32[]{:S(2)}) %all-to-all-start.2) | async-done | bytes 917536 | tf_op jit(solution)/shard_map/all_to_all | solution.py:661
  33.9 0.0 copy-done.3
  33.9 9.5 %attend.1 = (bf16[64,5,8,128]{3,2,1,0:T(8,128)(2,1)}, s32[1]{0:T(128)}) custom-call(bf16[64,7,8,128]{3,2,1,0:T(8,128)(2,1)S(1)} %all-to-all-done.2.queries_ref.packets_ref, bf16[8192,128]{1,0:T(8,128)(2,1)S(1)} %bitcast.21, bf16[8192,128]{1,0:T(8,128)(2,1)} %bitcast.23), custom_call_target="tpu_custom_call" | custom-call | flops 4294967296 | bytes 6291456 | tf_op jit(solution)/shard_map/attend/pallas_call | solution.py:234
  43.9 0.3 conditional.1
  44.2 0.7 copy-done.4
  44.9 5.9 %all-to-all-start.3 = ((bf16[64,5,8,128]{3,2,1,0:T(8,128)(2,1)}), bf16[64,5,8,128]{3,2,1,0:T(8,128)(2,1)S(1)}, u32[]{:S(2)}, u32[]{:S(2)}) async-start(bf16[64,5,8,128]{3,2,1,0:T(8,128)(2,1)} %get-tuple-element.49), calls=%async_computation.3 | async-start | bytes 1310720 | tf_op jit(solution)/shard_map/all_to_all | solution.py:664
  50.8 0.0 copy-start
  50.8 9.1 %gram.1 = (f32[512,128]{1,0:T(8,128)S(1)}, f32[512,512]{1,0:T(8,128)S(1)}, f32[512,512]{1,0:T(8,128)S(1)}, f32[128,128]{1,0:T(8,128)S(1)}, f32[512,128]{1,0:T(8,128)S(1)}, /*index=5*/f32[128,512]{1,0:T(8,128)S(1)}) custom-call(s32[1]{0:T(128)} %get-tuple-element.39.flag_ref, s32[4,512]{1,0:T(4,128)S(1)} %copy-done.5, ...), custom_call_target="tpu_custom_call" | custom-call | flops 10000000000 | bytes 6291456 | tf_op jit(solution)/shard_map/gram/pallas_call | solution.py:475
  59.9 1.0 %copy-done.1 = f32[512,512]{1,0:T(8,128)} copy-done((f32[512,512]{1,0:T(8,128)}, f32[512,512]{1,0:T(8,128)S(1)}, u32[]{:S(2)}) %copy-start.1) | copy-done | bytes 1048600
  60.9 0.0 collective-permute-done.v1_ref
  60.9 0.0 collective-permute-done.1.v2_ref
  60.9 0.0 collective-permute-done.2.v3_ref
  60.9 2.2 %all-to-all-done.3.parts_ref = bf16[64,5,8,128]{3,2,1,0:T(8,128)(2,1)S(1)} async-done(((bf16[64,5,8,128]{3,2,1,0:T(8,128)(2,1)}), bf16[64,5,8,128]{3,2,1,0:T(8,128)(2,1)S(1)}, u32[]{:S(2)}, u32[]{:S(2)}) %all-to-all-start.3) | async-done | bytes 655392 | tf_op jit(solution)/shard_map/all_to_all | solution.py:664
  63.1 1.5 %combine.1 = (f32[4,8,128]{2,1,0:T(8,128)S(1)}, bf16[16,20,8,128]{3,2,1,0:T(8,128)(2,1)}) custom-call(bf16[64,5,8,128]{3,2,1,0:T(8,128)(2,1)S(1)} %all-to-all-done.3.parts_ref, bf16[3,8,128]{2,1,0:T(8,128)(2,1)S(1)} %copy-done, bf16[3,8,128]{2,1,0:T(8,128)(2,1)S(1)} %collective-permute-done.v1_ref, bf16[3,8,128]{2,1,0:T(8,128)(2,1)S(1)} %collective-permute-done.1.v2_ref, ...), custom_call_target="tpu_custom_call" | custom-call | flops 2097152 | bytes 2097152 | tf_op jit(solution)/shard_map/combine/pallas_call | solution.py:283
  64.6 5.0 %all-to-all-start.4 = ((bf16[16,20,8,128]{3,2,1,0:T(8,128)(2,1)}), bf16[16,20,8,128]{3,2,1,0:T(8,128)(2,1)S(1)}, u32[]{:S(2)}, u32[]{:S(2)}) async-start(bf16[16,20,8,128]{3,2,1,0:T(8,128)(2,1)} %get-tuple-element.55), calls=%async_computation.4 | async-start | bytes 1310720 | tf_op jit(solution)/shard_map/all_to_all | solution.py:675
  69.6 1.2 %copy-done.2 = f32[512,512]{1,0:T(8,128)S(1)} copy-done((f32[512,512]{1,0:T(8,128)S(1)}, f32[512,512]{1,0:T(8,128)}, u32[]{:S(2)}) %copy-start.2) | copy-done | bytes 1048600
  70.9 16.8 %weigh.1 = (bf16[96,512]{1,0:T(8,128)(2,1)S(1)}, bf16[96,1536]{1,0:T(8,128)(2,1)S(1)}, f32[32,128]{1,0:T(8,128)S(1)}) custom-call(s32[1]{0:T(128)} %get-tuple-element.39.flag_ref, f32[512,128]{1,0:T(8,128)S(1)} %get-tuple-element.40.slot_ref, f32[512,512]{1,0:T(8,128)S(1)} %get-tuple-element.41.mixing_ref, f32[512,512]{1,0:T(8,128)S(1)} %copy-done.2, ...), custom_call_target="tpu_custom_call" | custom-call | flops 20000000000 | bytes 6291456 | tf_op jit(solution)/shard_map/weigh/pallas_call | solution.py:556
  87.7 0.0 all-to-all-done.4.sent_ref
  87.7 0.3 finish.1
  88.0 1.6 %collective-permute-start.3 = (f32[16,128]{1,0:T(8,128)S(1)}, f32[16,128]{1,0:T(8,128)S(1)}, u32[]{:S(2)}, u32[]{:S(2)}) collective-permute-start(f32[16,128]{1,0:T(8,128)S(1)} %get-tuple-element.57), channel_id=1, source_target_pairs={{0,32},{32,0},{64,96},{96,64},{1,33},{33,1},{65,97},{97,65},{2,34}... | collective-permute-start | bytes 24584 | tf_op jit(solution)/shard_map/ppermute | solution.py:651
  89.6 2.9 %collective-permute-start.4 = (f32[16,128]{1,0:T(8,128)S(1)}, f32[16,128]{1,0:T(8,128)S(1)}, u32[]{:S(2)}, u32[]{:S(2)}) collective-permute-start(f32[16,128]{1,0:T(8,128)S(1)} %get-tuple-element.58), channel_id=1, source_target_pairs={{0,64},{32,96},{64,0},{96,32},{1,65},{33,97},{65,1},{97,33},{2,66}... | collective-permute-start | bytes 24584 | tf_op jit(solution)/shard_map/ppermute | solution.py:651
  92.5 0.3 collective-permute-start.5
  92.7 0.0 collective-permute-done.3.b1_ref
  92.7 2.0 %collective-permute-done.4.b2_ref = f32[16,128]{1,0:T(8,128)S(1)} collective-permute-done((f32[16,128]{1,0:T(8,128)S(1)}, f32[16,128]{1,0:T(8,128)S(1)}, u32[]{:S(2)}, u32[]{:S(2)}) %collective-permute-start.4) | collective-permute-done | bytes 8224 | tf_op jit(solution)/shard_map/ppermute | solution.py:651
  94.7 2.6 %collective-permute-done.5.b3_ref = f32[16,128]{1,0:T(8,128)S(1)} collective-permute-done((f32[16,128]{1,0:T(8,128)S(1)}, f32[16,128]{1,0:T(8,128)S(1)}, u32[]{:S(2)}, u32[]{:S(2)}) %collective-permute-start.5) | collective-permute-done | bytes 8224 | tf_op jit(solution)/shard_map/ppermute | solution.py:651
  97.3 0.6 arrange.1
  (7 shorter events, 0.0 us)
Async XLA Ops:
  1.3 32.6 %copy-start.3 = (bf16[2048,4,128]{2,1,0:T(4,128)(2,1)S(1)}, bf16[2048,4,128]{2,1,0:T(4,128)(2,1)}, u32[]{:S(2)}) copy-start(bf16[2048,4,128]{2,1,0:T(4,128)(2,1)} %param.9) | copy-start | bytes 6291460
  6.2 27.6 %all-to-all-start.2 = ((bf16[64,7,8,128]{3,2,1,0:T(8,128)(2,1)}), bf16[64,7,8,128]{3,2,1,0:T(8,128)(2,1)S(1)}, u32[]{:S(2)}, u32[]{:S(2)}) async-start(bf16[64,7,8,128]{3,2,1,0:T(8,128)(2,1)} %get-tuple-element.38), calls=%async_computation.2 | async-start | bytes 1835008 | tf_op jit(solution)/shard_map/all_to_all | solution.py:661
  17.7 43.2 %collective-permute-start = (bf16[3,8,128]{2,1,0:T(8,128)(2,1)}, bf16[3,8,128]{2,1,0:T(8,128)(2,1)S(1)}, u32[]{:S(2)}, u32[]{:S(2)}) collective-permute-start(bf16[3,8,128]{2,1,0:T(8,128)(2,1)} %get-tuple-element.51), channel_id=1, source_target_pairs={{0,32},{32,0},{64,96},{96,64},{1,33},{33,1},{65,97},{97,65},{2,34}... | collective-permute-start | bytes 18440 | tf_op jit(solution)/shard_map/ppermute | solution.py:651
  19.2 41.7 %collective-permute-start.1 = (bf16[3,8,128]{2,1,0:T(8,128)(2,1)}, bf16[3,8,128]{2,1,0:T(8,128)(2,1)S(1)}, u32[]{:S(2)}, u32[]{:S(2)}) collective-permute-start(bf16[3,8,128]{2,1,0:T(8,128)(2,1)} %get-tuple-element.52), channel_id=1, source_target_pairs={{0,64},{32,96},{64,0},{96,32},{1,65},{33,97},{65,1},{97,33},{2,66}... | collective-permute-start | bytes 18440 | tf_op jit(solution)/shard_map/ppermute | solution.py:651
  22.1 38.8 %collective-permute-start.2 = (bf16[3,8,128]{2,1,0:T(8,128)(2,1)}, bf16[3,8,128]{2,1,0:T(8,128)(2,1)S(1)}, u32[]{:S(2)}, u32[]{:S(2)}) collective-permute-start(bf16[3,8,128]{2,1,0:T(8,128)(2,1)} %get-tuple-element.53), channel_id=1, source_target_pairs={{0,96},{32,64},{64,32},{96,0},{1,97},{33,65},{65,33},{97,1},{2,98}... | collective-permute-start | bytes 18440 | tf_op jit(solution)/shard_map/ppermute | solution.py:651
  22.5 21.5 %copy-start.5 = (s32[4,512]{1,0:T(4,128)S(1)}, s32[4,512]{1,0:T(4,128)}, u32[]{:S(2)}) copy-start(s32[4,512]{1,0:T(4,128)} %index_ref.3) | copy-start | bytes 24580
  44.2 0.7 copy-start.4
  44.9 18.2 %all-to-all-start.3 = ((bf16[64,5,8,128]{3,2,1,0:T(8,128)(2,1)}), bf16[64,5,8,128]{3,2,1,0:T(8,128)(2,1)S(1)}, u32[]{:S(2)}, u32[]{:S(2)}) async-start(bf16[64,5,8,128]{3,2,1,0:T(8,128)(2,1)} %get-tuple-element.49), calls=%async_computation.3 | async-start | bytes 1310720 | tf_op jit(solution)/shard_map/all_to_all | solution.py:664
  50.8 12.3 %copy-start = (bf16[3,8,128]{2,1,0:T(8,128)(2,1)S(1)}, bf16[3,8,128]{2,1,0:T(8,128)(2,1)}, u32[]{:S(2)}) copy-start(bf16[3,8,128]{2,1,0:T(8,128)(2,1)} %get-tuple-element.50.v0_ref) | copy-start | bytes 18436
  59.9 1.0 %copy-start.1 = (f32[512,512]{1,0:T(8,128)}, f32[512,512]{1,0:T(8,128)S(1)}, u32[]{:S(2)}) copy-start(f32[512,512]{1,0:T(8,128)S(1)} %get-tuple-element.42.a_ref) | copy-start | bytes 3145732
  64.6 23.1 %all-to-all-start.4 = ((bf16[16,20,8,128]{3,2,1,0:T(8,128)(2,1)}), bf16[16,20,8,128]{3,2,1,0:T(8,128)(2,1)S(1)}, u32[]{:S(2)}, u32[]{:S(2)}) async-start(bf16[16,20,8,128]{3,2,1,0:T(8,128)(2,1)} %get-tuple-element.55), calls=%async_computation.4 | async-start | bytes 1310720 | tf_op jit(solution)/shard_map/all_to_all | solution.py:675
  69.6 1.2 %copy-start.2 = (f32[512,512]{1,0:T(8,128)S(1)}, f32[512,512]{1,0:T(8,128)}, u32[]{:S(2)}) copy-start(f32[512,512]{1,0:T(8,128)} %copy-done.1) | copy-start | bytes 3145732
  88.0 4.8 %collective-permute-start.3 = (f32[16,128]{1,0:T(8,128)S(1)}, f32[16,128]{1,0:T(8,128)S(1)}, u32[]{:S(2)}, u32[]{:S(2)}) collective-permute-start(f32[16,128]{1,0:T(8,128)S(1)} %get-tuple-element.57), channel_id=1, source_target_pairs={{0,32},{32,0},{64,96},{96,64},{1,33},{33,1},{65,97},{97,65},{2,34}... | collective-permute-start | bytes 24584 | tf_op jit(solution)/shard_map/ppermute | solution.py:651
  89.6 5.2 %collective-permute-start.4 = (f32[16,128]{1,0:T(8,128)S(1)}, f32[16,128]{1,0:T(8,128)S(1)}, u32[]{:S(2)}, u32[]{:S(2)}) collective-permute-start(f32[16,128]{1,0:T(8,128)S(1)} %get-tuple-element.58), channel_id=1, source_target_pairs={{0,64},{32,96},{64,0},{96,32},{1,65},{33,97},{65,1},{97,33},{2,66}... | collective-permute-start | bytes 24584 | tf_op jit(solution)/shard_map/ppermute | solution.py:651
  92.5 4.9 %collective-permute-start.5 = (f32[16,128]{1,0:T(8,128)S(1)}, f32[16,128]{1,0:T(8,128)S(1)}, u32[]{:S(2)}, u32[]{:S(2)}) collective-permute-start(f32[16,128]{1,0:T(8,128)S(1)} %get-tuple-element.59), channel_id=1, source_target_pairs={{0,96},{32,64},{64,32},{96,0},{1,97},{33,65},{65,33},{97,1},{2,98}... | collective-permute-start | bytes 24584 | tf_op jit(solution)/shard_map/ppermute | solution.py:651

commit v4 on v3

--- a/solution.py
+++ b/solution.py
@@ -21,11 +21,10 @@
 width = 128
 local_len = 2048
 kept = 512
-chunk = 512
+chunk = 1024
 slots = 24
 slot_tiles = slots // 8
 panel = 64
-early = 1
 scale = width ** (-0.5)
 scale_log2 = scale * math.log2(math.e)
 
@@ -313,7 +312,7 @@
     return left, turned, (s * r, -q * r, p * r), r
 
 
-def invert_block(a, n, h):
+def invert_block(a, n, h, start, stop):
     b = 4
     lane = lax.broadcasted_iota(jnp.int32, (8, n), 1)
     sub = lax.broadcasted_iota(jnp.int32, (8, n), 0)
@@ -322,7 +321,7 @@
     def over(v, r):
         return jnp.broadcast_to(v[r % 8 : r % 8 + 1, :], (8, n))
 
-    for first in range(0, n, h):
+    for first in range(start, stop, h):
         tiles = [a[first + 8 * i : first + 8 * i + 8, :] for i in range(h // 8)]
         d = None
         for k in range(first, first + h, b):
@@ -385,34 +384,38 @@
     return a
 
 
-def block_steps(a, d, left, r, first, stop):
+def block_step(k, p, a, d, left, r):
     n = 128
     row = lax.broadcasted_iota(jnp.int32, (n, n), 0)
     column = lax.broadcasted_iota(jnp.int32, (n, n), 1)
     eye = jnp.where(row == column, 1.0, 0.0)
-
-    def step(k, _):
-        at = pl.ds(pl.multiple_of(k * n, n), n)
-        then = pl.ds(pl.multiple_of(jnp.minimum(k + 1, kept // n - 1) * n, n), n)
-        a[...] -= jnp.dot(left[...], r[...], precision=highest, preferred_element_type=f32)
-        p = invert_block(d[...], n, panel)
-        a[at, at] = -eye
-        left[...] = a[:, at]
-        a[:, at] = jnp.zeros((kept, n), f32)
-        a[at, at] = eye
-        r[...] = jnp.dot(p, a[at, :], precision=highest, preferred_element_type=f32)
-        a[at, :] = jnp.zeros((n, kept), f32)
-        d[...] = a[then, then] - jnp.dot(
-            left[then, :], r[:, then], precision=highest, preferred_element_type=f32
-        )
-        return 0
-
-    lax.fori_loop(first, stop, step, 0)
+    at = pl.ds(pl.multiple_of(k * n, n), n)
+    then = pl.ds(pl.multiple_of(jnp.minimum(k + 1, kept // n - 1) * n, n), n)
+    a[at, at] = -eye
+    left[...] = a[:, at]
+    a[:, at] = jnp.zeros((kept, n), f32)
+    a[at, at] = eye
+    r[...] = jnp.dot(p, a[at, :], precision=highest, preferred_element_type=f32)
+    a[at, :] = jnp.zeros((n, kept), f32)
+    d[...] = a[then, then] - jnp.dot(
+        left[then, :], r[:, then], precision=highest, preferred_element_type=f32
+    )
+
+
+def update(a, left, r):
+    a[...] -= jnp.dot(left[...], r[...], precision=highest, preferred_element_type=f32)
+
+
+def mix(keys, q):
+    s = lax.dot_general(
+        keys[...], q[...], (((1,), (1,)), ((), ())), preferred_element_type=f32
+    )
+    e = jnp.exp((s - jnp.max(s, axis=0, keepdims=True)) * scale)
+    return e / jnp.sum(e, axis=0, keepdims=True)
 
 
 def gram_kernel(
-    flag_ref, index_ref, packets_ref, dense_ref,
-    slot_ref, mixing_ref, a, d, left, r, keys, dense, slot, mixing, sems,
+    flag_ref, index_ref, packets_ref, dense_ref, slot, keys, q_ref, a, d, left, r, dense, mixing
 ):
     head = spread_index()[0]
     index = index_ref[pl.ds(head, 1), :]
@@ -427,8 +430,6 @@
     rank = jnp.sum(same, axis=1, keepdims=True)
     own = (down & 15) * 4 + ((down >> 4) ^ head)
     slot[...] = (own * slots).astype(f32) + rank
-    slot_out = pltpu.make_async_copy(slot, slot_ref, sems.at[0])
-    slot_out.start()
     sent = packets_ref[:, heads_here:].astype(f32).reshape(count_rows * slots, width).astype(bf16)
     keys[...] = jnp.dot(
         one_hot((down * slots).astype(f32) + rank, count_rows * slots),
@@ -438,20 +439,12 @@
 
     @pl.when(flag_ref[0] > 0)
     def _():
-        slot_out.wait()
         pltpu.sync_copy(dense_ref, dense)
         keys[...] = dense[:, :width]
         slot[...] = dense[:, width:].astype(f32)
-        slot_out.start()
-
-    q = packets_ref[:, head].astype(f32).reshape(count_rows * group, width).astype(bf16)
-    s = lax.dot_general(
-        keys[...], q, (((1,), (1,)), ((), ())), preferred_element_type=f32
-    )
-    e = jnp.exp((s - jnp.max(s, axis=0, keepdims=True)) * scale)
-    mixing[...] = e / jnp.sum(e, axis=0, keepdims=True)
-    mixing_out = pltpu.make_async_copy(mixing, mixing_ref, sems.at[1])
-    mixing_out.start()
+
+    q_ref[...] = packets_ref[:, head].astype(f32).reshape(kept, width).astype(bf16)
+    mixing[...] = mix(keys, q_ref)
     row = lax.broadcasted_iota(jnp.int32, (kept, kept), 0)
     column = lax.broadcasted_iota(jnp.int32, (kept, kept), 1)
     a[...] = lax.dot_general(
@@ -462,12 +455,9 @@
         preferred_element_type=f32,
     ) + jnp.where(row == column, ridge_weight, 0.0)
     n = 128
-    d[...] = a[:n, :n]
-    left[...] = jnp.zeros(left.shape, f32)
-    r[...] = jnp.zeros(r.shape, f32)
-    block_steps(a, d, left, r, 0, early)
-    slot_out.wait()
-    mixing_out.wait()
+    block_step(jnp.int32(0), invert_block(a[:n, :n], n, panel, 0, n), a, d, left, r)
+    update(a, left, r)
+    d[...] = invert_block(d[...], n, panel, 0, n // 2)
 
 
 def gram(flag, kept_index, packets, dense):
@@ -477,20 +467,18 @@
         "gram",
         (
             shape((kept, width), f32),
-            shape((kept, kept), f32),
+            shape((kept, width), bf16),
+            shape((count_rows * group, width), bf16),
             shape((kept, kept), f32),
             shape((n, n), f32),
-            shape((kept, n), f32),
-            shape((n, kept), f32),
         ),
         in_specs=[whole_smem] + [whole_vmem] * 2 + [whole_any],
-        out_specs=[whole_any] * 2 + [whole_vmem] * 4,
+        out_specs=[whole_vmem] * 5,
         scratch_shapes=[
-            pltpu.VMEM((kept, width), bf16),
+            pltpu.VMEM((kept, n), f32),
+            pltpu.VMEM((n, kept), f32),
             pltpu.VMEM((kept, 2 * width), bf16),
-            pltpu.VMEM((kept, width), f32),
             pltpu.VMEM((kept, kept), f32),
-            pltpu.SemaphoreType.DMA((2,)),
         ],
         cost_estimate=pl.CostEstimate(
             flops=10**10, bytes_accessed=6 * 2**20, transcendentals=2**18
@@ -508,19 +496,21 @@
 
 
 def weigh_kernel(
-    flag_ref, slot_ref, mixing_ref, a_ref, d_ref, left_ref, r_ref,
-    weight_ref, share_ref, plain_ref, a, d, left, r, slot, mixing, sems,
+    flag_ref, slot, keys, q, a_ref, d_ref,
+    weight_ref, share_ref, plain_ref, a, d, left, r, mixing,
 ):
-    slot_in = pltpu.make_async_copy(slot_ref, slot, sems.at[0])
-    mixing_in = pltpu.make_async_copy(mixing_ref, mixing, sems.at[1])
-    slot_in.start()
-    mixing_in.start()
+    mixing[...] = mix(keys, q)
     a[...] = a_ref[...]
-    d[...] = d_ref[...]
-    left[...] = left_ref[...]
-    r[...] = r_ref[...]
+    n = 128
+    block_step(jnp.int32(1), invert_block(d_ref[...], n, panel, n // 2, n), a, d, left, r)
+
+    def step(k, _):
+        update(a, left, r)
+        block_step(k, invert_block(d[...], n, panel, 0, n), a, d, left, r)
+        return 0
+
+    lax.fori_loop(2, kept // n, step, 0)
     plane, own = spread_index()
-    block_steps(a, d, left, r, early, 4)
     rows = [pl.ds(pl.multiple_of(128 * (plane ^ k) + 8 * own, 8), 8) for k in range(4)]
     picked = jnp.concatenate([a[at, :] for at in rows], 0)
     picked -= jnp.dot(
@@ -529,8 +519,6 @@
         precision=highest,
         preferred_element_type=f32,
     )
-    slot_in.wait()
-    mixing_in.wait()
     weight_ref[...] = in_pieces(
         jnp.dot(picked, mixing[...], precision=highest, preferred_element_type=f32)
     )
@@ -551,7 +539,7 @@
         )
 
 
-def weigh(flag, slot, mixing, a, d, left, r):
+def weigh(flag, *state):
     n = 128
     return call(
         weigh_kernel,
@@ -561,22 +549,20 @@
             shape((96, count_rows * slots), bf16),
             shape((32, width), f32),
         ),
-        in_specs=[whole_smem] + [whole_any] * 2 + [whole_vmem] * 4,
+        in_specs=[whole_smem] + [whole_vmem] * 5,
         out_specs=[whole_vmem] * 3,
         scratch_shapes=[
             pltpu.VMEM((kept, kept), f32),
             pltpu.VMEM((n, n), f32),
             pltpu.VMEM((kept, n), f32),
             pltpu.VMEM((n, kept), f32),
-            pltpu.VMEM((kept, width), f32),
             pltpu.VMEM((kept, kept), f32),
-            pltpu.SemaphoreType.DMA((2,)),
         ],
         cost_estimate=pl.CostEstimate(
             flops=2 * 10**10, bytes_accessed=6 * 2**20, transcendentals=0
         ),
         compiler_params=params(20),
-    )(flag, slot, mixing, a, d, left, r)
+    )(flag, *state)
 
 
 def finish_kernel(weight_ref, share_ref, plain_ref, full_ref, sent_ref, *out_refs):

time: 98.5 us -> 94.8 us (0.962)
  local copies, waits for them, and re-layouts: 2.95 us -> 0.04 us
    unnamed x12 -> x6, local copies, waits for them, and re-layouts: 2.92 us -> 0.01 us
    pallas_call x1, Pallas kernels: 9.06 us -> 10.9 us  [gram(): call(gram_kernel, 'gram', (shape((kept, width), f32), shape((kept, width)...]
    pallas_call x1, Pallas kernels: 16.8 us -> 15.2 us  [weigh(): call(weigh_kernel, 'weigh', (shape((96, kept), bf16), shape((96, count_ro...]
  transfers between devices with their start and end apart: 9 -> 9, of which waited for: 4 -> 4; matrix products, arithmetic and copies ran while one was open for 0% -> 0% of each run, Pallas kernels for 36% -> 38%
where the time goes in v4:
time: 94.8 us; the launch traced here: 94.3 us
  Pallas kernels  41.9 us (44%)
  starting transfers between devices  32.8 us (35%)
  waiting for transfers between devices  17.3 us (18%)
  between operations  2.02 us (2%)
    pallas_call x1, Pallas kernels, weigh(): call(weigh_kernel, 'weigh', (shape((96, kept), bf16), shape((96, count_ro...  15.2 us
    all_to_all x1, starting transfers between devices, on_device(): packets = lax.all_to_all(packets, seq_axes, 0, 0)  11.4 us
    all_to_all x1, waiting for transfers between devices, on_device(): packets = lax.all_to_all(packets, seq_axes, 0, 0)  11.4 us
    pallas_call x1, Pallas kernels, gram(): call(gram_kernel, 'gram', (shape((kept, width), f32), shape((kept, width)...  10.9 us
    ppermute x6, starting transfers between devices, along_x(): lax.ppermute(blocks[k], 'x', [(i, i ^ k) for i in range(4)])  9.56 us
    pallas_call x1, Pallas kernels, attend(): call(attend_kernel, 'attend', (shape((count_rows, heads_here + 1, group,...  9.51 us
    all_to_all x1, starting transfers between devices, on_device(): parts = lax.all_to_all(parts, seq_axes, 0, 0)  5.9 us
    all_to_all x1, starting transfers between devices, on_device(): sent = lax.all_to_all(sent, ('y', 'z'), 0, 0)  5.89 us
  transfers between devices with their start and end apart: 9, of which 4 were waited for; matrix products, arithmetic and copies ran while one was open for 0% of the time, Pallas kernels for 38%

profile of v4, /device:TPU:8, one launch (start us, length us, event | category | flops | bytes accessed | tf_op | source)
XLA Modules:
  0.0 94.3 jit_solution(16373120496336645506)
XLA Ops:
  1.3 0.0 copy-start.1
  1.3 4.0 %pack.1 = (bf16[64,7,8,128]{3,2,1,0:T(8,128)(2,1)}, bf16[3,8,128]{2,1,0:T(8,128)(2,1)}, bf16[3,8,128]{2,1,0:T(8,128)(2,1)}, bf16[3,8,128]{2,1,0:T(8,128)(2,1)}, bf16[3,8,128]{2,1,0:T(8,128)(2,1)}) custom-call(s32[1]{0:T(128)S(6)} %copy.10.pos_ref, s32[4,512]{1,0:T(4,128)} %index_ref.3, bf16[4,8,128]{2,1,0:T(8,128)(2,1)} %bitcast.27, ...), custom_call_target="tpu_custom_call" | custom-call | flops 536870912 | bytes 5242880 | tf_op jit(solution)/shard_map/pack/pallas_call | solution.py:129
  5.3 11.4 %all-to-all-start.2 = ((bf16[64,7,8,128]{3,2,1,0:T(8,128)(2,1)}), bf16[64,7,8,128]{3,2,1,0:T(8,128)(2,1)S(1)}, u32[]{:S(2)}, u32[]{:S(2)}) async-start(bf16[64,7,8,128]{3,2,1,0:T(8,128)(2,1)} %get-tuple-element.37), calls=%async_computation.2 | async-start | bytes 1835008 | tf_op jit(solution)/shard_map/all_to_all | solution.py:647
  16.7 1.6 %collective-permute-start = (bf16[3,8,128]{2,1,0:T(8,128)(2,1)}, bf16[3,8,128]{2,1,0:T(8,128)(2,1)S(1)}, u32[]{:S(2)}, u32[]{:S(2)}) collective-permute-start(bf16[3,8,128]{2,1,0:T(8,128)(2,1)} %get-tuple-element.49), channel_id=1, source_target_pairs={{0,32},{32,0},{64,96},{96,64},{1,33},{33,1},{65,97},{97,65},{2,34}... | collective-permute-start | bytes 18440 | tf_op jit(solution)/shard_map/ppermute | solution.py:637
  18.3 2.9 %collective-permute-start.1 = (bf16[3,8,128]{2,1,0:T(8,128)(2,1)}, bf16[3,8,128]{2,1,0:T(8,128)(2,1)S(1)}, u32[]{:S(2)}, u32[]{:S(2)}) collective-permute-start(bf16[3,8,128]{2,1,0:T(8,128)(2,1)} %get-tuple-element.50), channel_id=1, source_target_pairs={{0,64},{32,96},{64,0},{96,32},{1,65},{33,97},{65,1},{97,33},{2,66}... | collective-permute-start | bytes 18440 | tf_op jit(solution)/shard_map/ppermute | solution.py:637
  21.2 0.3 collective-permute-start.2
  21.5 0.0 copy-start.2
  21.5 11.4 %all-to-all-done.2.queries_ref.packets_ref = bf16[64,7,8,128]{3,2,1,0:T(8,128)(2,1)S(1)} async-done(((bf16[64,7,8,128]{3,2,1,0:T(8,128)(2,1)}), bf16[64,7,8,128]{3,2,1,0:T(8,128)(2,1)S(1)}, u32[]{:S(2)}, u32[]{:S(2)}) %all-to-all-start.2) | async-done | bytes 917536 | tf_op jit(solution)/shard_map/all_to_all | solution.py:647
  32.9 0.0 copy-done.1
  32.9 9.5 %attend.1 = (bf16[64,5,8,128]{3,2,1,0:T(8,128)(2,1)}, s32[1]{0:T(128)}) custom-call(bf16[64,7,8,128]{3,2,1,0:T(8,128)(2,1)S(1)} %all-to-all-done.2.queries_ref.packets_ref, bf16[8192,128]{1,0:T(8,128)(2,1)S(1)} %bitcast.21, bf16[8192,128]{1,0:T(8,128)(2,1)} %bitcast.23), custom_call_target="tpu_custom_call" | custom-call | flops 4294967296 | bytes 6291456 | tf_op jit(solution)/shard_map/attend/pallas_call | solution.py:233
  43.1 0.0 copy-done.2
  43.1 0.3 conditional.1
  43.3 5.9 %all-to-all-start.3 = ((bf16[64,5,8,128]{3,2,1,0:T(8,128)(2,1)}), bf16[64,5,8,128]{3,2,1,0:T(8,128)(2,1)S(1)}, u32[]{:S(2)}, u32[]{:S(2)}) async-start(bf16[64,5,8,128]{3,2,1,0:T(8,128)(2,1)} %get-tuple-element.47), calls=%async_computation.3 | async-start | bytes 1310720 | tf_op jit(solution)/shard_map/all_to_all | solution.py:650
  49.2 0.0 copy-start
  49.3 10.9 %gram.1 = (f32[512,128]{1,0:T(8,128)S(1)}, bf16[512,128]{1,0:T(8,128)(2,1)S(1)}, bf16[512,128]{1,0:T(8,128)(2,1)S(1)}, f32[512,512]{1,0:T(8,128)S(1)}, f32[128,128]{1,0:T(8,128)S(1)}) custom-call(s32[1]{0:T(128)} %get-tuple-element.38.flag_ref, s32[4,512]{1,0:T(4,128)S(1)} %copy-done.2, bf16[64,7,8,128]{3,2,1,0:T(8,128)(2,1)S(1)} %all-to-all-done.2.queries_ref.packets_ref, ...), custom_call_target="tpu_custom_call" | custom-call | flops 10000000000 | bytes 6291456 | tf_op jit(solution)/shard_map/gram/pallas_call | solution.py:465
  60.2 0.0 collective-permute-done.v1_ref
  60.2 0.0 collective-permute-done.1.v2_ref
  60.2 0.0 collective-permute-done.2.v3_ref
  60.2 1.4 %all-to-all-done.3.parts_ref = bf16[64,5,8,128]{3,2,1,0:T(8,128)(2,1)S(1)} async-done(((bf16[64,5,8,128]{3,2,1,0:T(8,128)(2,1)}), bf16[64,5,8,128]{3,2,1,0:T(8,128)(2,1)S(1)}, u32[]{:S(2)}, u32[]{:S(2)}) %all-to-all-start.3) | async-done | bytes 655392 | tf_op jit(solution)/shard_map/all_to_all | solution.py:650
  61.6 0.0 copy-done
  61.6 1.5 %combine.1 = (f32[4,8,128]{2,1,0:T(8,128)S(1)}, bf16[16,20,8,128]{3,2,1,0:T(8,128)(2,1)}) custom-call(bf16[64,5,8,128]{3,2,1,0:T(8,128)(2,1)S(1)} %all-to-all-done.3.parts_ref, bf16[3,8,128]{2,1,0:T(8,128)(2,1)S(1)} %copy-done, bf16[3,8,128]{2,1,0:T(8,128)(2,1)S(1)} %collective-permute-done.v1_ref, bf16[3,8,128]{2,1,0:T(8,128)(2,1)S(1)} %collective-permute-done.1.v2_ref, ...), custom_call_target="tpu_custom_call" | custom-call | flops 2097152 | bytes 2097152 | tf_op jit(solution)/shard_map/combine/pallas_call | solution.py:282
  63.0 5.9 %all-to-all-start.4 = ((bf16[16,20,8,128]{3,2,1,0:T(8,128)(2,1)}), bf16[16,20,8,128]{3,2,1,0:T(8,128)(2,1)S(1)}, u32[]{:S(2)}, u32[]{:S(2)}) async-start(bf16[16,20,8,128]{3,2,1,0:T(8,128)(2,1)} %get-tuple-element.53), calls=%async_computation.4 | async-start | bytes 1310720 | tf_op jit(solution)/shard_map/all_to_all | solution.py:661
  68.9 15.2 %weigh.1 = (bf16[96,512]{1,0:T(8,128)(2,1)S(1)}, bf16[96,1536]{1,0:T(8,128)(2,1)S(1)}, f32[32,128]{1,0:T(8,128)S(1)}) custom-call(s32[1]{0:T(128)} %get-tuple-element.38.flag_ref, f32[512,128]{1,0:T(8,128)S(1)} %get-tuple-element.39.slot, bf16[512,128]{1,0:T(8,128)(2,1)S(1)} %get-tuple-element.40.keys, bf16[512,128]{1,0:T(8,128)(2,1)S(1)} %get-tuple-element.41.q, ...), custom_call_target="tpu_custom_call" | custom-call | flops 20000000000 | bytes 6291456 | tf_op jit(solution)/shard_map/weigh/pallas_call | solution.py:544
  84.1 0.0 all-to-all-done.4.sent_ref
  84.1 0.3 finish.1
  84.4 1.6 %collective-permute-start.3 = (f32[16,128]{1,0:T(8,128)S(1)}, f32[16,128]{1,0:T(8,128)S(1)}, u32[]{:S(2)}, u32[]{:S(2)}) collective-permute-start(f32[16,128]{1,0:T(8,128)S(1)} %get-tuple-element.55), channel_id=1, source_target_pairs={{0,32},{32,0},{64,96},{96,64},{1,33},{33,1},{65,97},{97,65},{2,34}... | collective-permute-start | bytes 24584 | tf_op jit(solution)/shard_map/ppermute | solution.py:637
  86.0 2.9 %collective-permute-start.4 = (f32[16,128]{1,0:T(8,128)S(1)}, f32[16,128]{1,0:T(8,128)S(1)}, u32[]{:S(2)}, u32[]{:S(2)}) collective-permute-start(f32[16,128]{1,0:T(8,128)S(1)} %get-tuple-element.56), channel_id=1, source_target_pairs={{0,64},{32,96},{64,0},{96,32},{1,65},{33,97},{65,1},{97,33},{2,66}... | collective-permute-start | bytes 24584 | tf_op jit(solution)/shard_map/ppermute | solution.py:637
  88.9 0.3 collective-permute-start.5
  89.1 0.0 collective-permute-done.3.b1_ref
  89.2 2.0 %collective-permute-done.4.b2_ref = f32[16,128]{1,0:T(8,128)S(1)} collective-permute-done((f32[16,128]{1,0:T(8,128)S(1)}, f32[16,128]{1,0:T(8,128)S(1)}, u32[]{:S(2)}, u32[]{:S(2)}) %collective-permute-start.4) | collective-permute-done | bytes 8224 | tf_op jit(solution)/shard_map/ppermute | solution.py:637
  91.1 2.6 %collective-permute-done.5.b3_ref = f32[16,128]{1,0:T(8,128)S(1)} collective-permute-done((f32[16,128]{1,0:T(8,128)S(1)}, f32[16,128]{1,0:T(8,128)S(1)}, u32[]{:S(2)}, u32[]{:S(2)}) %collective-permute-start.5) | collective-permute-done | bytes 8224 | tf_op jit(solution)/shard_map/ppermute | solution.py:637
  93.7 0.6 arrange.1
  (1 shorter events, 0.0 us)
Async XLA Ops:
  1.3 31.7 %copy-start.1 = (bf16[2048,4,128]{2,1,0:T(4,128)(2,1)S(1)}, bf16[2048,4,128]{2,1,0:T(4,128)(2,1)}, u32[]{:S(2)}) copy-start(bf16[2048,4,128]{2,1,0:T(4,128)(2,1)} %param.9) | copy-start | bytes 6291460
  5.3 27.6 %all-to-all-start.2 = ((bf16[64,7,8,128]{3,2,1,0:T(8,128)(2,1)}), bf16[64,7,8,128]{3,2,1,0:T(8,128)(2,1)S(1)}, u32[]{:S(2)}, u32[]{:S(2)}) async-start(bf16[64,7,8,128]{3,2,1,0:T(8,128)(2,1)} %get-tuple-element.37), calls=%async_computation.2 | async-start | bytes 1835008 | tf_op jit(solution)/shard_map/all_to_all | solution.py:647
  16.7 43.5 %collective-permute-start = (bf16[3,8,128]{2,1,0:T(8,128)(2,1)}, bf16[3,8,128]{2,1,0:T(8,128)(2,1)S(1)}, u32[]{:S(2)}, u32[]{:S(2)}) collective-permute-start(bf16[3,8,128]{2,1,0:T(8,128)(2,1)} %get-tuple-element.49), channel_id=1, source_target_pairs={{0,32},{32,0},{64,96},{96,64},{1,33},{33,1},{65,97},{97,65},{2,34}... | collective-permute-start | bytes 18440 | tf_op jit(solution)/shard_map/ppermute | solution.py:637
  18.3 41.9 %collective-permute-start.1 = (bf16[3,8,128]{2,1,0:T(8,128)(2,1)}, bf16[3,8,128]{2,1,0:T(8,128)(2,1)S(1)}, u32[]{:S(2)}, u32[]{:S(2)}) collective-permute-start(bf16[3,8,128]{2,1,0:T(8,128)(2,1)} %get-tuple-element.50), channel_id=1, source_target_pairs={{0,64},{32,96},{64,0},{96,32},{1,65},{33,97},{65,1},{97,33},{2,66}... | collective-permute-start | bytes 18440 | tf_op jit(solution)/shard_map/ppermute | solution.py:637
  21.2 39.0 %collective-permute-start.2 = (bf16[3,8,128]{2,1,0:T(8,128)(2,1)}, bf16[3,8,128]{2,1,0:T(8,128)(2,1)S(1)}, u32[]{:S(2)}, u32[]{:S(2)}) collective-permute-start(bf16[3,8,128]{2,1,0:T(8,128)(2,1)} %get-tuple-element.51), channel_id=1, source_target_pairs={{0,96},{32,64},{64,32},{96,0},{1,97},{33,65},{65,33},{97,1},{2,98}... | collective-permute-start | bytes 18440 | tf_op jit(solution)/shard_map/ppermute | solution.py:637
  21.5 21.6 %copy-start.2 = (s32[4,512]{1,0:T(4,128)S(1)}, s32[4,512]{1,0:T(4,128)}, u32[]{:S(2)}) copy-start(s32[4,512]{1,0:T(4,128)} %index_ref.3) | copy-start | bytes 24580
  43.3 18.2 %all-to-all-start.3 = ((bf16[64,5,8,128]{3,2,1,0:T(8,128)(2,1)}), bf16[64,5,8,128]{3,2,1,0:T(8,128)(2,1)S(1)}, u32[]{:S(2)}, u32[]{:S(2)}) async-start(bf16[64,5,8,128]{3,2,1,0:T(8,128)(2,1)} %get-tuple-element.47), calls=%async_computation.3 | async-start | bytes 1310720 | tf_op jit(solution)/shard_map/all_to_all | solution.py:650
  49.2 12.3 %copy-start = (bf16[3,8,128]{2,1,0:T(8,128)(2,1)S(1)}, bf16[3,8,128]{2,1,0:T(8,128)(2,1)}, u32[]{:S(2)}) copy-start(bf16[3,8,128]{2,1,0:T(8,128)(2,1)} %get-tuple-element.48.v0_ref) | copy-start | bytes 18436
  63.0 21.1 %all-to-all-start.4 = ((bf16[16,20,8,128]{3,2,1,0:T(8,128)(2,1)}), bf16[16,20,8,128]{3,2,1,0:T(8,128)(2,1)S(1)}, u32[]{:S(2)}, u32[]{:S(2)}) async-start(bf16[16,20,8,128]{3,2,1,0:T(8,128)(2,1)} %get-tuple-element.53), calls=%async_computation.4 | async-start | bytes 1310720 | tf_op jit(solution)/shard_map/all_to_all | solution.py:661
  84.4 4.8 %collective-permute-start.3 = (f32[16,128]{1,0:T(8,128)S(1)}, f32[16,128]{1,0:T(8,128)S(1)}, u32[]{:S(2)}, u32[]{:S(2)}) collective-permute-start(f32[16,128]{1,0:T(8,128)S(1)} %get-tuple-element.55), channel_id=1, source_target_pairs={{0,32},{32,0},{64,96},{96,64},{1,33},{33,1},{65,97},{97,65},{2,34}... | collective-permute-start | bytes 24584 | tf_op jit(solution)/shard_map/ppermute | solution.py:637
  86.0 5.2 %collective-permute-start.4 = (f32[16,128]{1,0:T(8,128)S(1)}, f32[16,128]{1,0:T(8,128)S(1)}, u32[]{:S(2)}, u32[]{:S(2)}) collective-permute-start(f32[16,128]{1,0:T(8,128)S(1)} %get-tuple-element.56), channel_id=1, source_target_pairs={{0,64},{32,96},{64,0},{96,32},{1,65},{33,97},{65,1},{97,33},{2,66}... | collective-permute-start | bytes 24584 | tf_op jit(solution)/shard_map/ppermute | solution.py:637
  88.9 4.9 %collective-permute-start.5 = (f32[16,128]{1,0:T(8,128)S(1)}, f32[16,128]{1,0:T(8,128)S(1)}, u32[]{:S(2)}, u32[]{:S(2)}) collective-permute-start(f32[16,128]{1,0:T(8,128)S(1)} %get-tuple-element.57), channel_id=1, source_target_pairs={{0,96},{32,64},{64,32},{96,0},{1,97},{33,65},{65,33},{97,1},{2,98}... | collective-permute-start | bytes 24584 | tf_op jit(solution)/shard_map/ppermute | solution.py:637

commit v5 on v4

--- a/solution.py
+++ b/solution.py
@@ -186,13 +186,9 @@
     side[...] = jnp.zeros(side.shape, f32)
 
     def scores(h, part):
-        at = pl.ds(h, local_len, stride=heads_here)
         if part == 0:
+            at = pl.ds(h, local_len, stride=heads_here)
             keys[h % 2, :, :width] = wide[0, at, :].astype(bf16)
-            if h == 0:
-                move.wait()
-                wide[1] = raw[...].astype(f32)
-            values[h % 2, :, :width] = wide[1, at, :].astype(bf16)
         rows = tile // group
         q = queries_ref[part * rows : (part + 1) * rows, h].astype(f32).reshape(tile, width)
         own = jnp.where(row_t // group + part * rows == lane_t, 1.0, 0.0)
@@ -207,6 +203,12 @@
         after = scores(*steps[i + 1]) if i + 1 < len(steps) else None
         peak = jnp.max(s, axis=1, keepdims=True)
         w = jnp.exp2((s - peak) * scale_log2).astype(bf16)
+        if i == 0:
+            move.wait()
+            wide[1] = raw[...].astype(f32)
+        if part == 0:
+            at = pl.ds(h, local_len, stride=heads_here)
+            values[h % 2, :, :width] = wide[1, at, :].astype(bf16)
         o = jnp.dot(w, values[h % 2], preferred_element_type=f32)
         sums = o[:, width : width + 1]
         mass = peak * scale_log2 + jnp.log2(sums)
@@ -457,7 +459,7 @@
     n = 128
     block_step(jnp.int32(0), invert_block(a[:n, :n], n, panel, 0, n), a, d, left, r)
     update(a, left, r)
-    d[...] = invert_block(d[...], n, panel, 0, n // 2)
+    d[...] = invert_block(d[...], n, 32, 0, 96)
 
 
 def gram(flag, kept_index, packets, dense):
@@ -502,7 +504,7 @@
     mixing[...] = mix(keys, q)
     a[...] = a_ref[...]
     n = 128
-    block_step(jnp.int32(1), invert_block(d_ref[...], n, panel, n // 2, n), a, d, left, r)
+    block_step(jnp.int32(1), invert_block(d_ref[...], n, 32, 96, n), a, d, left, r)
 
     def step(k, _):
         update(a, left, r)

time: 94.8 us -> 93.9 us (level)
  starting transfers between devices: 32.8 us -> 34.1 us
  waiting for transfers between devices: 17.3 us -> 16 us
    pallas_call x1, Pallas kernels: 10.9 us -> 12.4 us  [gram(): call(gram_kernel, 'gram', (shape((kept, width), f32), shape((kept, width)...]
    pallas_call x1, Pallas kernels: 15.2 us -> 13.7 us  [weigh(): call(weigh_kernel, 'weigh', (shape((96, kept), bf16), shape((96, count_ro...]
    all_to_all x1, waiting for transfers between devices: 1.35 us -> 0.01 us  [on_device(): parts = lax.all_to_all(parts, seq_axes, 0, 0)]
    all_to_all x1, starting transfers between devices: 5.89 us -> 7.22 us  [on_device(): sent = lax.all_to_all(sent, ('y', 'z'), 0, 0)]
  transfers between devices with their start and end apart: 9 -> 9, of which waited for: 4 -> 3; matrix products, arithmetic and copies ran while one was open for 0% -> 0% of each run, Pallas kernels for 38% -> 37%
where the time goes in v5:
time: 93.9 us; the launch traced here: 93.5 us
  Pallas kernels  41.1 us (44%)
  starting transfers between devices  34.1 us (36%)
  waiting for transfers between devices  16 us (17%)
  between operations  2.03 us (2%)
    pallas_call x1, Pallas kernels, weigh(): call(weigh_kernel, 'weigh', (shape((96, kept), bf16), shape((96, count_ro...  13.7 us
    pallas_call x1, Pallas kernels, gram(): call(gram_kernel, 'gram', (shape((kept, width), f32), shape((kept, width)...  12.4 us
    all_to_all x1, starting transfers between devices, on_device(): packets = lax.all_to_all(packets, seq_axes, 0, 0)  11.4 us
    all_to_all x1, waiting for transfers between devices, on_device(): packets = lax.all_to_all(packets, seq_axes, 0, 0)  11.4 us
    ppermute x6, starting transfers between devices, along_x(): lax.ppermute(blocks[k], 'x', [(i, i ^ k) for i in range(4)])  9.56 us
    pallas_call x1, Pallas kernels, attend(): call(attend_kernel, 'attend', (shape((count_rows, heads_here + 1, group,...  8.63 us
    all_to_all x1, starting transfers between devices, on_device(): sent = lax.all_to_all(sent, ('y', 'z'), 0, 0)  7.22 us
    all_to_all x1, starting transfers between devices, on_device(): parts = lax.all_to_all(parts, seq_axes, 0, 0)  5.9 us
  transfers between devices with their start and end apart: 9, of which 3 were waited for; matrix products, arithmetic and copies ran while one was open for 0% of the time, Pallas kernels for 37%

profile of v5, /device:TPU:8, one launch (start us, length us, event | category | flops | bytes accessed | tf_op | source)
XLA Modules:
  0.0 93.5 jit_solution(10802910027464797144)
XLA Ops:
  1.3 0.0 copy-start.1
  1.3 4.0 %pack.1 = (bf16[64,7,8,128]{3,2,1,0:T(8,128)(2,1)}, bf16[3,8,128]{2,1,0:T(8,128)(2,1)}, bf16[3,8,128]{2,1,0:T(8,128)(2,1)}, bf16[3,8,128]{2,1,0:T(8,128)(2,1)}, bf16[3,8,128]{2,1,0:T(8,128)(2,1)}) custom-call(s32[1]{0:T(128)S(6)} %copy.10.pos_ref, s32[4,512]{1,0:T(4,128)} %index_ref.3, bf16[4,8,128]{2,1,0:T(8,128)(2,1)} %bitcast.27, ...), custom_call_target="tpu_custom_call" | custom-call | flops 536870912 | bytes 5242880 | tf_op jit(solution)/shard_map/pack/pallas_call | solution.py:129
  5.3 11.4 %all-to-all-start.2 = ((bf16[64,7,8,128]{3,2,1,0:T(8,128)(2,1)}), bf16[64,7,8,128]{3,2,1,0:T(8,128)(2,1)S(1)}, u32[]{:S(2)}, u32[]{:S(2)}) async-start(bf16[64,7,8,128]{3,2,1,0:T(8,128)(2,1)} %get-tuple-element.37), calls=%async_computation.2 | async-start | bytes 1835008 | tf_op jit(solution)/shard_map/all_to_all | solution.py:649
  16.7 1.6 %collective-permute-start = (bf16[3,8,128]{2,1,0:T(8,128)(2,1)}, bf16[3,8,128]{2,1,0:T(8,128)(2,1)S(1)}, u32[]{:S(2)}, u32[]{:S(2)}) collective-permute-start(bf16[3,8,128]{2,1,0:T(8,128)(2,1)} %get-tuple-element.49), channel_id=1, source_target_pairs={{0,32},{32,0},{64,96},{96,64},{1,33},{33,1},{65,97},{97,65},{2,34}... | collective-permute-start | bytes 18440 | tf_op jit(solution)/shard_map/ppermute | solution.py:639
  18.3 2.9 %collective-permute-start.1 = (bf16[3,8,128]{2,1,0:T(8,128)(2,1)}, bf16[3,8,128]{2,1,0:T(8,128)(2,1)S(1)}, u32[]{:S(2)}, u32[]{:S(2)}) collective-permute-start(bf16[3,8,128]{2,1,0:T(8,128)(2,1)} %get-tuple-element.50), channel_id=1, source_target_pairs={{0,64},{32,96},{64,0},{96,32},{1,65},{33,97},{65,1},{97,33},{2,66}... | collective-permute-start | bytes 18440 | tf_op jit(solution)/shard_map/ppermute | solution.py:639
  21.2 0.3 collective-permute-start.2
  21.5 0.0 copy-start.2
  21.5 11.4 %all-to-all-done.2.queries_ref.packets_ref = bf16[64,7,8,128]{3,2,1,0:T(8,128)(2,1)S(1)} async-done(((bf16[64,7,8,128]{3,2,1,0:T(8,128)(2,1)}), bf16[64,7,8,128]{3,2,1,0:T(8,128)(2,1)S(1)}, u32[]{:S(2)}, u32[]{:S(2)}) %all-to-all-start.2) | async-done | bytes 917536 | tf_op jit(solution)/shard_map/all_to_all | solution.py:649
  32.9 0.0 copy-done.1
  32.9 8.6 %attend.1 = (bf16[64,5,8,128]{3,2,1,0:T(8,128)(2,1)}, s32[1]{0:T(128)}) custom-call(bf16[64,7,8,128]{3,2,1,0:T(8,128)(2,1)S(1)} %all-to-all-done.2.queries_ref.packets_ref, bf16[8192,128]{1,0:T(8,128)(2,1)S(1)} %bitcast.21, bf16[8192,128]{1,0:T(8,128)(2,1)} %bitcast.23), custom_call_target="tpu_custom_call" | custom-call | flops 4294967296 | bytes 6291456 | tf_op jit(solution)/shard_map/attend/pallas_call | solution.py:235
  42.2 0.0 copy-done.2
  42.2 0.3 conditional.1
  42.5 5.9 %all-to-all-start.3 = ((bf16[64,5,8,128]{3,2,1,0:T(8,128)(2,1)}), bf16[64,5,8,128]{3,2,1,0:T(8,128)(2,1)S(1)}, u32[]{:S(2)}, u32[]{:S(2)}) async-start(bf16[64,5,8,128]{3,2,1,0:T(8,128)(2,1)} %get-tuple-element.47), calls=%async_computation.3 | async-start | bytes 1310720 | tf_op jit(solution)/shard_map/all_to_all | solution.py:652
  48.4 0.0 copy-start
  48.4 12.4 %gram.1 = (f32[512,128]{1,0:T(8,128)S(1)}, bf16[512,128]{1,0:T(8,128)(2,1)S(1)}, bf16[512,128]{1,0:T(8,128)(2,1)S(1)}, f32[512,512]{1,0:T(8,128)S(1)}, f32[128,128]{1,0:T(8,128)S(1)}) custom-call(s32[1]{0:T(128)} %get-tuple-element.38.flag_ref, s32[4,512]{1,0:T(4,128)S(1)} %copy-done.2, bf16[64,7,8,128]{3,2,1,0:T(8,128)(2,1)S(1)} %all-to-all-done.2.queries_ref.packets_ref, ...), custom_call_target="tpu_custom_call" | custom-call | flops 10000000000 | bytes 6291456 | tf_op jit(solution)/shard_map/gram/pallas_call | solution.py:467
  60.8 0.0 collective-permute-done.v1_ref
  60.8 0.0 collective-permute-done.1.v2_ref
  60.8 0.0 collective-permute-done.2.v3_ref
  60.9 0.0 all-to-all-done.3.parts_ref
  60.9 0.0 copy-done
  60.9 1.5 %combine.1 = (f32[4,8,128]{2,1,0:T(8,128)S(1)}, bf16[16,20,8,128]{3,2,1,0:T(8,128)(2,1)}) custom-call(bf16[64,5,8,128]{3,2,1,0:T(8,128)(2,1)S(1)} %all-to-all-done.3.parts_ref, bf16[3,8,128]{2,1,0:T(8,128)(2,1)S(1)} %copy-done, bf16[3,8,128]{2,1,0:T(8,128)(2,1)S(1)} %collective-permute-done.v1_ref, bf16[3,8,128]{2,1,0:T(8,128)(2,1)S(1)} %collective-permute-done.1.v2_ref, ...), custom_call_target="tpu_custom_call" | custom-call | flops 2097152 | bytes 2097152 | tf_op jit(solution)/shard_map/combine/pallas_call | solution.py:284
  62.3 7.2 %all-to-all-start.4 = ((bf16[16,20,8,128]{3,2,1,0:T(8,128)(2,1)}), bf16[16,20,8,128]{3,2,1,0:T(8,128)(2,1)S(1)}, u32[]{:S(2)}, u32[]{:S(2)}) async-start(bf16[16,20,8,128]{3,2,1,0:T(8,128)(2,1)} %get-tuple-element.53), calls=%async_computation.4 | async-start | bytes 1310720 | tf_op jit(solution)/shard_map/all_to_all | solution.py:663
  69.6 13.7 %weigh.1 = (bf16[96,512]{1,0:T(8,128)(2,1)S(1)}, bf16[96,1536]{1,0:T(8,128)(2,1)S(1)}, f32[32,128]{1,0:T(8,128)S(1)}) custom-call(s32[1]{0:T(128)} %get-tuple-element.38.flag_ref, f32[512,128]{1,0:T(8,128)S(1)} %get-tuple-element.39.slot, bf16[512,128]{1,0:T(8,128)(2,1)S(1)} %get-tuple-element.40.keys, bf16[512,128]{1,0:T(8,128)(2,1)S(1)} %get-tuple-element.41.q, ...), custom_call_target="tpu_custom_call" | custom-call | flops 20000000000 | bytes 6291456 | tf_op jit(solution)/shard_map/weigh/pallas_call | solution.py:546
  83.2 0.0 all-to-all-done.4.sent_ref
  83.2 0.3 finish.1
  83.5 1.6 %collective-permute-start.3 = (f32[16,128]{1,0:T(8,128)S(1)}, f32[16,128]{1,0:T(8,128)S(1)}, u32[]{:S(2)}, u32[]{:S(2)}) collective-permute-start(f32[16,128]{1,0:T(8,128)S(1)} %get-tuple-element.55), channel_id=1, source_target_pairs={{0,32},{32,0},{64,96},{96,64},{1,33},{33,1},{65,97},{97,65},{2,34}... | collective-permute-start | bytes 24584 | tf_op jit(solution)/shard_map/ppermute | solution.py:639
  85.1 2.9 %collective-permute-start.4 = (f32[16,128]{1,0:T(8,128)S(1)}, f32[16,128]{1,0:T(8,128)S(1)}, u32[]{:S(2)}, u32[]{:S(2)}) collective-permute-start(f32[16,128]{1,0:T(8,128)S(1)} %get-tuple-element.56), channel_id=1, source_target_pairs={{0,64},{32,96},{64,0},{96,32},{1,65},{33,97},{65,1},{97,33},{2,66}... | collective-permute-start | bytes 24584 | tf_op jit(solution)/shard_map/ppermute | solution.py:639
  88.0 0.3 collective-permute-start.5
  88.3 0.0 collective-permute-done.3.b1_ref
  88.3 2.0 %collective-permute-done.4.b2_ref = f32[16,128]{1,0:T(8,128)S(1)} collective-permute-done((f32[16,128]{1,0:T(8,128)S(1)}, f32[16,128]{1,0:T(8,128)S(1)}, u32[]{:S(2)}, u32[]{:S(2)}) %collective-permute-start.4) | collective-permute-done | bytes 8224 | tf_op jit(solution)/shard_map/ppermute | solution.py:639
  90.3 2.6 %collective-permute-done.5.b3_ref = f32[16,128]{1,0:T(8,128)S(1)} collective-permute-done((f32[16,128]{1,0:T(8,128)S(1)}, f32[16,128]{1,0:T(8,128)S(1)}, u32[]{:S(2)}, u32[]{:S(2)}) %collective-permute-start.5) | collective-permute-done | bytes 8224 | tf_op jit(solution)/shard_map/ppermute | solution.py:639
  92.9 0.6 arrange.1
  (1 shorter events, 0.0 us)
Async XLA Ops:
  1.3 31.7 %copy-start.1 = (bf16[2048,4,128]{2,1,0:T(4,128)(2,1)S(1)}, bf16[2048,4,128]{2,1,0:T(4,128)(2,1)}, u32[]{:S(2)}) copy-start(bf16[2048,4,128]{2,1,0:T(4,128)(2,1)} %param.9) | copy-start | bytes 6291460
  5.3 27.6 %all-to-all-start.2 = ((bf16[64,7,8,128]{3,2,1,0:T(8,128)(2,1)}), bf16[64,7,8,128]{3,2,1,0:T(8,128)(2,1)S(1)}, u32[]{:S(2)}, u32[]{:S(2)}) async-start(bf16[64,7,8,128]{3,2,1,0:T(8,128)(2,1)} %get-tuple-element.37), calls=%async_computation.2 | async-start | bytes 1835008 | tf_op jit(solution)/shard_map/all_to_all | solution.py:649
  16.7 44.1 %collective-permute-start = (bf16[3,8,128]{2,1,0:T(8,128)(2,1)}, bf16[3,8,128]{2,1,0:T(8,128)(2,1)S(1)}, u32[]{:S(2)}, u32[]{:S(2)}) collective-permute-start(bf16[3,8,128]{2,1,0:T(8,128)(2,1)} %get-tuple-element.49), channel_id=1, source_target_pairs={{0,32},{32,0},{64,96},{96,64},{1,33},{33,1},{65,97},{97,65},{2,34}... | collective-permute-start | bytes 18440 | tf_op jit(solution)/shard_map/ppermute | solution.py:639
  18.3 42.6 %collective-permute-start.1 = (bf16[3,8,128]{2,1,0:T(8,128)(2,1)}, bf16[3,8,128]{2,1,0:T(8,128)(2,1)S(1)}, u32[]{:S(2)}, u32[]{:S(2)}) collective-permute-start(bf16[3,8,128]{2,1,0:T(8,128)(2,1)} %get-tuple-element.50), channel_id=1, source_target_pairs={{0,64},{32,96},{64,0},{96,32},{1,65},{33,97},{65,1},{97,33},{2,66}... | collective-permute-start | bytes 18440 | tf_op jit(solution)/shard_map/ppermute | solution.py:639
  21.2 39.7 %collective-permute-start.2 = (bf16[3,8,128]{2,1,0:T(8,128)(2,1)}, bf16[3,8,128]{2,1,0:T(8,128)(2,1)S(1)}, u32[]{:S(2)}, u32[]{:S(2)}) collective-permute-start(bf16[3,8,128]{2,1,0:T(8,128)(2,1)} %get-tuple-element.51), channel_id=1, source_target_pairs={{0,96},{32,64},{64,32},{96,0},{1,97},{33,65},{65,33},{97,1},{2,98}... | collective-permute-start | bytes 18440 | tf_op jit(solution)/shard_map/ppermute | solution.py:639
  21.5 20.7 %copy-start.2 = (s32[4,512]{1,0:T(4,128)S(1)}, s32[4,512]{1,0:T(4,128)}, u32[]{:S(2)}) copy-start(s32[4,512]{1,0:T(4,128)} %index_ref.3) | copy-start | bytes 24580
  42.5 18.4 %all-to-all-start.3 = ((bf16[64,5,8,128]{3,2,1,0:T(8,128)(2,1)}), bf16[64,5,8,128]{3,2,1,0:T(8,128)(2,1)S(1)}, u32[]{:S(2)}, u32[]{:S(2)}) async-start(bf16[64,5,8,128]{3,2,1,0:T(8,128)(2,1)} %get-tuple-element.47), calls=%async_computation.3 | async-start | bytes 1310720 | tf_op jit(solution)/shard_map/all_to_all | solution.py:652
  48.4 12.5 %copy-start = (bf16[3,8,128]{2,1,0:T(8,128)(2,1)S(1)}, bf16[3,8,128]{2,1,0:T(8,128)(2,1)}, u32[]{:S(2)}) copy-start(bf16[3,8,128]{2,1,0:T(8,128)(2,1)} %get-tuple-element.48.v0_ref) | copy-start | bytes 18436
  62.3 20.9 %all-to-all-start.4 = ((bf16[16,20,8,128]{3,2,1,0:T(8,128)(2,1)}), bf16[16,20,8,128]{3,2,1,0:T(8,128)(2,1)S(1)}, u32[]{:S(2)}, u32[]{:S(2)}) async-start(bf16[16,20,8,128]{3,2,1,0:T(8,128)(2,1)} %get-tuple-element.53), calls=%async_computation.4 | async-start | bytes 1310720 | tf_op jit(solution)/shard_map/all_to_all | solution.py:663
  83.5 4.8 %collective-permute-start.3 = (f32[16,128]{1,0:T(8,128)S(1)}, f32[16,128]{1,0:T(8,128)S(1)}, u32[]{:S(2)}, u32[]{:S(2)}) collective-permute-start(f32[16,128]{1,0:T(8,128)S(1)} %get-tuple-element.55), channel_id=1, source_target_pairs={{0,32},{32,0},{64,96},{96,64},{1,33},{33,1},{65,97},{97,65},{2,34}... | collective-permute-start | bytes 24584 | tf_op jit(solution)/shard_map/ppermute | solution.py:639
  85.1 5.2 %collective-permute-start.4 = (f32[16,128]{1,0:T(8,128)S(1)}, f32[16,128]{1,0:T(8,128)S(1)}, u32[]{:S(2)}, u32[]{:S(2)}) collective-permute-start(f32[16,128]{1,0:T(8,128)S(1)} %get-tuple-element.56), channel_id=1, source_target_pairs={{0,64},{32,96},{64,0},{96,32},{1,65},{33,97},{65,1},{97,33},{2,66}... | collective-permute-start | bytes 24584 | tf_op jit(solution)/shard_map/ppermute | solution.py:639
  88.0 4.9 %collective-permute-start.5 = (f32[16,128]{1,0:T(8,128)S(1)}, f32[16,128]{1,0:T(8,128)S(1)}, u32[]{:S(2)}, u32[]{:S(2)}) collective-permute-start(f32[16,128]{1,0:T(8,128)S(1)} %get-tuple-element.57), channel_id=1, source_target_pairs={{0,96},{32,64},{64,32},{96,0},{1,97},{33,65},{65,33},{97,1},{2,98}... | collective-permute-start | bytes 24584 | tf_op jit(solution)/shard_map/ppermute | solution.py:639

commit v6 on v5

--- a/solution.py
+++ b/solution.py
@@ -502,7 +502,6 @@
     weight_ref, share_ref, plain_ref, a, d, left, r, mixing,
 ):
     mixing[...] = mix(keys, q)
-    a[...] = a_ref[...]
     n = 128
     block_step(jnp.int32(1), invert_block(d_ref[...], n, 32, 96, n), a, d, left, r)
 
@@ -550,11 +549,12 @@
             shape((96, kept), bf16),
             shape((96, count_rows * slots), bf16),
             shape((32, width), f32),
+            shape((kept, kept), f32),
         ),
         in_specs=[whole_smem] + [whole_vmem] * 5,
-        out_specs=[whole_vmem] * 3,
+        out_specs=[whole_vmem] * 4,
+        input_output_aliases={4: 3},
         scratch_shapes=[
-            pltpu.VMEM((kept, kept), f32),
             pltpu.VMEM((n, n), f32),
             pltpu.VMEM((kept, n), f32),
             pltpu.VMEM((n, kept), f32),
@@ -564,7 +564,7 @@
             flops=2 * 10**10, bytes_accessed=6 * 2**20, transcendentals=0
         ),
         compiler_params=params(20),
-    )(flag, *state)
+    )(flag, *state)[:3]
 
 
 def finish_kernel(weight_ref, share_ref, plain_ref, full_ref, sent_ref, *out_refs):

time: 93.9 us -> 93.9 us (level)
  no operation moved by 1% of the time
where the time goes in v6:
time: 93.9 us; the launch traced here: 93.5 us
  Pallas kernels  41.1 us (44%)
  starting transfers between devices  34.1 us (36%)
  waiting for transfers between devices  16 us (17%)
  between operations  2.03 us (2%)
    pallas_call x1, Pallas kernels, weigh(): call(weigh_kernel, 'weigh', (shape((96, kept), bf16), shape((96, count_ro...  13.7 us
    pallas_call x1, Pallas kernels, gram(): call(gram_kernel, 'gram', (shape((kept, width), f32), shape((kept, width)...  12.4 us
    all_to_all x1, starting transfers between devices, on_device(): packets = lax.all_to_all(packets, seq_axes, 0, 0)  11.4 us
    all_to_all x1, waiting for transfers between devices, on_device(): packets = lax.all_to_all(packets, seq_axes, 0, 0)  11.4 us
    ppermute x6, starting transfers between devices, along_x(): lax.ppermute(blocks[k], 'x', [(i, i ^ k) for i in range(4)])  9.56 us
    pallas_call x1, Pallas kernels, attend(): call(attend_kernel, 'attend', (shape((count_rows, heads_here + 1, group,...  8.63 us
    all_to_all x1, starting transfers between devices, on_device(): sent = lax.all_to_all(sent, ('y', 'z'), 0, 0)  7.22 us
    all_to_all x1, starting transfers between devices, on_device(): parts = lax.all_to_all(parts, seq_axes, 0, 0)  5.9 us
  transfers between devices with their start and end apart: 9, of which 3 were waited for; matrix products, arithmetic and copies ran while one was open for 0% of the time, Pallas kernels for 37%

profile of v6, /device:TPU:8, one launch (start us, length us, event | category | flops | bytes accessed | tf_op | source)
XLA Modules:
  0.0 93.5 jit_solution(5839318264763679167)
XLA Ops:
  1.3 0.0 copy-start.1
  1.3 4.0 %pack.1 = (bf16[64,7,8,128]{3,2,1,0:T(8,128)(2,1)}, bf16[3,8,128]{2,1,0:T(8,128)(2,1)}, bf16[3,8,128]{2,1,0:T(8,128)(2,1)}, bf16[3,8,128]{2,1,0:T(8,128)(2,1)}, bf16[3,8,128]{2,1,0:T(8,128)(2,1)}) custom-call(s32[1]{0:T(128)S(6)} %copy.12.pos_ref, s32[4,512]{1,0:T(4,128)} %index_ref.3, bf16[4,8,128]{2,1,0:T(8,128)(2,1)} %bitcast.27, ...), custom_call_target="tpu_custom_call" | custom-call | flops 536870912 | bytes 5242880 | tf_op jit(solution)/shard_map/pack/pallas_call | solution.py:129
  5.3 11.4 %all-to-all-start.2 = ((bf16[64,7,8,128]{3,2,1,0:T(8,128)(2,1)}), bf16[64,7,8,128]{3,2,1,0:T(8,128)(2,1)S(1)}, u32[]{:S(2)}, u32[]{:S(2)}) async-start(bf16[64,7,8,128]{3,2,1,0:T(8,128)(2,1)} %get-tuple-element.37), calls=%async_computation.2 | async-start | bytes 1835008 | tf_op jit(solution)/shard_map/all_to_all | solution.py:649
  16.7 1.6 %collective-permute-start = (bf16[3,8,128]{2,1,0:T(8,128)(2,1)}, bf16[3,8,128]{2,1,0:T(8,128)(2,1)S(1)}, u32[]{:S(2)}, u32[]{:S(2)}) collective-permute-start(bf16[3,8,128]{2,1,0:T(8,128)(2,1)} %get-tuple-element.49), channel_id=1, source_target_pairs={{0,32},{32,0},{64,96},{96,64},{1,33},{33,1},{65,97},{97,65},{2,34}... | collective-permute-start | bytes 18440 | tf_op jit(solution)/shard_map/ppermute | solution.py:639
  18.3 2.9 %collective-permute-start.1 = (bf16[3,8,128]{2,1,0:T(8,128)(2,1)}, bf16[3,8,128]{2,1,0:T(8,128)(2,1)S(1)}, u32[]{:S(2)}, u32[]{:S(2)}) collective-permute-start(bf16[3,8,128]{2,1,0:T(8,128)(2,1)} %get-tuple-element.50), channel_id=1, source_target_pairs={{0,64},{32,96},{64,0},{96,32},{1,65},{33,97},{65,1},{97,33},{2,66}... | collective-permute-start | bytes 18440 | tf_op jit(solution)/shard_map/ppermute | solution.py:639
  21.2 0.3 collective-permute-start.2
  21.5 0.0 copy-start.2
  21.5 11.4 %all-to-all-done.2.queries_ref.packets_ref = bf16[64,7,8,128]{3,2,1,0:T(8,128)(2,1)S(1)} async-done(((bf16[64,7,8,128]{3,2,1,0:T(8,128)(2,1)}), bf16[64,7,8,128]{3,2,1,0:T(8,128)(2,1)S(1)}, u32[]{:S(2)}, u32[]{:S(2)}) %all-to-all-start.2) | async-done | bytes 917536 | tf_op jit(solution)/shard_map/all_to_all | solution.py:649
  32.9 0.0 copy-done.1
  32.9 8.6 %attend.1 = (bf16[64,5,8,128]{3,2,1,0:T(8,128)(2,1)}, s32[1]{0:T(128)}) custom-call(bf16[64,7,8,128]{3,2,1,0:T(8,128)(2,1)S(1)} %all-to-all-done.2.queries_ref.packets_ref, bf16[8192,128]{1,0:T(8,128)(2,1)S(1)} %bitcast.21, bf16[8192,128]{1,0:T(8,128)(2,1)} %bitcast.23), custom_call_target="tpu_custom_call" | custom-call | flops 4294967296 | bytes 6291456 | tf_op jit(solution)/shard_map/attend/pallas_call | solution.py:235
  42.2 0.0 copy-done.2
  42.2 0.3 conditional.1
  42.5 5.9 %all-to-all-start.3 = ((bf16[64,5,8,128]{3,2,1,0:T(8,128)(2,1)}), bf16[64,5,8,128]{3,2,1,0:T(8,128)(2,1)S(1)}, u32[]{:S(2)}, u32[]{:S(2)}) async-start(bf16[64,5,8,128]{3,2,1,0:T(8,128)(2,1)} %get-tuple-element.47), calls=%async_computation.3 | async-start | bytes 1310720 | tf_op jit(solution)/shard_map/all_to_all | solution.py:652
  48.4 0.0 copy-start
  48.4 12.4 %gram.1 = (f32[512,128]{1,0:T(8,128)S(1)}, bf16[512,128]{1,0:T(8,128)(2,1)S(1)}, bf16[512,128]{1,0:T(8,128)(2,1)S(1)}, f32[512,512]{1,0:T(8,128)S(1)}, f32[128,128]{1,0:T(8,128)S(1)}) custom-call(s32[1]{0:T(128)} %get-tuple-element.38.flag_ref, s32[4,512]{1,0:T(4,128)S(1)} %copy-done.2, bf16[64,7,8,128]{3,2,1,0:T(8,128)(2,1)S(1)} %all-to-all-done.2.queries_ref.packets_ref, ...), custom_call_target="tpu_custom_call" | custom-call | flops 10000000000 | bytes 6291456 | tf_op jit(solution)/shard_map/gram/pallas_call | solution.py:467
  60.8 0.0 collective-permute-done.v1_ref
  60.8 0.0 collective-permute-done.1.v2_ref
  60.8 0.0 collective-permute-done.2.v3_ref
  60.9 0.0 all-to-all-done.3.parts_ref
  60.9 0.0 copy-done
  60.9 1.5 %combine.1 = (f32[4,8,128]{2,1,0:T(8,128)S(1)}, bf16[16,20,8,128]{3,2,1,0:T(8,128)(2,1)}) custom-call(bf16[64,5,8,128]{3,2,1,0:T(8,128)(2,1)S(1)} %all-to-all-done.3.parts_ref, bf16[3,8,128]{2,1,0:T(8,128)(2,1)S(1)} %copy-done, bf16[3,8,128]{2,1,0:T(8,128)(2,1)S(1)} %collective-permute-done.v1_ref, bf16[3,8,128]{2,1,0:T(8,128)(2,1)S(1)} %collective-permute-done.1.v2_ref, ...), custom_call_target="tpu_custom_call" | custom-call | flops 2097152 | bytes 2097152 | tf_op jit(solution)/shard_map/combine/pallas_call | solution.py:284
  62.3 7.2 %all-to-all-start.4 = ((bf16[16,20,8,128]{3,2,1,0:T(8,128)(2,1)}), bf16[16,20,8,128]{3,2,1,0:T(8,128)(2,1)S(1)}, u32[]{:S(2)}, u32[]{:S(2)}) async-start(bf16[16,20,8,128]{3,2,1,0:T(8,128)(2,1)} %get-tuple-element.53), calls=%async_computation.4 | async-start | bytes 1310720 | tf_op jit(solution)/shard_map/all_to_all | solution.py:663
  69.6 13.7 %weigh.1 = (bf16[96,512]{1,0:T(8,128)(2,1)S(1)}, bf16[96,1536]{1,0:T(8,128)(2,1)S(1)}, f32[32,128]{1,0:T(8,128)S(1)}, f32[512,512]{1,0:T(8,128)S(1)}) custom-call(s32[1]{0:T(128)} %get-tuple-element.38.flag_ref, f32[512,128]{1,0:T(8,128)S(1)} %get-tuple-element.39.slot, ...), custom_call_target="tpu_custom_call", output_to_operand_aliasing={{3}: (4, {})} | custom-call | flops 20000000000 | bytes 6291456 | tf_op jit(solution)/shard_map/weigh/pallas_call | solution.py:545
  83.2 0.0 all-to-all-done.4.sent_ref
  83.2 0.3 finish.1
  83.5 1.6 %collective-permute-start.3 = (f32[16,128]{1,0:T(8,128)S(1)}, f32[16,128]{1,0:T(8,128)S(1)}, u32[]{:S(2)}, u32[]{:S(2)}) collective-permute-start(f32[16,128]{1,0:T(8,128)S(1)} %get-tuple-element.55), channel_id=1, source_target_pairs={{0,32},{32,0},{64,96},{96,64},{1,33},{33,1},{65,97},{97,65},{2,34}... | collective-permute-start | bytes 24584 | tf_op jit(solution)/shard_map/ppermute | solution.py:639
  85.1 2.9 %collective-permute-start.4 = (f32[16,128]{1,0:T(8,128)S(1)}, f32[16,128]{1,0:T(8,128)S(1)}, u32[]{:S(2)}, u32[]{:S(2)}) collective-permute-start(f32[16,128]{1,0:T(8,128)S(1)} %get-tuple-element.56), channel_id=1, source_target_pairs={{0,64},{32,96},{64,0},{96,32},{1,65},{33,97},{65,1},{97,33},{2,66}... | collective-permute-start | bytes 24584 | tf_op jit(solution)/shard_map/ppermute | solution.py:639
  88.0 0.3 collective-permute-start.5
  88.3 0.0 collective-permute-done.3.b1_ref
  88.3 2.0 %collective-permute-done.4.b2_ref = f32[16,128]{1,0:T(8,128)S(1)} collective-permute-done((f32[16,128]{1,0:T(8,128)S(1)}, f32[16,128]{1,0:T(8,128)S(1)}, u32[]{:S(2)}, u32[]{:S(2)}) %collective-permute-start.4) | collective-permute-done | bytes 8224 | tf_op jit(solution)/shard_map/ppermute | solution.py:639
  90.3 2.6 %collective-permute-done.5.b3_ref = f32[16,128]{1,0:T(8,128)S(1)} collective-permute-done((f32[16,128]{1,0:T(8,128)S(1)}, f32[16,128]{1,0:T(8,128)S(1)}, u32[]{:S(2)}, u32[]{:S(2)}) %collective-permute-start.5) | collective-permute-done | bytes 8224 | tf_op jit(solution)/shard_map/ppermute | solution.py:639
  92.9 0.6 arrange.1
  (1 shorter events, 0.0 us)
Async XLA Ops:
  1.3 31.7 %copy-start.1 = (bf16[2048,4,128]{2,1,0:T(4,128)(2,1)S(1)}, bf16[2048,4,128]{2,1,0:T(4,128)(2,1)}, u32[]{:S(2)}) copy-start(bf16[2048,4,128]{2,1,0:T(4,128)(2,1)} %param.9) | copy-start | bytes 6291460
  5.3 27.6 %all-to-all-start.2 = ((bf16[64,7,8,128]{3,2,1,0:T(8,128)(2,1)}), bf16[64,7,8,128]{3,2,1,0:T(8,128)(2,1)S(1)}, u32[]{:S(2)}, u32[]{:S(2)}) async-start(bf16[64,7,8,128]{3,2,1,0:T(8,128)(2,1)} %get-tuple-element.37), calls=%async_computation.2 | async-start | bytes 1835008 | tf_op jit(solution)/shard_map/all_to_all | solution.py:649
  16.7 44.1 %collective-permute-start = (bf16[3,8,128]{2,1,0:T(8,128)(2,1)}, bf16[3,8,128]{2,1,0:T(8,128)(2,1)S(1)}, u32[]{:S(2)}, u32[]{:S(2)}) collective-permute-start(bf16[3,8,128]{2,1,0:T(8,128)(2,1)} %get-tuple-element.49), channel_id=1, source_target_pairs={{0,32},{32,0},{64,96},{96,64},{1,33},{33,1},{65,97},{97,65},{2,34}... | collective-permute-start | bytes 18440 | tf_op jit(solution)/shard_map/ppermute | solution.py:639
  18.3 42.6 %collective-permute-start.1 = (bf16[3,8,128]{2,1,0:T(8,128)(2,1)}, bf16[3,8,128]{2,1,0:T(8,128)(2,1)S(1)}, u32[]{:S(2)}, u32[]{:S(2)}) collective-permute-start(bf16[3,8,128]{2,1,0:T(8,128)(2,1)} %get-tuple-element.50), channel_id=1, source_target_pairs={{0,64},{32,96},{64,0},{96,32},{1,65},{33,97},{65,1},{97,33},{2,66}... | collective-permute-start | bytes 18440 | tf_op jit(solution)/shard_map/ppermute | solution.py:639
  21.2 39.7 %collective-permute-start.2 = (bf16[3,8,128]{2,1,0:T(8,128)(2,1)}, bf16[3,8,128]{2,1,0:T(8,128)(2,1)S(1)}, u32[]{:S(2)}, u32[]{:S(2)}) collective-permute-start(bf16[3,8,128]{2,1,0:T(8,128)(2,1)} %get-tuple-element.51), channel_id=1, source_target_pairs={{0,96},{32,64},{64,32},{96,0},{1,97},{33,65},{65,33},{97,1},{2,98}... | collective-permute-start | bytes 18440 | tf_op jit(solution)/shard_map/ppermute | solution.py:639
  21.5 20.7 %copy-start.2 = (s32[4,512]{1,0:T(4,128)S(1)}, s32[4,512]{1,0:T(4,128)}, u32[]{:S(2)}) copy-start(s32[4,512]{1,0:T(4,128)} %index_ref.3) | copy-start | bytes 24580
  42.5 18.4 %all-to-all-start.3 = ((bf16[64,5,8,128]{3,2,1,0:T(8,128)(2,1)}), bf16[64,5,8,128]{3,2,1,0:T(8,128)(2,1)S(1)}, u32[]{:S(2)}, u32[]{:S(2)}) async-start(bf16[64,5,8,128]{3,2,1,0:T(8,128)(2,1)} %get-tuple-element.47), calls=%async_computation.3 | async-start | bytes 1310720 | tf_op jit(solution)/shard_map/all_to_all | solution.py:652
  48.4 12.5 %copy-start = (bf16[3,8,128]{2,1,0:T(8,128)(2,1)S(1)}, bf16[3,8,128]{2,1,0:T(8,128)(2,1)}, u32[]{:S(2)}) copy-start(bf16[3,8,128]{2,1,0:T(8,128)(2,1)} %get-tuple-element.48.v0_ref) | copy-start | bytes 18436
  62.3 20.9 %all-to-all-start.4 = ((bf16[16,20,8,128]{3,2,1,0:T(8,128)(2,1)}), bf16[16,20,8,128]{3,2,1,0:T(8,128)(2,1)S(1)}, u32[]{:S(2)}, u32[]{:S(2)}) async-start(bf16[16,20,8,128]{3,2,1,0:T(8,128)(2,1)} %get-tuple-element.53), calls=%async_computation.4 | async-start | bytes 1310720 | tf_op jit(solution)/shard_map/all_to_all | solution.py:663
  83.5 4.8 %collective-permute-start.3 = (f32[16,128]{1,0:T(8,128)S(1)}, f32[16,128]{1,0:T(8,128)S(1)}, u32[]{:S(2)}, u32[]{:S(2)}) collective-permute-start(f32[16,128]{1,0:T(8,128)S(1)} %get-tuple-element.55), channel_id=1, source_target_pairs={{0,32},{32,0},{64,96},{96,64},{1,33},{33,1},{65,97},{97,65},{2,34}... | collective-permute-start | bytes 24584 | tf_op jit(solution)/shard_map/ppermute | solution.py:639
  85.1 5.2 %collective-permute-start.4 = (f32[16,128]{1,0:T(8,128)S(1)}, f32[16,128]{1,0:T(8,128)S(1)}, u32[]{:S(2)}, u32[]{:S(2)}) collective-permute-start(f32[16,128]{1,0:T(8,128)S(1)} %get-tuple-element.56), channel_id=1, source_target_pairs={{0,64},{32,96},{64,0},{96,32},{1,65},{33,97},{65,1},{97,33},{2,66}... | collective-permute-start | bytes 24584 | tf_op jit(solution)/shard_map/ppermute | solution.py:639
  88.0 4.9 %collective-permute-start.5 = (f32[16,128]{1,0:T(8,128)S(1)}, f32[16,128]{1,0:T(8,128)S(1)}, u32[]{:S(2)}, u32[]{:S(2)}) collective-permute-start(f32[16,128]{1,0:T(8,128)S(1)} %get-tuple-element.57), channel_id=1, source_target_pairs={{0,96},{32,64},{64,32},{96,0},{1,97},{33,65},{65,33},{97,1},{2,98}... | collective-permute-start | bytes 24584 | tf_op jit(solution)/shard_map/ppermute | solution.py:639
